TPU v7x, 128 devices: a whole 4x4x4 slice. The times are simulated.
128 devices in a mesh: seq: 16 (over x, z), head: 8 (over y, core).
Axes of the slice: x: 4, y: 4, z: 4, core: 2. Of those that a mesh axis runs over, the one named last changes fastest.
Arguments:
- conv_input: bfloat16 [16384, 8, 1280], P(('seq', 'head')), may hold values from -6 to 6
- gate_input: bfloat16 [16384, 8192], P(('seq', 'head')), may hold values from -40 to 40
- step_size: bfloat16 [16384, 128], P(('seq', 'head')), may hold values from 0.0015 to 0.18
- decay_log: bfloat16 [16384, 128], P(('seq', 'head')), may hold values from -0.6 to 0
- conv_weight: float32 [4, 8, 1280], P(None, 'head'), may hold values from -3 to 3
- conv_bias: float32 [8, 1280], P('head'), may hold values from -3 to 3
- skip_gain: float32 [128], replicated, may hold values from 0.5 to 1.5
- norm_gain: float32 [8192], replicated, may hold values from 0.5 to 1.5
- seg_length: int32 [16], P('seq'), may hold values from 64 to 1024, as said below
- seg_first: int32 [16], P('seq'), may hold values from 0 to 1, as said below
Outputs:
- normed: bfloat16 [16384, 8192], P(('seq', 'head'))
Inputs may be any that keep to these rules, and one draw needn't show every extreme that they name: The first seg_length[s] slots of segment s hold tokens, the rest are padding; in every draw one segment is full (1024). 1 where segment s begins a new request, 0 where it continues the request of segment s - 1; seg_first[0] = 1 and seg_first[15] = 0.
All inputs are finite; a program needn't handle non-finite values.
Results may differ from a plain program's by a relative error of at most 0.012.
Values may be sent and summed in bfloat16 or wider, within the bound.
No kernel may reach another device: no remote copies, remote signals or barrier semaphores. Data moves between devices by JAX's collectives and lax.ppermute only.
A program may use at most 128 MiB of HBM per device.

v0:
```python
import jax
import jax.numpy as jnp
from jax import lax
from jax.sharding import PartitionSpec as P

HEAD_DIM = 64
STATE = 128
KERNEL = 4
BLOCK = 256


EPSILON = 1e-05


def passed_along(value, axis, steps):
    count = lax.axis_size(axis)
    leading, last = (max(0, -steps), min(count, count - steps))
    return lax.ppermute(value, axis, [(source, source + steps) for source in range(leading, last)])


def block_terms(state_pair, x_heads, b_rows, c_rows, log_rate, input_gain):
    h_prev, offset = state_pair
    block_len = log_rate.shape[0]
    head_count = log_rate.shape[1]
    groups = b_rows.shape[1]
    per_group = head_count // groups
    head_dim = x_heads.shape[2]
    state_dim = b_rows.shape[2]
    running = jnp.cumsum(log_rate, axis=0)
    running_t = running.T
    spread = running_t[:, :, None] - running_t[:, None, :]
    causal = (jnp.arange(block_len)[:, None] >= jnp.arange(block_len)[None, :])[None]
    decay_mat = jnp.where(causal, jnp.exp(jnp.where(causal, spread, 0.0)), 0.0)
    scores = jnp.einsum("tgn,ugn->gtu", c_rows, b_rows, preferred_element_type=jnp.float32)
    weights = (
        scores[:, None]
        * decay_mat.reshape(groups, per_group, block_len, block_len)
        * input_gain.T.reshape(groups, per_group, 1, block_len)
    )
    weights = weights.astype(jnp.bfloat16).reshape(head_count, block_len, block_len)
    y_in = jnp.einsum("htu,uhp->thp", weights, x_heads, preferred_element_type=jnp.float32)
    state_four = h_prev.reshape(groups, per_group, head_dim, state_dim)
    readout = jnp.einsum(
        "tgn,gkpn->tgkp", c_rows.astype(jnp.float32), state_four, precision=lax.Precision.HIGHEST
    )
    y_off = jnp.exp(running)[:, :, None] * readout.reshape(block_len, head_count, head_dim)
    final_log = running[-1]
    to_final = jnp.exp(final_log[None, :] - running)
    weighted = ((to_final * input_gain)[:, :, None] * x_heads.astype(jnp.float32)).astype(
        jnp.bfloat16
    )
    update = jnp.einsum(
        "ugkp,ugn->gkpn",
        weighted.reshape(block_len, groups, per_group, head_dim),
        b_rows,
        preferred_element_type=jnp.float32,
    )
    h_next = jnp.exp(final_log)[:, None, None] * h_prev + update.reshape(
        head_count, head_dim, state_dim
    )
    return ((h_next, offset + final_log), (y_in + y_off, offset[None, :] + running))


def gate_norm(values, gates, gains):
    gated = values.astype(jnp.float32) * jax.nn.silu(gates.astype(jnp.float32))
    mean_square = jnp.mean(gated * gated, axis=-1, keepdims=True)
    return gated * lax.rsqrt(mean_square + EPSILON) * gains[None]


def body(
    conv_input,
    gate_input,
    step_size,
    decay_log,
    conv_weight,
    conv_bias,
    skip_gain,
    norm_gain,
    seg_length,
    seg_first,
):
    head_devices = lax.axis_size("head")
    head_index = lax.axis_index("head")
    groups_here = conv_weight.shape[1]
    heads_here = step_size.shape[1] // head_devices
    per_group = heads_here // groups_here
    xwidth = per_group * HEAD_DIM
    tok_rows = conv_input.shape[0]
    seg_rows = tok_rows * head_devices
    length = seg_length[0]
    keep_flag = (1 - seg_first[0]).astype(jnp.float32)
    conv_rows, gate_rows, step_rows, decay_rows = (
        lax.all_to_all(conv_input, "head", split_axis=1, concat_axis=0, tiled=True),
        lax.all_to_all(gate_input, "head", split_axis=1, concat_axis=0, tiled=True),
        lax.all_to_all(step_size, "head", split_axis=1, concat_axis=0, tiled=True),
        lax.all_to_all(decay_log, "head", split_axis=1, concat_axis=0, tiled=True),
    )
    tail_rows = lax.dynamic_slice_in_dim(conv_rows, length - (KERNEL - 1), KERNEL - 1, 0)
    tail_rows = passed_along(tail_rows, "seq", 1) * keep_flag.astype(jnp.bfloat16)
    padded = jnp.concatenate([tail_rows, conv_rows], axis=0)
    mixed = conv_bias[None]
    for tap_index in range(KERNEL):
        mixed = mixed + conv_weight[tap_index][None] * padded[
            tap_index : tap_index + seg_rows
        ].astype(jnp.float32)
    activated = jax.nn.silu(mixed).astype(jnp.bfloat16)
    x_heads = activated[:, :, :xwidth].reshape(seg_rows, heads_here, HEAD_DIM)
    b_rows = activated[:, :, xwidth : xwidth + STATE]
    c_rows = activated[:, :, xwidth + STATE :]
    is_live = jnp.arange(seg_rows) < length
    log_rate = jnp.where(is_live[:, None], decay_rows.astype(jnp.float32), 0.0)
    input_gain = jnp.where(is_live[:, None], step_rows.astype(jnp.float32), 0.0)
    operands = (x_heads, b_rows, c_rows, log_rate, input_gain)
    nblocks = seg_rows // BLOCK
    start_state = (
        jnp.zeros((heads_here, HEAD_DIM, STATE), jnp.float32),
        jnp.zeros((heads_here,), jnp.float32),
    )
    blocked = tuple((operand.reshape((nblocks, BLOCK) + operand.shape[1:]) for operand in operands))
    (local_state, total_log), (y_local, running) = lax.scan(
        lambda state_pair, block_data: block_terms(state_pair, *block_data), start_state, blocked
    )
    y_local = y_local.reshape(seg_rows, heads_here, HEAD_DIM)
    running = running.reshape(seg_rows, heads_here)
    total_decay = jnp.exp(total_log)

    def relay_turn(turn_index, incoming):
        outgoing = total_decay[:, None, None] * incoming + local_state
        return keep_flag * passed_along(outgoing, "seq", 1)

    incoming = lax.fori_loop(0, lax.axis_size("seq") - 1, relay_turn, jnp.zeros_like(local_state))
    readout = jnp.einsum(
        "tgn,gkpn->tgkp",
        c_rows.astype(jnp.float32),
        incoming.reshape(groups_here, per_group, HEAD_DIM, STATE),
        precision=lax.Precision.HIGHEST,
    )
    readout = readout.reshape(seg_rows, heads_here, HEAD_DIM)
    skip_here = lax.dynamic_slice_in_dim(skip_gain, head_index * heads_here, heads_here, 0)
    output_y = (
        y_local
        + jnp.exp(running)[:, :, None] * readout
        + skip_here[None, :, None] * x_heads.astype(jnp.float32)
    ).astype(jnp.bfloat16)
    gain_here = lax.dynamic_slice_in_dim(
        norm_gain, head_index * heads_here * HEAD_DIM, heads_here * HEAD_DIM, 0
    )
    result = gate_norm(
        output_y.reshape(seg_rows, groups_here, xwidth),
        gate_rows.reshape(seg_rows, groups_here, xwidth),
        gain_here.reshape(groups_here, xwidth),
    )
    result = jnp.where(
        is_live[:, None], result.reshape(seg_rows, heads_here * HEAD_DIM), 0.0
    ).astype(jnp.bfloat16)
    return lax.all_to_all(result, "head", split_axis=0, concat_axis=1, tiled=True)


def solution(mesh):
    return jax.shard_map(
        body,
        mesh=mesh,
        in_specs=(
            P(("seq", "head"), None, None),
            P(("seq", "head"), None),
            P(("seq", "head"), None),
            P(("seq", "head"), None),
            P(None, "head", None),
            P("head", None),
            P(),
            P(),
            P("seq"),
            P("seq"),
        ),
        out_specs=P(("seq", "head"), None),
        check_vma=False,
    )
```

profile of v0, /device:TPU:6, one launch (start us, length us, event | category | flops | bytes accessed | tf_op | source)
XLA Modules:
  0.0 491.7 jit_solution(13236479750119831430)
XLA Ops:
  26.9 29.5 %all-to-all-done.2 = bf16[128,8,1280]{2,0,1:T(8,128)(2,1)S(1)} async-done(((bf16[128,8,1280]{2,0,1:T(8,128)(2,1)}), bf16[128,8,1280]{2,0,1:T(8,128)(2,1)S(1)}, u32[]{:S(2)}, u32[]{:S(2)}) %all-to-all-start.2) | async-done | bytes 2621472 | tf_op jit(solution)/shard_map/all_to_all | solution.py:93
  66.6 21.4 %all-to-all-done.3 = bf16[128,8,1024]{2,0,1:T(8,128)(2,1)} async-done(((bf16[128,8,1024]{2,0,1:T(8,128)(2,1)}), bf16[128,8,1024]{2,0,1:T(8,128)(2,1)}, u32[]{:S(2)}, u32[]{:S(2)}) %all-to-all-start.3) | async-done | bytes 2097184 | tf_op jit(solution)/shard_map/all_to_all | solution.py:94
  101.7 5.8 %copy.74 = bf16[4,256,16,64]{1,3,2,0:T(8,128)(2,1)} copy(bf16[4,256,16,64]{3,2,1,0:T(8,128)(2,1)} %reshape.358) | data formatting | bytes 4194304
  107.6 28.4 %while.28 = (s32[]{:T(128)}, f32[16,64,128]{2,1,0:T(8,128)S(1)}, f32[16]{0:T(128)S(1)}, f32[4,256,16,64]{1,3,2,0:T(8,128)}, f32[4,256,16]{1,2,0:T(8,128)S(1)}, /...) while((s32[]{:T(128)}, f32[16,64,128]{2,1,0:T(8,128)S(1)}, ...), condition=%wide.region_3.4_spmd.clone, body=%wide.region_0.3_spmd.clone.sunk | while | flops 629493824 | bytes 7085273 | solution.py:120
  136.0 282.8 %while.29 = (s32[]{:T(128)}, f32[16,64,128]{2,1,0:T(8,128)}, f32[]{:T(128)}, f32[16]{0:T(128)S(1)}, f32[16,64,128]{2,1,0:T(8,128)S(1)}, /*index=5*/s32[]{:T(128)}, s32[]{:T(128)}) while((s32[]{:T(128)}, f32[16,64,128]{2,1,0:T(8,128)}, f32[]{:T(128)}, f32[16]{0:T(128)S(1)}, f32[16,64,128]{2,1,0:T(8,128)S(1)}, /*index=5*/s32[]{:T(128)}, ...), condition=%wide.region_5.6_spmd.clone, body=%wide.region_4.5_spmd.clone.sunk | while | flops 524291 | bytes 4718787 | solution.py:131
  140.8 14.4 %collective-permute-done = f32[16,64,128]{2,1,0:T(8,128)} collective-permute-done((f32[16,64,128]{2,1,0:T(8,128)}, f32[16,64,128]{2,1,0:T(8,128)}, u32[]{:S(2)}, u32[]{:S(2)}) %collective-permute-start) | collective-permute-done | bytes 524320 | tf_op jit(solution)/shard_map/while/body/eval_jaxpr/ppermute | solution.py:18
  161.0 15.3 %collective-permute-done = f32[16,64,128]{2,1,0:T(8,128)} collective-permute-done((f32[16,64,128]{2,1,0:T(8,128)}, f32[16,64,128]{2,1,0:T(8,128)}, u32[]{:S(2)}, u32[]{:S(2)}) %collective-permute-start) | collective-permute-done | bytes 524320 | tf_op jit(solution)/shard_map/while/body/eval_jaxpr/ppermute | solution.py:18
  182.1 14.4 %collective-permute-done = f32[16,64,128]{2,1,0:T(8,128)} collective-permute-done((f32[16,64,128]{2,1,0:T(8,128)}, f32[16,64,128]{2,1,0:T(8,128)}, u32[]{:S(2)}, u32[]{:S(2)}) %collective-permute-start) | collective-permute-done | bytes 524320 | tf_op jit(solution)/shard_map/while/body/eval_jaxpr/ppermute | solution.py:18
  202.2 13.4 %collective-permute-done = f32[16,64,128]{2,1,0:T(8,128)} collective-permute-done((f32[16,64,128]{2,1,0:T(8,128)}, f32[16,64,128]{2,1,0:T(8,128)}, u32[]{:S(2)}, u32[]{:S(2)}) %collective-permute-start) | collective-permute-done | bytes 524320 | tf_op jit(solution)/shard_map/while/body/eval_jaxpr/ppermute | solution.py:18
  221.5 12.5 %collective-permute-done = f32[16,64,128]{2,1,0:T(8,128)} collective-permute-done((f32[16,64,128]{2,1,0:T(8,128)}, f32[16,64,128]{2,1,0:T(8,128)}, u32[]{:S(2)}, u32[]{:S(2)}) %collective-permute-start) | collective-permute-done | bytes 524320 | tf_op jit(solution)/shard_map/while/body/eval_jaxpr/ppermute | solution.py:18
  239.7 11.6 %collective-permute-done = f32[16,64,128]{2,1,0:T(8,128)} collective-permute-done((f32[16,64,128]{2,1,0:T(8,128)}, f32[16,64,128]{2,1,0:T(8,128)}, u32[]{:S(2)}, u32[]{:S(2)}) %collective-permute-start) | collective-permute-done | bytes 524320 | tf_op jit(solution)/shard_map/while/body/eval_jaxpr/ppermute | solution.py:18
  257.1 11.6 %collective-permute-done = f32[16,64,128]{2,1,0:T(8,128)} collective-permute-done((f32[16,64,128]{2,1,0:T(8,128)}, f32[16,64,128]{2,1,0:T(8,128)}, u32[]{:S(2)}, u32[]{:S(2)}) %collective-permute-start) | collective-permute-done | bytes 524320 | tf_op jit(solution)/shard_map/while/body/eval_jaxpr/ppermute | solution.py:18
  274.5 11.6 %collective-permute-done = f32[16,64,128]{2,1,0:T(8,128)} collective-permute-done((f32[16,64,128]{2,1,0:T(8,128)}, f32[16,64,128]{2,1,0:T(8,128)}, u32[]{:S(2)}, u32[]{:S(2)}) %collective-permute-start) | collective-permute-done | bytes 524320 | tf_op jit(solution)/shard_map/while/body/eval_jaxpr/ppermute | solution.py:18
  291.8 11.6 %collective-permute-done = f32[16,64,128]{2,1,0:T(8,128)} collective-permute-done((f32[16,64,128]{2,1,0:T(8,128)}, f32[16,64,128]{2,1,0:T(8,128)}, u32[]{:S(2)}, u32[]{:S(2)}) %collective-permute-start) | collective-permute-done | bytes 524320 | tf_op jit(solution)/shard_map/while/body/eval_jaxpr/ppermute | solution.py:18
  309.2 11.6 %collective-permute-done = f32[16,64,128]{2,1,0:T(8,128)} collective-permute-done((f32[16,64,128]{2,1,0:T(8,128)}, f32[16,64,128]{2,1,0:T(8,128)}, u32[]{:S(2)}, u32[]{:S(2)}) %collective-permute-start) | collective-permute-done | bytes 524320 | tf_op jit(solution)/shard_map/while/body/eval_jaxpr/ppermute | solution.py:18
  326.5 12.3 %collective-permute-done = f32[16,64,128]{2,1,0:T(8,128)} collective-permute-done((f32[16,64,128]{2,1,0:T(8,128)}, f32[16,64,128]{2,1,0:T(8,128)}, u32[]{:S(2)}, u32[]{:S(2)}) %collective-permute-start) | collective-permute-done | bytes 524320 | tf_op jit(solution)/shard_map/while/body/eval_jaxpr/ppermute | solution.py:18
  344.6 13.4 %collective-permute-done = f32[16,64,128]{2,1,0:T(8,128)} collective-permute-done((f32[16,64,128]{2,1,0:T(8,128)}, f32[16,64,128]{2,1,0:T(8,128)}, u32[]{:S(2)}, u32[]{:S(2)}) %collective-permute-start) | collective-permute-done | bytes 524320 | tf_op jit(solution)/shard_map/while/body/eval_jaxpr/ppermute | solution.py:18
  363.7 14.4 %collective-permute-done = f32[16,64,128]{2,1,0:T(8,128)} collective-permute-done((f32[16,64,128]{2,1,0:T(8,128)}, f32[16,64,128]{2,1,0:T(8,128)}, u32[]{:S(2)}, u32[]{:S(2)}) %collective-permute-start) | collective-permute-done | bytes 524320 | tf_op jit(solution)/shard_map/while/body/eval_jaxpr/ppermute | solution.py:18
  384.0 15.5 %collective-permute-done = f32[16,64,128]{2,1,0:T(8,128)} collective-permute-done((f32[16,64,128]{2,1,0:T(8,128)}, f32[16,64,128]{2,1,0:T(8,128)}, u32[]{:S(2)}, u32[]{:S(2)}) %collective-permute-start) | collective-permute-done | bytes 524320 | tf_op jit(solution)/shard_map/while/body/eval_jaxpr/ppermute | solution.py:18
  405.3 11.6 %collective-permute-done = f32[16,64,128]{2,1,0:T(8,128)} collective-permute-done((f32[16,64,128]{2,1,0:T(8,128)}, f32[16,64,128]{2,1,0:T(8,128)}, u32[]{:S(2)}, u32[]{:S(2)}) %collective-permute-start) | collective-permute-done | bytes 524320 | tf_op jit(solution)/shard_map/while/body/eval_jaxpr/ppermute | solution.py:18
  428.9 8.1 %copy.86 = f32[4,256,16,64]{3,2,1,0:T(8,128)} copy(f32[4,256,16,64]{1,3,2,0:T(8,128)} %get-tuple-element.87) | data formatting | bytes 8388608 | tf_op jit(solution)/shard_map/reshape | solution.py:123
  437.0 7.6 %reshape.359 = f32[1024,1,1024]{2,0,1:T(8,128)} reshape(f32[4,256,16,64]{3,2,1,0:T(8,128)} %copy.86) | data formatting | bytes 8388608 | tf_op jit(solution)/shard_map/reshape | solution.py:123
  452.5 6.9 %multiply_reduce_fusion = (f32[1024]{0:T(1024)S(1)}, f32[1024,1,1024]{2,0,1:T(8,128)S(1)}) fusion(bf16[1024,1,1280]{2,0,1:T(8,128)(2,1)S(1)} %copy-done.1, f32[1024]{0:T(1024)S(1)} %mul.229, f32[1024,1,1024]{2,0,1:T(8,128)} %reshape.359, f32[1024,1,1024]{2,0,1:T(8,128)} %copy.79, f32[1024,1,1024]{2,0,1:T(8,128)} %copy.80, f32[1024,1,1024]{2,0,1:T(8,128)} %bitcast.173), kind=kLoop, calls=%fused_computation.65 | loop fusion | flops 14679040 | bytes 23076864 | tf_op jit(solution)/shard_map/reduce_sum | solution.py:66
  460.2 30.0 %all_to_all.73 = bf16[8,128,1024]{2,1,0:T(8,128)(2,1)S(1)} all-to-all(bf16[8,128,1024]{2,1,0:T(8,128)(2,1)S(1)} %select_convert_fusion), channel_id=1, replica_groups=mesh['seq'=16,'head'=8] {'head'}, dimensions={0} | all-to-all | bytes 4194304 | tf_op jit(solution)/shard_map/all_to_all | solution.py:156
  (174 shorter events, 185.3 us)
Async XLA Ops:
  1.5 9.9 %all-to-all-start = ((bf16[128,8,16]{0,2,1:T(8,128)(2,1)}), bf16[128,8,16]{0,2,1:T(8,128)(2,1)S(1)}, u32[]{:S(2)}, u32[]{:S(2)}) async-start(bf16[128,8,16]{0,2,1:T(8,128)(2,1)} %bitcast.1), calls=%async_computation | async-start | bytes 65536 | tf_op jit(solution)/shard_map/all_to_all | solution.py:96
  11.4 8.7 %all-to-all-start.1 = ((bf16[128,8,16]{0,2,1:T(8,128)(2,1)}), bf16[128,8,16]{0,2,1:T(8,128)(2,1)S(1)}, u32[]{:S(2)}, u32[]{:S(2)}) async-start(bf16[128,8,16]{0,2,1:T(8,128)(2,1)} %bitcast.3), calls=%async_computation.1 | async-start | bytes 65536 | tf_op jit(solution)/shard_map/all_to_all | solution.py:95
  20.1 36.4 %all-to-all-start.2 = ((bf16[128,8,1280]{2,0,1:T(8,128)(2,1)}), bf16[128,8,1280]{2,0,1:T(8,128)(2,1)S(1)}, u32[]{:S(2)}, u32[]{:S(2)}) async-start(bf16[128,8,1280]{2,0,1:T(8,128)(2,1)} %copy.69), calls=%async_computation.2 | async-start | bytes 5242880 | tf_op jit(solution)/shard_map/all_to_all | solution.py:93
  23.7 38.4 %copy-start.4 = (f32[128]{0:T(128)S(1)}, f32[128]{0:T(128)}, u32[]{:S(2)}) copy-start(f32[128]{0:T(128)} %param.20) | copy-start | bytes 1540
  23.7 38.7 %copy-start.3 = (f32[1,1280]{1,0:T(1,128)S(1)}, f32[1,1280]{1,0:T(1,128)}, u32[]{:S(2)}) copy-start(f32[1,1280]{1,0:T(1,128)} %param.19) | copy-start | bytes 15364
  23.8 38.7 %copy-start.2 = (f32[4,1,1280]{2,1,0:T(1,128)S(1)}, f32[4,1,1280]{2,1,0:T(1,128)}, u32[]{:S(2)}) copy-start(f32[4,1,1280]{2,1,0:T(1,128)} %param.18) | copy-start | bytes 61444
  56.5 31.5 %all-to-all-start.3 = ((bf16[128,8,1024]{2,0,1:T(8,128)(2,1)}), bf16[128,8,1024]{2,0,1:T(8,128)(2,1)}, u32[]{:S(2)}, u32[]{:S(2)}) async-start(bf16[128,8,1024]{2,0,1:T(8,128)(2,1)} %bitcast.177), calls=%async_computation.3 | async-start | bytes 4194304 | tf_op jit(solution)/shard_map/all_to_all | solution.py:94
  62.7 29.3 %collective-permute-start.1 = (bf16[3,1,1280]{2,0,1:T(4,128)(2,1)S(1)}, bf16[3,1,1280]{2,0,1:T(4,128)(2,1)S(1)}, u32[]{:S(2)}, u32[]{:S(2)}) collective-permute-start(bf16[3,1,1280]{2,0,1:T(4,128)(2,1)S(1)} %constant_dynamic-slice_fusion.2), channel_id=1, source_target_pairs={{0,8},{8,16},{16,24},{24,32},{32,40},{40,48},{48,56},{56,64},{64,7... | collective-permute-start | bytes 23048 | tf_op jit(solution)/shard_map/ppermute | solution.py:18
  135.9 282.8 %copy-start.1 = (bf16[1024,1,1280]{2,0,1:T(8,128)(2,1)S(1)}, bf16[1024,1,1280]{2,0,1:T(8,128)(2,1)}, u32[]{:S(2)}) copy-start(bf16[1024,1,1280]{2,0,1:T(8,128)(2,1)} %copy-done) | copy-start | bytes 7864324
  136.9 18.4 %collective-permute-start = (f32[16,64,128]{2,1,0:T(8,128)}, f32[16,64,128]{2,1,0:T(8,128)}, u32[]{:S(2)}, u32[]{:S(2)}) collective-permute-start(f32[16,64,128]{2,1,0:T(8,128)} %fusion.73), channel_id=1, source_target_pairs={{0,8},{8,16},{16,24},{24,32},{32,40},{40,48},{48,56},{56,64},{64,7... | collective-permute-start | bytes 1572872 | tf_op jit(solution)/shard_map/while/body/eval_jaxpr/ppermute | solution.py:18
  159.1 17.2 %collective-permute-start = (f32[16,64,128]{2,1,0:T(8,128)}, f32[16,64,128]{2,1,0:T(8,128)}, u32[]{:S(2)}, u32[]{:S(2)}) collective-permute-start(f32[16,64,128]{2,1,0:T(8,128)} %fusion.73), channel_id=1, source_target_pairs={{0,8},{8,16},{16,24},{24,32},{32,40},{40,48},{48,56},{56,64},{64,7... | collective-permute-start | bytes 1572872 | tf_op jit(solution)/shard_map/while/body/eval_jaxpr/ppermute | solution.py:18
  180.2 16.3 %collective-permute-start = (f32[16,64,128]{2,1,0:T(8,128)}, f32[16,64,128]{2,1,0:T(8,128)}, u32[]{:S(2)}, u32[]{:S(2)}) collective-permute-start(f32[16,64,128]{2,1,0:T(8,128)} %fusion.73), channel_id=1, source_target_pairs={{0,8},{8,16},{16,24},{24,32},{32,40},{40,48},{48,56},{56,64},{64,7... | collective-permute-start | bytes 1572872 | tf_op jit(solution)/shard_map/while/body/eval_jaxpr/ppermute | solution.py:18
  200.3 15.4 %collective-permute-start = (f32[16,64,128]{2,1,0:T(8,128)}, f32[16,64,128]{2,1,0:T(8,128)}, u32[]{:S(2)}, u32[]{:S(2)}) collective-permute-start(f32[16,64,128]{2,1,0:T(8,128)} %fusion.73), channel_id=1, source_target_pairs={{0,8},{8,16},{16,24},{24,32},{32,40},{40,48},{48,56},{56,64},{64,7... | collective-permute-start | bytes 1572872 | tf_op jit(solution)/shard_map/while/body/eval_jaxpr/ppermute | solution.py:18
  219.5 14.4 %collective-permute-start = (f32[16,64,128]{2,1,0:T(8,128)}, f32[16,64,128]{2,1,0:T(8,128)}, u32[]{:S(2)}, u32[]{:S(2)}) collective-permute-start(f32[16,64,128]{2,1,0:T(8,128)} %fusion.73), channel_id=1, source_target_pairs={{0,8},{8,16},{16,24},{24,32},{32,40},{40,48},{48,56},{56,64},{64,7... | collective-permute-start | bytes 1572872 | tf_op jit(solution)/shard_map/while/body/eval_jaxpr/ppermute | solution.py:18
  237.8 13.5 %collective-permute-start = (f32[16,64,128]{2,1,0:T(8,128)}, f32[16,64,128]{2,1,0:T(8,128)}, u32[]{:S(2)}, u32[]{:S(2)}) collective-permute-start(f32[16,64,128]{2,1,0:T(8,128)} %fusion.73), channel_id=1, source_target_pairs={{0,8},{8,16},{16,24},{24,32},{32,40},{40,48},{48,56},{56,64},{64,7... | collective-permute-start | bytes 1572872 | tf_op jit(solution)/shard_map/while/body/eval_jaxpr/ppermute | solution.py:18
  255.2 13.5 %collective-permute-start = (f32[16,64,128]{2,1,0:T(8,128)}, f32[16,64,128]{2,1,0:T(8,128)}, u32[]{:S(2)}, u32[]{:S(2)}) collective-permute-start(f32[16,64,128]{2,1,0:T(8,128)} %fusion.73), channel_id=1, source_target_pairs={{0,8},{8,16},{16,24},{24,32},{32,40},{40,48},{48,56},{56,64},{64,7... | collective-permute-start | bytes 1572872 | tf_op jit(solution)/shard_map/while/body/eval_jaxpr/ppermute | solution.py:18
  272.6 13.5 %collective-permute-start = (f32[16,64,128]{2,1,0:T(8,128)}, f32[16,64,128]{2,1,0:T(8,128)}, u32[]{:S(2)}, u32[]{:S(2)}) collective-permute-start(f32[16,64,128]{2,1,0:T(8,128)} %fusion.73), channel_id=1, source_target_pairs={{0,8},{8,16},{16,24},{24,32},{32,40},{40,48},{48,56},{56,64},{64,7... | collective-permute-start | bytes 1572872 | tf_op jit(solution)/shard_map/while/body/eval_jaxpr/ppermute | solution.py:18
  289.9 13.5 %collective-permute-start = (f32[16,64,128]{2,1,0:T(8,128)}, f32[16,64,128]{2,1,0:T(8,128)}, u32[]{:S(2)}, u32[]{:S(2)}) collective-permute-start(f32[16,64,128]{2,1,0:T(8,128)} %fusion.73), channel_id=1, source_target_pairs={{0,8},{8,16},{16,24},{24,32},{32,40},{40,48},{48,56},{56,64},{64,7... | collective-permute-start | bytes 1572872 | tf_op jit(solution)/shard_map/while/body/eval_jaxpr/ppermute | solution.py:18
  307.3 13.5 %collective-permute-start = (f32[16,64,128]{2,1,0:T(8,128)}, f32[16,64,128]{2,1,0:T(8,128)}, u32[]{:S(2)}, u32[]{:S(2)}) collective-permute-start(f32[16,64,128]{2,1,0:T(8,128)} %fusion.73), channel_id=1, source_target_pairs={{0,8},{8,16},{16,24},{24,32},{32,40},{40,48},{48,56},{56,64},{64,7... | collective-permute-start | bytes 1572872 | tf_op jit(solution)/shard_map/while/body/eval_jaxpr/ppermute | solution.py:18
  324.6 14.2 %collective-permute-start = (f32[16,64,128]{2,1,0:T(8,128)}, f32[16,64,128]{2,1,0:T(8,128)}, u32[]{:S(2)}, u32[]{:S(2)}) collective-permute-start(f32[16,64,128]{2,1,0:T(8,128)} %fusion.73), channel_id=1, source_target_pairs={{0,8},{8,16},{16,24},{24,32},{32,40},{40,48},{48,56},{56,64},{64,7... | collective-permute-start | bytes 1572872 | tf_op jit(solution)/shard_map/while/body/eval_jaxpr/ppermute | solution.py:18
  342.7 15.3 %collective-permute-start = (f32[16,64,128]{2,1,0:T(8,128)}, f32[16,64,128]{2,1,0:T(8,128)}, u32[]{:S(2)}, u32[]{:S(2)}) collective-permute-start(f32[16,64,128]{2,1,0:T(8,128)} %fusion.73), channel_id=1, source_target_pairs={{0,8},{8,16},{16,24},{24,32},{32,40},{40,48},{48,56},{56,64},{64,7... | collective-permute-start | bytes 1572872 | tf_op jit(solution)/shard_map/while/body/eval_jaxpr/ppermute | solution.py:18
  361.8 16.4 %collective-permute-start = (f32[16,64,128]{2,1,0:T(8,128)}, f32[16,64,128]{2,1,0:T(8,128)}, u32[]{:S(2)}, u32[]{:S(2)}) collective-permute-start(f32[16,64,128]{2,1,0:T(8,128)} %fusion.73), channel_id=1, source_target_pairs={{0,8},{8,16},{16,24},{24,32},{32,40},{40,48},{48,56},{56,64},{64,7... | collective-permute-start | bytes 1572872 | tf_op jit(solution)/shard_map/while/body/eval_jaxpr/ppermute | solution.py:18
  382.0 17.4 %collective-permute-start = (f32[16,64,128]{2,1,0:T(8,128)}, f32[16,64,128]{2,1,0:T(8,128)}, u32[]{:S(2)}, u32[]{:S(2)}) collective-permute-start(f32[16,64,128]{2,1,0:T(8,128)} %fusion.73), channel_id=1, source_target_pairs={{0,8},{8,16},{16,24},{24,32},{32,40},{40,48},{48,56},{56,64},{64,7... | collective-permute-start | bytes 1572872 | tf_op jit(solution)/shard_map/while/body/eval_jaxpr/ppermute | solution.py:18
  403.4 13.5 %collective-permute-start = (f32[16,64,128]{2,1,0:T(8,128)}, f32[16,64,128]{2,1,0:T(8,128)}, u32[]{:S(2)}, u32[]{:S(2)}) collective-permute-start(f32[16,64,128]{2,1,0:T(8,128)} %fusion.73), channel_id=1, source_target_pairs={{0,8},{8,16},{16,24},{24,32},{32,40},{40,48},{48,56},{56,64},{64,7... | collective-permute-start | bytes 1572872 | tf_op jit(solution)/shard_map/while/body/eval_jaxpr/ppermute | solution.py:18
  (2 other events, 8.4 us)
where the time goes:
time: 495 us; the launch traced here: 492 us
  waiting for transfers between devices  252 us (51%)
  other arithmetic  76.2 us (15%)
  local copies, waits for them, and re-layouts  53.9 us (11%)
  starting transfers between devices  50.3 us (10%)
  blocking collectives  30 us (6%)
  matrix products  27.7 us (6%)
    ppermute x16, waiting for transfers between devices, passed_along(): lax.ppermute(value, axis, [(source, source + steps) for source in range(l...  195 us
    ppermute x16, starting transfers between devices, passed_along(): lax.ppermute(value, axis, [(source, source + steps) for source in range(l...  34.5 us
    all_to_all x1, blocking collectives, body(): lax.all_to_all(result, 'head', split_axis=0, concat_axis=1, tiled=True)  30 us
    all_to_all x1, waiting for transfers between devices, body(): lax.all_to_all(conv_input, 'head', split_axis=1, concat_axis=0, tiled=True)  29.5 us
    mul x15, other arithmetic, relay_turn(): return keep_flag * passed_along(outgoing, 'seq', 1)  28.6 us
    add x15, other arithmetic, relay_turn(): outgoing = total_decay[:, None, None] * incoming + local_state  28.2 us
    all_to_all x1, waiting for transfers between devices, body(): lax.all_to_all(gate_input, 'head', split_axis=1, concat_axis=0, tiled=True)  21.4 us
    reshape x2, local copies, waits for them, and re-layouts, body(): y_local = y_local.reshape(seg_rows, heads_here, HEAD_DIM)  15.7 us
  transfers between devices with their start and end apart: 20, of which 19 were waited for; matrix products, arithmetic and copies ran while one was open for 3% of the time, Pallas kernels for 0%

commit v1 on v0

v1 whole, which is shorter than its diff:
```python
import functools

import jax
import jax.numpy as jnp
from jax import lax
from jax.experimental import pallas as pl
from jax.experimental.pallas import tpu as pltpu
from jax.sharding import Mesh, PartitionSpec as P

HEAD_DIM = 64
KERNEL = 4
EPSILON = 1e-05
TOK = 128
GROUPS = 8
XW = 1024
GW = 1280
LANE = 128
LW = 256
CHUNKS = 64
ROWS = 80
AXES = ("seq", "y", "core")
CHIPS = ("seq", "y")
F32 = jnp.float32
BF16 = jnp.bfloat16
VMEM_LIMIT = 56 * 1024 * 1024


def iota(shape, dim):
    return lax.broadcasted_iota(jnp.int32, shape, dim)


def split3(v):
    hi = v.astype(BF16).astype(F32)
    mid = (v - hi).astype(BF16).astype(F32)
    return hi, mid, v - hi - mid


def widen(table, first):
    rows = table.shape[0]
    low = iota((rows, LANE), 1) < HEAD_DIM
    cols = [jnp.broadcast_to(table[:, first + q : first + q + 1], (rows, LANE)) for q in range(4)]
    return jnp.concatenate([jnp.where(low, cols[0], cols[1]), jnp.where(low, cols[2], cols[3])], axis=1)


def head_place():
    return lax.axis_index("y") * 2 + lax.axis_index("core")


def prep_kernel(len_ref, decay_ref, step_ref, conv_ref, tab_ref, dt_ref, cand_ref, rows_ref, sems):
    first_row = len_ref[0] - head_place() * TOK
    copies = []
    for k in range(KERNEL - 1):
        row = jnp.clip(first_row - (KERNEL - 1) + k, 0, TOK - 1)
        copy = pltpu.make_async_copy(conv_ref.at[pl.ds(row, 1)], rows_ref.at[pl.ds(k, 1)], sems.at[k])
        copy.start()
        copies.append(copy)
    to = iota((LANE, LANE), 1)
    head = ((to % 32) // 4) * 16 + (to // 32) * 4 + to % 4
    order = jnp.where(iota((LANE, LANE), 0) == head, 1.0, 0.0).astype(BF16)
    live = iota((TOK, LANE), 0) < first_row
    log_rate = jnp.where(live, jnp.dot(decay_ref[...], order, preferred_element_type=F32), 0.0)
    gain = jnp.where(live, jnp.dot(step_ref[...], order, preferred_element_type=F32), 0.0)
    upto = jnp.where(iota((TOK, TOK), 0) >= iota((TOK, TOK), 1), 1.0, 0.0).astype(BF16)
    running = jnp.dot(upto, log_rate.astype(BF16), preferred_element_type=F32)
    middle = running[TOK // 2 - 1 : TOK // 2]
    total = running[TOK - 1 : TOK]
    tab_ref[0] = jnp.exp(total - running) * gain
    tab_ref[1] = jnp.exp(middle - running) * gain
    tab_ref[2] = jnp.exp(running - middle)
    tab_ref[3] = jnp.exp(running)
    dt_ref[...] = jnp.broadcast_to(jnp.exp(total), (8, LANE))
    for k in range(KERNEL - 1):
        copies[k].wait()
        row = first_row - (KERNEL - 1) + k
        inside = jnp.where((row >= 0) & (row < TOK), 1.0, 0.0)
        cand_ref[k] = (rows_ref[k].astype(F32) * inside).astype(BF16)


def prep(seg_length, decay_log, step_size, conv_input):
    return pl.pallas_call(
        prep_kernel,
        in_specs=[
            pl.BlockSpec(memory_space=pltpu.SMEM),
            pl.BlockSpec(memory_space=pltpu.VMEM),
            pl.BlockSpec(memory_space=pltpu.VMEM),
            pl.BlockSpec(memory_space=pl.ANY),
        ],
        out_specs=[pl.BlockSpec(memory_space=pltpu.VMEM)] * 3,
        out_shape=[
            jax.ShapeDtypeStruct((4, TOK, LANE), F32),
            jax.ShapeDtypeStruct((8, LANE), F32),
            jax.ShapeDtypeStruct((KERNEL - 1, GROUPS, GW), BF16),
        ],
        scratch_shapes=[pltpu.VMEM((KERNEL - 1, GROUPS, GW), BF16), pltpu.SemaphoreType.DMA((KERNEL - 1,))],
        compiler_params=pltpu.CompilerParams(vmem_limit_bytes=VMEM_LIMIT),
        name="prep",
    )(seg_length, decay_log, step_size, conv_input)


def conv_kernel(core_ref, conv_ref, halo_ref, w_ref, decay_ref, x_ref, bc_ref, own_ref, oth_ref, act_ref, bt_ref):
    step = pl.program_id(0)
    core = core_ref[0]
    taps = [w_ref[k] * 0.5 for k in range(KERNEL)]
    bias = w_ref[KERNEL] * 0.5

    def activate(window, at):
        half = bias[None] + taps[0][None] * window[0:8]
        for k in range(1, KERNEL):
            half = half + taps[k][None] * window[k : k + 8]
        half = half + half * jnp.tanh(half)
        for tile in range(2):
            act_ref[tile, pl.ds(at, 64), :] = half[:, :, tile * LANE : (tile + 1) * LANE].reshape(64, LANE)

    def of_group(g):
        return jnp.concatenate([act_ref[tile, pl.ds(g, TOK, stride=GROUPS), :] for tile in range(2)], axis=1)

    activate(jnp.concatenate([halo_ref[...].astype(F32), conv_ref[0:8].astype(F32)], axis=0), 0)

    def tokens(i, carry):
        activate(conv_ref[pl.ds(i * 8 - (KERNEL - 1), 8 + KERNEL - 1)].astype(F32), pl.multiple_of(i * 64, 64))
        return carry

    lax.fori_loop(1, TOK // 8, tokens, 0, unroll=3)

    @pl.when(step == 0)
    def _():
        for g in range(GROUPS):
            both = of_group(g)
            bc_ref[g] = both.astype(BF16)
            bt_ref[g] = both[:, :LANE].T.astype(BF16)

    @pl.when(step > 0)
    def _():
        decay = pltpu.roll(decay_ref[...], (LANE - 32 * (step - 1)) % LANE, 1)
        for g in range(GROUPS):
            x = of_group(g)
            x_ref[g] = x.astype(BF16)
            carried = (x * widen(decay, g * 4)).astype(BF16)
            state = jnp.dot(bt_ref[g], carried, preferred_element_type=F32).astype(BF16)

            def put(ref):
                for tile in range(2):
                    for part in range(2):
                        ref[g % 4, 0, tile * 2 + part] = state[part * 64 : part * 64 + 64, tile * LANE : (tile + 1) * LANE]

            pl.when(core == g // 4)(functools.partial(put, own_ref))
            pl.when(core != g // 4)(functools.partial(put, oth_ref))


def conv_states(core, conv_input, halo, weights, decay):
    lanes = lambda j, s: (0, 0, (j + 4) % 5)
    later = lambda j: jnp.maximum(j - 1, 0)
    half = jax.ShapeDtypeStruct((4, 4, 4, 64, LANE), BF16)
    half_spec = pl.BlockSpec((4, 1, 4, 64, LANE), lambda j, s: (0, later(j), 0, 0, 0))
    return pl.pallas_call(
        conv_kernel,
        grid_spec=pltpu.PrefetchScalarGridSpec(
            num_scalar_prefetch=1,
            grid=(5,),
            in_specs=[
                pl.BlockSpec((TOK, GROUPS, LW), lanes),
                pl.BlockSpec((KERNEL - 1, GROUPS, LW), lanes),
                pl.BlockSpec((KERNEL + 1, GROUPS, LW), lanes),
                pl.BlockSpec((TOK, LANE), lambda j, s: (0, 0)),
            ],
            out_specs=[
                pl.BlockSpec((GROUPS, TOK, LW), lambda j, s: (0, 0, later(j))),
                pl.BlockSpec((GROUPS, TOK, LW), lambda j, s: (0, 0, 0)),
                half_spec,
                half_spec,
            ],
            scratch_shapes=[pltpu.VMEM((2, TOK * GROUPS, LANE), F32), pltpu.VMEM((GROUPS, LANE, TOK), BF16)],
        ),
        out_shape=[
            jax.ShapeDtypeStruct((GROUPS, TOK, XW), BF16),
            jax.ShapeDtypeStruct((GROUPS, TOK, LW), BF16),
            half,
            half,
        ],
        compiler_params=pltpu.CompilerParams(vmem_limit_bytes=VMEM_LIMIT),
        name="conv_states",
    )(core, conv_input, halo, weights, decay)


def combine_kernel(core_ref, first_ref, own_ref, sib_ref, dto_ref, dts_ref, out_ref):
    core = core_ref[0]
    keep = jnp.where(lax.axis_index("y") == 0, 1 - first_ref[0], 1).astype(F32)
    shift = (2 * LANE - 16 * core - 4 * pl.program_id(0)) % LANE
    d_own = pltpu.roll(dto_ref[...], shift, 1)
    d_sib = pltpu.roll(dts_ref[...], shift, 1)
    on_own = jnp.where(core == 0, d_sib, 1.0)
    on_sib = jnp.where(core == 1, d_own, 1.0)
    row = iota((16, LANE), 0)
    for j in range(4):
        a, b, d = (widen(v, 32 * j)[0:1] for v in (on_own, on_sib, d_own * d_sib))
        hi, mid, low = split3(d)
        for tile in range(2):
            at = slice(tile * LANE, (tile + 1) * LANE)
            extra = jnp.where(row == 0, hi[:, at], jnp.where(row == 1, mid[:, at], jnp.where(row == 2, low[:, at], keep)))
            for part in range(2):
                state = own_ref[0, j, tile * 2 + part].astype(F32) * a[:, at]
                state = state + sib_ref[0, j, tile * 2 + part].astype(F32) * b[:, at]
                piece = (j * 2 + tile) * 2 + part
                out_ref[piece, 0:64] = state.astype(BF16)
                out_ref[piece, 64:ROWS] = extra.astype(BF16)


def combine(core, seg_first, own, sib, d_own, d_sib):
    half_spec = pl.BlockSpec((1, 4, 4, 64, LANE), lambda i, s: (i, 0, 0, 0, 0))
    row_spec = pl.BlockSpec((8, LANE), lambda i, s: (0, 0))
    return pl.pallas_call(
        combine_kernel,
        grid_spec=pltpu.PrefetchScalarGridSpec(
            num_scalar_prefetch=1,
            grid=(4,),
            in_specs=[pl.BlockSpec(memory_space=pltpu.SMEM), half_spec, half_spec, row_spec, row_spec],
            out_specs=pl.BlockSpec((16, ROWS, LANE), lambda i, s: (i, 0, 0)),
        ),
        out_shape=jax.ShapeDtypeStruct((CHUNKS, ROWS, LANE), BF16),
        compiler_params=pltpu.CompilerParams(vmem_limit_bytes=VMEM_LIMIT),
        name="combine",
    )(core, seg_first, own, sib, d_own, d_sib)


def scan_kernel(chips, in_ref, out_ref):
    each = in_ref.shape[0] // chips

    def chip(c, states):
        after = []
        for i, state in enumerate(states):
            at = c * each + i
            extra = in_ref[at, 64:ROWS].astype(F32)
            state = extra[3:4] * state
            out_ref[at] = state.astype(BF16)
            decay = extra[0:1] + extra[1:2] + extra[2:3]
            after.append(decay * state + in_ref[at, 0:64].astype(F32))
        return tuple(after)

    lax.fori_loop(0, chips, chip, tuple(jnp.zeros((64, LANE), F32) for _ in range(each)), unroll=4)


def scan(chips, pieces):
    return pl.pallas_call(
        functools.partial(scan_kernel, chips),
        in_specs=[pl.BlockSpec(memory_space=pltpu.VMEM)],
        out_specs=pl.BlockSpec(memory_space=pltpu.VMEM),
        out_shape=jax.ShapeDtypeStruct((CHUNKS, 64, LANE), BF16),
        compiler_params=pltpu.CompilerParams(vmem_limit_bytes=VMEM_LIMIT),
        name="scan",
    )(pieces)


def local_kernel(other, core_ref, len_ref, x_ref, bc_ref, tab_ref, before_ref, dts_ref, gate_ref, skip_ref, p_ref, q_ref):
    core = core_ref[0]
    group = ((core + other) % 2) * 4 + pl.program_id(0)
    shift = (LANE - 4 * group) % LANE
    inner, after, since = (pltpu.roll(tab_ref[k], shift, 1) for k in (1, 2, 3))
    d_before = jnp.where(core == 1, pltpu.roll(dts_ref[...], shift, 1), 1.0)
    b = bc_ref[0, :, :LANE]
    c = bc_ref[0, :, LANE:]
    scores = lax.dot_general(c, b, (((1,), (1,)), ((), ())), preferred_element_type=F32)
    causal = iota((TOK, TOK), 0) >= iota((TOK, TOK), 1)
    scores = jnp.where(causal, scores, 0.0).astype(BF16)
    live = iota((TOK, LW), 0) < len_ref[0] - head_place() * TOK
    for j in range(4):
        at = slice(j * LW, (j + 1) * LW)
        x = x_ref[0, :, at].astype(F32)
        scaled = (x * widen(inner, 32 * j)).astype(BF16)
        y = widen(after, 32 * j) * jnp.dot(scores, scaled, preferred_element_type=F32)
        before = jnp.concatenate(
            [jnp.concatenate([before_ref[0, j, tile * 2], before_ref[0, j, tile * 2 + 1]], axis=0) for tile in range(2)],
            axis=1,
        )
        grown = widen(since, 32 * j)
        y = y + grown * (core.astype(F32) * jnp.dot(c, before, preferred_element_type=F32))
        y = y + skip_ref[:, at] * x
        half = gate_ref[:, at].astype(F32) * 0.5
        silu = half + half * jnp.tanh(half)
        p_ref[0, :, at] = jnp.where(live, y * silu, 0.0).astype(BF16)
        q_ref[0, :, at] = jnp.where(live, grown * widen(d_before, 32 * j)[0:1] * silu, 0.0).astype(BF16)


def local(other, core, seg_length, x, bc, tables, before, d_sib, gate_input, skip):
    group = lambda i, s: ((s[0] + other) % 2) * 4 + i
    out = jax.ShapeDtypeStruct((4, TOK, XW), BF16)
    out_spec = pl.BlockSpec((1, TOK, XW), lambda i, s: (i, 0, 0))
    return pl.pallas_call(
        functools.partial(local_kernel, other),
        grid_spec=pltpu.PrefetchScalarGridSpec(
            num_scalar_prefetch=1,
            grid=(4,),
            in_specs=[
                pl.BlockSpec(memory_space=pltpu.SMEM),
                pl.BlockSpec((1, TOK, XW), lambda i, s: (group(i, s), 0, 0)),
                pl.BlockSpec((1, TOK, LW), lambda i, s: (group(i, s), 0, 0)),
                pl.BlockSpec((4, TOK, LANE), lambda i, s: (0, 0, 0)),
                pl.BlockSpec((1, 4, 4, 64, LANE), lambda i, s: (i, 0, 0, 0, 0)),
                pl.BlockSpec((8, LANE), lambda i, s: (0, 0)),
                pl.BlockSpec((TOK, XW), lambda i, s: (0, group(i, s))),
                pl.BlockSpec((1, XW), lambda i, s: (0, group(i, s))),
            ],
            out_specs=[out_spec, out_spec],
        ),
        out_shape=[out, out],
        compiler_params=pltpu.CompilerParams(vmem_limit_bytes=VMEM_LIMIT),
        cost_estimate=pl.CostEstimate(flops=400_000_000, bytes_accessed=8_000_000, transcendentals=600_000),
        name="local",
    )(core, seg_length, x, bc, tables, before, d_sib, gate_input, skip)


def finish_kernel(core_ref, p_ref, q_ref, c_ref, state_ref, gain_ref, *rest):
    out_ref = rest[-1]
    c = c_ref[0]
    gated = []
    for tile in range(0, 8, 2):
        state = jnp.concatenate(
            [jnp.concatenate([state_ref[(tile + k) * 2], state_ref[(tile + k) * 2 + 1]], axis=0) for k in range(2)],
            axis=1,
        )
        at = slice(tile * LANE, (tile + 2) * LANE)
        read = jnp.dot(c, state, preferred_element_type=F32)
        gated.append(p_ref[0, :, at].astype(F32) + read * q_ref[0, :, at].astype(F32))
    total = sum(jnp.sum(v * v, axis=1, keepdims=True) for v in gated)
    scale = lax.rsqrt(total / XW + EPSILON)
    for j, v in enumerate(gated):
        at = slice(j * LW, (j + 1) * LW)
        out_ref[:, at] = (v * scale * gain_ref[:, at]).astype(BF16)


def finish(other, core, p, q, bc, states, gain, out=None):
    group = lambda i, s: ((s[0] + other) % 2) * 4 + i
    operands = [core, p, q, bc, states, gain]
    in_specs = [
        pl.BlockSpec((1, TOK, XW), lambda i, s: (i, 0, 0)),
        pl.BlockSpec((1, TOK, XW), lambda i, s: (i, 0, 0)),
        pl.BlockSpec((1, TOK, LANE), lambda i, s: (group(i, s), 0, 1)),
        pl.BlockSpec((16, 64, LANE), lambda i, s: (i, 0, 0)),
        pl.BlockSpec((1, XW), lambda i, s: (0, group(i, s))),
    ]
    aliases = {}
    if out is not None:
        operands.append(out)
        in_specs.append(pl.BlockSpec(memory_space=pl.ANY))
        aliases = {6: 0}
    return pl.pallas_call(
        finish_kernel,
        grid_spec=pltpu.PrefetchScalarGridSpec(
            num_scalar_prefetch=1,
            grid=(4,),
            in_specs=in_specs,
            out_specs=pl.BlockSpec((TOK, XW), lambda i, s: (0, group(i, s))),
        ),
        out_shape=jax.ShapeDtypeStruct((TOK, GROUPS * XW), BF16),
        input_output_aliases=aliases,
        compiler_params=pltpu.CompilerParams(vmem_limit_bytes=VMEM_LIMIT),
        cost_estimate=pl.CostEstimate(flops=200_000_000, bytes_accessed=4_000_000, transcendentals=1000),
        name="finish",
    )(*operands)


def body(
    conv_input,
    gate_input,
    step_size,
    decay_log,
    conv_weight,
    conv_bias,
    skip_gain,
    norm_gain,
    seg_length,
    seg_first,
):
    segments = lax.axis_size("seq")
    in_segment = lax.axis_size("y") * lax.axis_size("core")
    count = segments * in_segment
    chips = count // 2
    core = lax.axis_index("core").astype(jnp.int32).reshape(1)
    swap = [(0, 1), (1, 0)]

    last = lax.ppermute(
        conv_input[TOK - (KERNEL - 1) :], AXES, [(i, i + 1) for i in range(count) if (i + 1) % in_segment]
    )
    tables, d_own, cand = prep(seg_length, decay_log, step_size, conv_input)
    tails = [
        lax.ppermute(cand, AXES, [(s * in_segment + h, (s + 1) * in_segment) for s in range(segments - 1)])
        for h in range(in_segment)
    ]
    d_sib = lax.ppermute(d_own, "core", swap)
    weights = jnp.concatenate([conv_weight[:, 0], conv_bias], axis=0)
    weights = jnp.broadcast_to(weights[None], (GROUPS,) + weights.shape)
    weights = lax.all_to_all(weights, ("y", "core"), 0, 0, tiled=True).transpose(1, 0, 2)
    keep = (1 - seg_first[0]).astype(BF16)
    halo = last + keep * functools.reduce(jnp.add, tails)

    x, bc, own, oth = conv_states(core, conv_input, halo, weights, tables[0])
    sib_own = lax.ppermute(oth, "core", swap)
    pieces = combine(core, seg_first, own, sib_own, d_own, d_sib)
    pieces = lax.all_to_all(pieces, CHIPS, 0, 0, tiled=True)
    sib_oth = lax.ppermute(own, "core", swap[:1])

    skip = jnp.repeat(skip_gain, HEAD_DIM)[None]
    p_own, q_own = local(0, core, seg_length, x, bc, tables, sib_own, d_sib, gate_input, skip)
    p_oth, q_oth = local(1, core, seg_length, x, bc, tables, sib_oth, d_sib, gate_input, skip)

    states = lax.all_to_all(scan(chips, pieces), CHIPS, 0, 0, tiled=True)
    states_oth = lax.ppermute(states, "core", swap)
    gain = norm_gain[None]
    out = finish(0, core, p_own, q_own, bc, states, gain)
    return finish(1, core, p_oth, q_oth, bc, states_oth, gain, out)


def solution(mesh):
    segments, in_segment = mesh.devices.shape
    fine = Mesh(mesh.devices.reshape(segments, in_segment // 2, 2), AXES)
    tokens = P(AXES, None)
    return jax.shard_map(
        body,
        mesh=fine,
        in_specs=(
            P(AXES, None, None),
            tokens,
            tokens,
            tokens,
            P(None, ("y", "core"), None),
            P(("y", "core"), None),
            P(),
            P(),
            P("seq"),
            P("seq"),
        ),
        out_specs=tokens,
        check_vma=False,
    )
```

time: 495 us -> 140 us (0.28)
  the two profiles are of different devices: /device:TPU:6 before, /device:TPU:1 now
where the time goes in v1:
time: 140 us; the launch traced here: 139 us
  Pallas kernels  48 us (34%)
  starting transfers between devices  33.5 us (24%)
  blocking collectives  31.6 us (23%)
  waiting for transfers between devices  17.3 us (12%)
  local copies, waits for them, and re-layouts  6.57 us (5%)
  between operations  1.56 us (1%)
    all_to_all x1, blocking collectives, body(): pieces = lax.all_to_all(pieces, CHIPS, 0, 0, tiled=True)  31.6 us
    pallas_call x1, Pallas kernels, conv_states(): pl.pallas_call(conv_kernel, grid_spec=pltpu.PrefetchScalarGridSpec(num_sc...  15.9 us
    all_to_all x1, waiting for transfers between devices, body(): states = lax.all_to_all(scan(chips, pieces), CHIPS, 0, 0, tiled=True)  14.9 us
    pallas_call x2, Pallas kernels, local(): pl.pallas_call(functools.partial(local_kernel, other), grid_spec=pltpu.Pr...  14.1 us
    ppermute x8, starting transfers between devices, body(): lax.ppermute(cand, AXES, [(s * in_segment + h, (s + 1) * in_segment) for...  12.7 us
    pallas_call x2, Pallas kernels, finish(): pl.pallas_call(finish_kernel, grid_spec=pltpu.PrefetchScalarGridSpec(num_...  8.75 us
    all_to_all x1, starting transfers between devices, body(): lax.all_to_all(weights, ('y', 'core'), 0, 0, tiled=True).transpose(1, 0, 2)  6.52 us
    all_to_all x1, starting transfers between devices, body(): states = lax.all_to_all(scan(chips, pieces), CHIPS, 0, 0, tiled=True)  5.67 us
  transfers between devices with their start and end apart: 15, of which 3 were waited for; matrix products, arithmetic and copies ran while one was open for 3% of the time, Pallas kernels for 13%

profile of v1, /device:TPU:1, one launch (start us, length us, event | category | flops | bytes accessed | tf_op | source)
XLA Modules:
  0.0 139.2 jit_solution(17730804845810813631)
XLA Ops:
  0.7 2.4 %prep.1 = (f32[4,128,128]{2,1,0:T(8,128)}, f32[8,128]{1,0:T(8,128)}, bf16[3,8,1280]{2,1,0:T(8,128)(2,1)}) custom-call(s32[1]{0:T(128)S(6)} %copy.19.len_ref, bf16[128,128]{1,0:T(8,128)(2,1)} %decay_ref.1, bf16[128,128]{1,0:T(8,128)(2,1)} %step_ref.1, bf16[128,8,1280]{2,1,0:T(8,128)(2,1)} %conv_ref.3), custom_call_target="tpu_custom_call" | custom-call | tf_op jit(solution)/shard_map/prep/pallas_call | solution.py:80
  3.7 8.0 %collective-permute-start.2 = (bf16[3,8,1280]{2,1,0:T(8,128)(2,1)}, bf16[3,8,1280]{2,1,0:T(8,128)(2,1)S(1)}, u32[]{:S(2)}, u32[]{:S(2)}) collective-permute-start(bf16[3,8,1280]{2,1,0:T(8,128)(2,1)} %get-tuple-element.16), channel_id=1, source_target_pairs={{1,8},{9,16},{17,24},{25,32},{33,40},{41,48},{49,56},{57,64},{65,7... | collective-permute-start | bytes 184328 | tf_op jit(solution)/shard_map/ppermute | solution.py:385
  13.8 0.7 broadcast_in_dim.12
  14.6 6.5 %all-to-all-start = ((f32[8,5,1280]{2,1,0:T(8,128)}), f32[8,5,1280]{2,1,0:T(8,128)S(1)}, u32[]{:S(2)}, u32[]{:S(2)}) async-start(f32[8,5,1280]{2,1,0:T(8,128)} %broadcast_in_dim.12), calls=%async_computation | async-start | bytes 655360 | tf_op jit(solution)/shard_map/all_to_all | solution.py:391
  21.1 0.8 slice.6
  24.0 3.5 %collective-permute-start = (bf16[3,8,1280]{2,1,0:T(8,128)(2,1)S(1)}, bf16[3,8,1280]{2,1,0:T(8,128)(2,1)S(1)}, u32[]{:S(2)}, u32[]{:S(2)}) collective-permute-start(bf16[3,8,1280]{2,1,0:T(8,128)(2,1)S(1)} %slice.6), channel_id=1, source_target_pairs={{0,1},{1,2},{2,3},{3,4},{4,5},{5,6},{6,7},{8,9},{9,10},{10,11},{11... | collective-permute-start | bytes 184328 | tf_op jit(solution)/shard_map/ppermute | solution.py:380
  27.5 1.5 %slice_bitcast_fusion.decay_ref = f32[128,128]{1,0:T(8,128)} fusion(f32[4,128,128]{2,1,0:T(8,128)} %get-tuple-element.17.tab_ref), kind=kLoop, calls=%fused_computation.1 | loop fusion | bytes 131072 | tf_op jit(solution)/shard_map/squeeze | solution.py:395
  30.4 0.7 copy.16
  31.1 15.9 %conv_states.1 = (bf16[8,128,1024]{2,1,0:T(8,128)(2,1)}, bf16[8,128,256]{2,1,0:T(8,128)(2,1)}, bf16[4,4,4,64,128]{4,3,2,1,0:T(8,128)(2,1)}, bf16[4,4,4,64,128]{4,3,2,1,0:T(8,128)(2,1)}) custom-call(s32[1]{0:T(128)} %bitcast.core_ref, bf16[128,8,1280]{2,1,0:T(8,128)(2,1)} %conv_ref.3, bf16[3,8,1280]{2,1,0:T(8,128)(2,1)} %multiply_add_fusion.halo_ref, ...), custom_call_target="tpu_custom_call" | custom-call | tf_op jit(solution)/shard_map/conv_states/pallas_call | solution.py:155
  47.5 1.8 %collective-permute-done.10.dts_ref = f32[8,128]{1,0:T(8,128)S(1)} collective-permute-done((f32[8,128]{1,0:T(8,128)S(1)}, f32[8,128]{1,0:T(8,128)S(1)}, u32[]{:S(2)}, u32[]{:S(2)}) %collective-permute-start.10) | collective-permute-done | bytes 4128 | tf_op jit(solution)/shard_map/ppermute | solution.py:388
  49.9 1.0 copy-done
  50.8 4.1 %combine.1 = bf16[64,80,128]{2,1,0:T(8,128)(2,1)} custom-call(s32[1]{0:T(128)} %bitcast.core_ref, s32[1]{0:T(128)S(6)} %copy.20.first_ref, bf16[4,4,4,64,128]{4,3,2,1,0:T(8,128)(2,1)} %get-tuple-element.20.own_ref, bf16[4,4,4,64,128]{4,3,2,1,0:T(8,128)(2,1)} %copy-done, f32[8,128]{1,0:T(8,128)} %get-tuple-element.21.dto_ref, f32[8,128]{1,0:T(8,128)} %copy-done.4), custom_call_target="tpu_custom_call" | custom-call | tf_op jit(solution)/shard_map/combine/pallas_call | solution.py:211
  54.9 31.6 %all_to_all.15.in_ref = bf16[64,80,128]{2,1,0:T(8,128)(2,1)} all-to-all(bf16[64,80,128]{2,1,0:T(8,128)(2,1)} %combine.1), channel_id=1, replica_groups=mesh['seq'=16,'y'=4,'core'=2] {'seq','y'}, dimensions={0} | all-to-all | bytes 2621440 | tf_op jit(solution)/shard_map/all_to_all | solution.py:398
  86.6 2.8 %scan.1 = bf16[64,64,128]{2,1,0:T(8,128)(2,1)} custom-call(bf16[64,80,128]{2,1,0:T(8,128)(2,1)} %all_to_all.15.in_ref), custom_call_target="tpu_custom_call" | custom-call | tf_op jit(solution)/shard_map/scan/pallas_call | solution.py:243
  89.4 5.7 %all-to-all-start.2 = ((bf16[64,64,128]{2,1,0:T(8,128)(2,1)}), bf16[64,64,128]{2,1,0:T(8,128)(2,1)S(1)}, u32[]{:S(2)}, u32[]{:S(2)}) async-start(bf16[64,64,128]{2,1,0:T(8,128)(2,1)} %scan.1), calls=%async_computation.2 | async-start | bytes 2097152 | tf_op jit(solution)/shard_map/all_to_all | solution.py:405
  95.1 1.3 collective-permute-start.9
  96.4 14.9 %all-to-all-done.2.state_ref = bf16[64,64,128]{2,1,0:T(8,128)(2,1)S(1)} async-done(((bf16[64,64,128]{2,1,0:T(8,128)(2,1)}), bf16[64,64,128]{2,1,0:T(8,128)(2,1)S(1)}, u32[]{:S(2)}, u32[]{:S(2)}) %all-to-all-start.2) | async-done | bytes 1048608 | tf_op jit(solution)/shard_map/all_to_all | solution.py:405
  111.3 3.3 %collective-permute-start.12 = (bf16[64,64,128]{2,1,0:T(8,128)(2,1)S(1)}, bf16[64,64,128]{2,1,0:T(8,128)(2,1)S(1)}, u32[]{:S(2)}, u32[]{:S(2)}) collective-permute-start(bf16[64,64,128]{2,1,0:T(8,128)(2,1)S(1)} %all-to-all-done.2.state_ref), channel_id=1, source_target_pairs={{0,1},{1,0},{2,3},{3,2},{4,5},{5,4},{6,7},{7,6},{8,9},{9,8},{10,11... | collective-permute-start | bytes 3145736 | tf_op jit(solution)/shard_map/ppermute | solution.py:406
  114.6 0.7 broadcast_in_dim_reshape.3.skip_ref
  115.4 7.0 %local.3 = (bf16[4,128,1024]{2,1,0:T(8,128)(2,1)}, bf16[4,128,1024]{2,1,0:T(8,128)(2,1)}) custom-call(s32[1]{0:T(128)} %bitcast.core_ref, s32[1]{0:T(128)S(6)} %copy.19.len_ref, bf16[8,128,1024]{2,1,0:T(8,128)(2,1)} %get-tuple-element.18.x_ref, bf16[8,128,256]{2,1,0:T(8,128)(2,1)} %get-tuple-element.19.bc_ref.c_ref, ...), custom_call_target="tpu_custom_call" | custom-call | flops 400000000 | bytes 8000000 | tf_op jit(solution)/shard_map/local/pallas_call | solution.py:287
  122.4 7.1 %local.2 = (bf16[4,128,1024]{2,1,0:T(8,128)(2,1)}, bf16[4,128,1024]{2,1,0:T(8,128)(2,1)}) custom-call(s32[1]{0:T(128)} %bitcast.core_ref, s32[1]{0:T(128)S(6)} %copy.19.len_ref, bf16[8,128,1024]{2,1,0:T(8,128)(2,1)} %get-tuple-element.18.x_ref, bf16[8,128,256]{2,1,0:T(8,128)(2,1)} %get-tuple-element.19.bc_ref.c_ref, ...), custom_call_target="tpu_custom_call" | custom-call | flops 400000000 | bytes 8000000 | tf_op jit(solution)/shard_map/local/pallas_call | solution.py:287
  129.5 4.4 %finish.2.rest_0_ = bf16[128,8192]{1,0:T(8,128)(2,1)} custom-call(s32[1]{0:T(128)} %bitcast.core_ref, bf16[4,128,1024]{2,1,0:T(8,128)(2,1)} %get-tuple-element.25.p_ref, bf16[4,128,1024]{2,1,0:T(8,128)(2,1)} %get-tuple-element.26.q_ref, bf16[8,128,256]{2,1,0:T(8,128)(2,1)} %get-tuple-element.19.bc_ref.c_ref, bf16[64,64,128]{2,1,0:T(8,128)(2,1)} %copy-done.1, ...), custom_call_target="tpu_custom_call" | custom-call | flops 200000000 | bytes 4000000 | tf_op jit(solution)/shard_map/finish/pallas_call | solution.py:345
  133.8 1.0 copy-done.2
  134.8 4.4 %finish.3 = bf16[128,8192]{1,0:T(8,128)(2,1)} custom-call(s32[1]{0:T(128)} %bitcast.core_ref, bf16[4,128,1024]{2,1,0:T(8,128)(2,1)} %get-tuple-element.22.p_ref, bf16[4,128,1024]{2,1,0:T(8,128)(2,1)} %get-tuple-element.23.q_ref, bf16[8,128,256]{2,1,0:T(8,128)(2,1)} %get-tuple-element.19.bc_ref.c_ref, ...), custom_call_target="tpu_custom_call", output_to_operand_aliasing={{}: (6, {})} | custom-call | flops 200000000 | bytes 4000000 | tf_op jit(solution)/shard_map/finish/pallas_call | solution.py:345
  (42 shorter events, 6.6 us)
Async XLA Ops:
  0.0 13.8 %copy-start.5 = (f32[4,1,1280]{2,1,0:T(1,128)S(1)}, f32[4,1,1280]{2,1,0:T(1,128)}, u32[]{:S(2)}) copy-start(f32[4,1,1280]{2,1,0:T(1,128)} %param.14) | copy-start | bytes 61444
  0.0 13.8 %copy-start.6 = (f32[1,1280]{1,0:T(1,128)S(1)}, f32[1,1280]{1,0:T(1,128)}, u32[]{:S(2)}) copy-start(f32[1,1280]{1,0:T(1,128)} %param.15) | copy-start | bytes 15364
  3.1 18.9 %collective-permute-start.1 = (bf16[3,8,1280]{2,1,0:T(8,128)(2,1)}, bf16[3,8,1280]{2,1,0:T(8,128)(2,1)S(1)}, u32[]{:S(2)}, u32[]{:S(2)}) collective-permute-start(bf16[3,8,1280]{2,1,0:T(8,128)(2,1)} %get-tuple-element.16), channel_id=1, source_target_pairs={{0,8},{8,16},{16,24},{24,32},{32,40},{40,48},{48,56},{56,64},{64,7... | collective-permute-start | bytes 184328 | tf_op jit(solution)/shard_map/ppermute | solution.py:385
  3.7 18.9 %collective-permute-start.2 = (bf16[3,8,1280]{2,1,0:T(8,128)(2,1)}, bf16[3,8,1280]{2,1,0:T(8,128)(2,1)S(1)}, u32[]{:S(2)}, u32[]{:S(2)}) collective-permute-start(bf16[3,8,1280]{2,1,0:T(8,128)(2,1)} %get-tuple-element.16), channel_id=1, source_target_pairs={{1,8},{9,16},{17,24},{25,32},{33,40},{41,48},{49,56},{57,64},{65,7... | collective-permute-start | bytes 184328 | tf_op jit(solution)/shard_map/ppermute | solution.py:385
  11.8 11.5 %collective-permute-start.3 = (bf16[3,8,1280]{2,1,0:T(8,128)(2,1)}, bf16[3,8,1280]{2,1,0:T(8,128)(2,1)S(1)}, u32[]{:S(2)}, u32[]{:S(2)}) collective-permute-start(bf16[3,8,1280]{2,1,0:T(8,128)(2,1)} %get-tuple-element.16), channel_id=1, source_target_pairs={{2,8},{10,16},{18,24},{26,32},{34,40},{42,48},{50,56},{58,64},{66,... | collective-permute-start | bytes 184328 | tf_op jit(solution)/shard_map/ppermute | solution.py:385
  12.4 11.5 %collective-permute-start.4 = (bf16[3,8,1280]{2,1,0:T(8,128)(2,1)}, bf16[3,8,1280]{2,1,0:T(8,128)(2,1)S(1)}, u32[]{:S(2)}, u32[]{:S(2)}) collective-permute-start(bf16[3,8,1280]{2,1,0:T(8,128)(2,1)} %get-tuple-element.16), channel_id=1, source_target_pairs={{3,8},{11,16},{19,24},{27,32},{35,40},{43,48},{51,56},{59,64},{67,... | collective-permute-start | bytes 184328 | tf_op jit(solution)/shard_map/ppermute | solution.py:385
  13.1 16.5 %collective-permute-start.5 = (bf16[3,8,1280]{2,1,0:T(8,128)(2,1)}, bf16[3,8,1280]{2,1,0:T(8,128)(2,1)S(1)}, u32[]{:S(2)}, u32[]{:S(2)}) collective-permute-start(bf16[3,8,1280]{2,1,0:T(8,128)(2,1)} %get-tuple-element.16), channel_id=1, source_target_pairs={{4,8},{12,16},{20,24},{28,32},{36,40},{44,48},{52,56},{60,64},{68,... | collective-permute-start | bytes 184328 | tf_op jit(solution)/shard_map/ppermute | solution.py:385
  14.6 15.8 %all-to-all-start = ((f32[8,5,1280]{2,1,0:T(8,128)}), f32[8,5,1280]{2,1,0:T(8,128)S(1)}, u32[]{:S(2)}, u32[]{:S(2)}) async-start(f32[8,5,1280]{2,1,0:T(8,128)} %broadcast_in_dim.12), calls=%async_computation | async-start | bytes 655360 | tf_op jit(solution)/shard_map/all_to_all | solution.py:391
  21.9 7.7 %collective-permute-start.6 = (bf16[3,8,1280]{2,1,0:T(8,128)(2,1)}, bf16[3,8,1280]{2,1,0:T(8,128)(2,1)S(1)}, u32[]{:S(2)}, u32[]{:S(2)}) collective-permute-start(bf16[3,8,1280]{2,1,0:T(8,128)(2,1)} %get-tuple-element.16), channel_id=1, source_target_pairs={{5,8},{13,16},{21,24},{29,32},{37,40},{45,48},{53,56},{61,64},{69,... | collective-permute-start | bytes 184328 | tf_op jit(solution)/shard_map/ppermute | solution.py:385
  22.6 7.1 %collective-permute-start.7 = (bf16[3,8,1280]{2,1,0:T(8,128)(2,1)}, bf16[3,8,1280]{2,1,0:T(8,128)(2,1)S(1)}, u32[]{:S(2)}, u32[]{:S(2)}) collective-permute-start(bf16[3,8,1280]{2,1,0:T(8,128)(2,1)} %get-tuple-element.16), channel_id=1, source_target_pairs={{6,8},{14,16},{22,24},{30,32},{38,40},{46,48},{54,56},{62,64},{70,... | collective-permute-start | bytes 184328 | tf_op jit(solution)/shard_map/ppermute | solution.py:385
  23.3 6.4 %collective-permute-start.8 = (bf16[3,8,1280]{2,1,0:T(8,128)(2,1)}, bf16[3,8,1280]{2,1,0:T(8,128)(2,1)S(1)}, u32[]{:S(2)}, u32[]{:S(2)}) collective-permute-start(bf16[3,8,1280]{2,1,0:T(8,128)(2,1)} %get-tuple-element.16), channel_id=1, source_target_pairs={{7,8},{15,16},{23,24},{31,32},{39,40},{47,48},{55,56},{63,64},{71,... | collective-permute-start | bytes 184328 | tf_op jit(solution)/shard_map/ppermute | solution.py:385
  24.0 5.7 %collective-permute-start = (bf16[3,8,1280]{2,1,0:T(8,128)(2,1)S(1)}, bf16[3,8,1280]{2,1,0:T(8,128)(2,1)S(1)}, u32[]{:S(2)}, u32[]{:S(2)}) collective-permute-start(bf16[3,8,1280]{2,1,0:T(8,128)(2,1)S(1)} %slice.6), channel_id=1, source_target_pairs={{0,1},{1,2},{2,3},{3,4},{4,5},{5,6},{6,7},{8,9},{9,10},{10,11},{11... | collective-permute-start | bytes 184328 | tf_op jit(solution)/shard_map/ppermute | solution.py:380
  27.5 19.5 %copy-start.7 = (f32[8,128]{1,0:T(8,128)S(1)}, f32[8,128]{1,0:T(8,128)}, u32[]{:S(2)}) copy-start(f32[8,128]{1,0:T(8,128)} %get-tuple-element.21.dto_ref) | copy-start | bytes 12292
  47.0 2.9 %collective-permute-start.11 = (bf16[4,4,4,64,128]{4,3,2,1,0:T(8,128)(2,1)}, bf16[4,4,4,64,128]{4,3,2,1,0:T(8,128)(2,1)S(1)}, u32[]{:S(2)}, u32[]{:S(2)}) collective-permute-start(bf16[4,4,4,64,128]{4,3,2,1,0:T(8,128)(2,1)} %get-tuple-element.24), channel_id=1, source_target_pairs={{0,1},{1,0},{2,3},{3,2},{4,5},{5,4},{6,7},{7,6},{8,9},{9,8},{10,11... | collective-permute-start | bytes 3145736 | tf_op jit(solution)/shard_map/ppermute | solution.py:396
  47.0 2.3 %collective-permute-start.10 = (f32[8,128]{1,0:T(8,128)S(1)}, f32[8,128]{1,0:T(8,128)S(1)}, u32[]{:S(2)}, u32[]{:S(2)}) collective-permute-start(f32[8,128]{1,0:T(8,128)S(1)} %copy-done.7), channel_id=1, source_target_pairs={{0,1},{1,0},{2,3},{3,2},{4,5},{5,4},{6,7},{7,6},{8,9},{9,8},{10,11... | collective-permute-start | bytes 12296 | tf_op jit(solution)/shard_map/ppermute | solution.py:388
  49.3 0.6 copy-start.4
  49.9 1.0 copy-start
  86.6 8.5 %copy-start.3 = (bf16[4,4,4,64,128]{4,3,2,1,0:T(8,128)(2,1)S(1)}, bf16[4,4,4,64,128]{4,3,2,1,0:T(8,128)(2,1)}, u32[]{:S(2)}) copy-start(bf16[4,4,4,64,128]{4,3,2,1,0:T(8,128)(2,1)} %get-tuple-element.20.own_ref) | copy-start | bytes 3145732
  86.6 28.0 %copy-start.8 = (f32[128]{0:T(128)S(1)}, f32[128]{0:T(128)}, u32[]{:S(2)}) copy-start(f32[128]{0:T(128)} %param.16) | copy-start | bytes 1540
  89.4 21.9 %all-to-all-start.2 = ((bf16[64,64,128]{2,1,0:T(8,128)(2,1)}), bf16[64,64,128]{2,1,0:T(8,128)(2,1)S(1)}, u32[]{:S(2)}, u32[]{:S(2)}) async-start(bf16[64,64,128]{2,1,0:T(8,128)(2,1)} %scan.1), calls=%async_computation.2 | async-start | bytes 2097152 | tf_op jit(solution)/shard_map/all_to_all | solution.py:405
  95.1 27.3 %collective-permute-start.9 = (bf16[4,4,4,64,128]{4,3,2,1,0:T(8,128)(2,1)S(1)}, bf16[4,4,4,64,128]{4,3,2,1,0:T(8,128)(2,1)}, u32[]{:S(2)}, u32[]{:S(2)}) collective-permute-start(bf16[4,4,4,64,128]{4,3,2,1,0:T(8,128)(2,1)S(1)} %copy-done.3), channel_id=1, source_target_pairs={{0,1},{2,3},{4,5},{6,7},{8,9},{10,11},{12,13},{14,15},{16,17},{18,... | collective-permute-start | bytes 3145736 | tf_op jit(solution)/shard_map/ppermute | solution.py:399
  111.3 11.1 %copy-start.1 = (bf16[64,64,128]{2,1,0:T(8,128)(2,1)}, bf16[64,64,128]{2,1,0:T(8,128)(2,1)S(1)}, u32[]{:S(2)}) copy-start(bf16[64,64,128]{2,1,0:T(8,128)(2,1)S(1)} %all-to-all-done.2.state_ref) | copy-start | bytes 3145732
  111.3 22.6 %collective-permute-start.12 = (bf16[64,64,128]{2,1,0:T(8,128)(2,1)S(1)}, bf16[64,64,128]{2,1,0:T(8,128)(2,1)S(1)}, u32[]{:S(2)}, u32[]{:S(2)}) collective-permute-start(bf16[64,64,128]{2,1,0:T(8,128)(2,1)S(1)} %all-to-all-done.2.state_ref), channel_id=1, source_target_pairs={{0,1},{1,0},{2,3},{3,2},{4,5},{5,4},{6,7},{7,6},{8,9},{9,8},{10,11... | collective-permute-start | bytes 3145736 | tf_op jit(solution)/shard_map/ppermute | solution.py:406
  133.8 1.0 copy-start.2

commit v2 on v1

v2 whole, which is shorter than its diff:
```python
import functools

import jax
import jax.numpy as jnp
from jax import lax
from jax.experimental import pallas as pl
from jax.experimental.pallas import tpu as pltpu
from jax.sharding import Mesh, PartitionSpec as P

HEAD_DIM = 64
KERNEL = 4
EPSILON = 1e-05
TOK = 128
GROUPS = 8
XW = 1024
GW = 1280
LANE = 128
LW = 256
CHUNKS = 64
ENDS = KERNEL - 1
PACK = 24
ROWS = 72
AXES = ("seq", "y", "core")
CHIPS = ("seq", "y")
F32 = jnp.float32
BF16 = jnp.bfloat16


def iota(shape, dim):
    return lax.broadcasted_iota(jnp.int32, shape, dim)


def split3(v):
    hi = v.astype(BF16).astype(F32)
    mid = (v - hi).astype(BF16).astype(F32)
    return hi, mid, v - hi - mid


def widen(table, first):
    lane = iota(table.shape, 1) // HEAD_DIM + first
    return jnp.take_along_axis(table, lane, axis=1, mode="promise_in_bounds")


def head_place():
    return lax.axis_index("y") * 2 + lax.axis_index("core")


def in_vmem(count):
    return [pl.BlockSpec(memory_space=pltpu.VMEM)] * count


def in_hbm(count):
    return [pl.BlockSpec(memory_space=pltpu.HBM)] * count


def in_smem(count):
    return [pl.BlockSpec(memory_space=pltpu.SMEM)] * count


def hbm(shape):
    return pltpu.HBM(shape, BF16)


def from_hbm(value):
    return pltpu.with_memory_space_constraint(value, pltpu.HBM)


def params(mib=16):
    return pltpu.CompilerParams(vmem_limit_bytes=mib * 1024 * 1024)


def start_kernel(
    len_ref, decay_hbm, step_hbm, conv_hbm, tab_ref, et_ref, tail_ref, decay_ref, step_ref, rows_ref, sems
):
    first_row = len_ref[0] - head_place() * TOK
    copies = [
        pltpu.make_async_copy(decay_hbm, decay_ref, sems.at[0]),
        pltpu.make_async_copy(step_hbm, step_ref, sems.at[1]),
    ]
    for k in range(ENDS):
        row = jnp.clip(first_row - ENDS + k, 0, TOK - 1)
        copies.append(pltpu.make_async_copy(conv_hbm.at[pl.ds(row, 1)], rows_ref.at[pl.ds(k, 1)], sems.at[2 + k]))
    for copy in copies:
        copy.start()
    for copy in copies:
        copy.wait()
    for k in range(ENDS):
        row = first_row - ENDS + k
        inside = jnp.where((row >= 0) & (row < TOK), 1.0, 0.0)
        tail_ref[k] = (rows_ref[k].astype(F32) * inside).astype(BF16)
    live = iota((TOK, LANE), 0) < first_row
    log_rate = jnp.where(live, decay_ref[...].astype(F32), 0.0)
    gain = jnp.where(live, step_ref[...].astype(F32), 0.0)
    upto = jnp.where(iota((TOK, TOK), 0) >= iota((TOK, TOK), 1), 1.0, 0.0).astype(BF16)
    running = jnp.dot(upto, log_rate.astype(BF16), preferred_element_type=F32)
    middle = running[TOK // 2 - 1 : TOK // 2]
    total = running[TOK - 1 : TOK]
    tab_ref[0] = jnp.exp(middle - running) * gain
    tab_ref[1] = jnp.exp(running - middle)
    tab_ref[2] = jnp.exp(running)
    et_ref[0:TOK] = jnp.exp(total - running) * gain
    et_ref[TOK:] = jnp.broadcast_to(jnp.exp(total), (8, LANE))


def start(seg_length, decay_log, step_size, conv_input):
    return pl.pallas_call(
        start_kernel,
        in_specs=in_smem(1) + in_hbm(3),
        out_specs=in_vmem(3),
        out_shape=[
            jax.ShapeDtypeStruct((3, TOK, LANE), F32),
            jax.ShapeDtypeStruct((TOK + 8, LANE), F32),
            jax.ShapeDtypeStruct((ENDS, GROUPS, GW), BF16),
        ],
        scratch_shapes=[
            pltpu.VMEM((TOK, LANE), BF16),
            pltpu.VMEM((TOK, LANE), BF16),
            pltpu.VMEM((ENDS, GROUPS, GW), BF16),
            pltpu.SemaphoreType.DMA((2 + ENDS,)),
        ],
        compiler_params=params(),
        name="start",
    )(seg_length, from_hbm(decay_log), from_hbm(step_size), from_hbm(conv_input))


def weight_row(m):
    return m // 4 * 8 + 4 + m % 4


def pack_kernel(first_ref, conv_hbm, tail_ref, weight_ref, bias_ref, out_hbm, last_ref, out_ref, sem, sems):
    load = pltpu.make_async_copy(conv_hbm.at[pl.ds(TOK - ENDS, ENDS)], last_ref, sem)
    load.start()
    place, core = lax.axis_index("y"), lax.axis_index("core")
    keep = (1 - first_ref[0]).astype(F32)
    row = iota((GROUPS, LANE), 0)
    low = row < 4
    load.wait()
    for tile in range(GW // LANE):
        at = slice(tile * LANE, (tile + 1) * LANE)
        rows = [weight_ref[k, :, at] for k in range(KERNEL)] + [bias_ref[:, at]]
        rows = rows + [v - v.astype(BF16).astype(F32) for v in rows]
        for k in range(ENDS):
            fill = jnp.zeros((GROUPS, LANE), F32)
            for m in range(4 * k, min(4 * k + 4, len(rows))):
                fill = jnp.where(row == 4 + m % 4, rows[m], fill)
            tail = tail_ref[k, :, at].astype(F32) * keep
            last = last_ref[k, :, at].astype(F32)
            for y in range(4):
                if y == 0:
                    value = tail
                else:
                    value = last * jnp.where((place == y - 1) & (core == 1), 1.0, 0.0)
                for c in range(2):
                    mine = value if c == 0 else pltpu.roll(value, 4, 0)
                    out_ref[y * 2 + c, k * 8 : k * 8 + 8, at] = jnp.where(low, mine, fill).astype(BF16)
    copies = [pltpu.make_async_copy(out_ref.at[pl.ds(4 * k, 4)], out_hbm.at[pl.ds(4 * k, 4)], sems.at[k]) for k in range(2)]
    for copy in copies:
        copy.start()
    for copy in copies:
        copy.wait()


def pack(seg_first, conv_input, tail, weight, bias):
    shape = (GROUPS, PACK, GW)
    return pl.pallas_call(
        pack_kernel,
        in_specs=in_smem(1) + in_hbm(1) + in_vmem(3),
        out_specs=in_hbm(1)[0],
        out_shape=hbm(shape),
        scratch_shapes=[
            pltpu.VMEM((ENDS, GROUPS, GW), BF16),
            pltpu.VMEM(shape, BF16),
            pltpu.SemaphoreType.DMA,
            pltpu.SemaphoreType.DMA((2,)),
        ],
        compiler_params=params(),
        name="pack",
    )(seg_first, from_hbm(conv_input), tail, weight, bias)


PART = 16


def convolve(window, taps):
    half = taps[KERNEL][None] + taps[0][None] * window[0:PART]
    for k in range(1, KERNEL):
        half = half + taps[k][None] * window[k : k + PART]
    half = half + half * jnp.tanh(half)
    return half.reshape(PART * GROUPS, LANE)


def load_lanes(refs, to_refs, sems):
    loads = []
    for i in range(GW // LW):
        at = pl.ds(i * LW, LW)
        loads.append(
            [pltpu.make_async_copy(ref.at[:, :, at], to.at[:, :, at], sems.at[k, i]) for k, (ref, to) in enumerate(zip(refs, to_refs))]
        )
        for load in loads[-1]:
            load.start()
    return loads


def states_kernel(
    core_ref, first_ref, own_hbm, sib_hbm, pack_ref, ets_ref, eto_ref, out_hbm, before_hbm, w_ref, halo_ref,
    own_ref, sib_ref, packed_ref, act_ref, pieces_ref, before_ref, sems, load_sems,
):
    core = core_ref[0]
    loads = load_lanes((own_hbm, sib_hbm), (own_ref, sib_ref), load_sems)
    low = iota((1, GROUPS, LANE), 1) < 4
    kept = low == (core == 0)
    swap = lambda v: pltpu.roll(v, 4, v.ndim - 2)
    for tile in range(GW // LANE):
        at = slice(tile * LANE, (tile + 1) * LANE)
        packed_ref[...] = pack_ref[:, :, at].astype(F32).reshape(GROUPS * PACK, LANE)
        before = [sum(packed_ref[d * PACK + k * 8 : d * PACK + k * 8 + 8] for d in range(GROUPS)) for k in range(ENDS)]
        before = jnp.stack([jnp.where(low[0], v, 0.0) for v in before])
        halo_ref[:, :, at] = before.astype(BF16)
        halves = [packed_ref[pl.ds(weight_row(m), GROUPS, stride=PACK), :] * 0.5 for m in range(2 * KERNEL + 2)]
        taps = [halves[k] + halves[k + KERNEL + 1] for k in range(KERNEL + 1)]
        for k, v in enumerate(taps):
            w_ref[k, :, at] = v
        taps = [jnp.where(kept[0], v, swap(v)) for v in taps]
        if tile % 2 == 0:
            for load in loads[tile // 2]:
                load.wait()

        def merged(rows, at=at):
            return jnp.where(kept, own_ref[rows, :, at].astype(F32), swap(sib_ref[rows, :, at].astype(F32)))

        def tokens(i, carry, tile=tile, taps=taps, merged=merged):
            window = merged(pl.ds(i * PART - (KERNEL - 1), PART + KERNEL - 1))
            act_ref[tile, pl.ds(pl.multiple_of(i * PART * GROUPS, PART * GROUPS), PART * GROUPS), :] = convolve(window, taps)
            return carry

        last = slice(TOK - (KERNEL - 1), TOK)
        between = jnp.where(core == 0, swap(own_ref[last, :, at].astype(F32)), sib_ref[last, :, at].astype(F32))
        window = jnp.concatenate([jnp.where(low, before, between), merged(slice(0, PART))], axis=0)
        act_ref[tile, 0 : PART * GROUPS, :] = convolve(window, taps)
        lax.fori_loop(1, TOK // PART, tokens, 0, unroll=True)

    own, sib = eto_ref[...], ets_ref[...]
    decay = [jnp.where(core == 0, own, sib), jnp.where(core == 0, sib, own)]
    d_last = decay[1][TOK:]
    d_chip = decay[0][TOK:] * d_last
    keep = jnp.where(lax.axis_index("y") == 0, 1 - first_ref[0], 1).astype(F32)
    row = iota((8, LANE), 0)
    copies = []
    for i in range(4):
        of_group = lambda half, tile: act_ref[tile, pl.ds(half * 4 + i, TOK, stride=GROUPS), :]
        b_t = [of_group(half, 8).T.astype(BF16) for half in range(2)]
        for j in range(4):
            states = []
            for half in range(2):
                carried = [
                    (of_group(half, tile) * widen(decay[half][:TOK], core * 64 + i * 16 + tile * 2)).astype(BF16)
                    for tile in (2 * j, 2 * j + 1)
                ]
                states.append(jnp.dot(b_t[half], jnp.concatenate(carried, axis=1), preferred_element_type=F32))
            for tile in range(2):
                lanes = slice(tile * LANE, (tile + 1) * LANE)
                head = core * 64 + i * 16 + (2 * j + tile) * 2
                hi, mid, bottom = split3(widen(d_chip, head))
                extra = jnp.where(row == 0, hi, jnp.where(row == 1, mid, jnp.where(row == 2, bottom, keep)))
                first = states[0][:, lanes]
                both = (first * widen(d_last, head)[0:1] + states[1][:, lanes]).astype(BF16)
                first = first.astype(BF16)
                for rows in range(2):
                    piece = (i * 8 + 2 * j + tile) * 2 + rows
                    before_ref[i, j, tile * 2 + rows] = first[rows * 64 : rows * 64 + 64]
                    pieces_ref[piece, 0:64] = both[rows * 64 : rows * 64 + 64]
                    pieces_ref[piece, 64:ROWS] = extra.astype(BF16)
        group = pl.ds(i * 16, 16)
        copies.append(pltpu.make_async_copy(pieces_ref.at[group], out_hbm.at[group], sems.at[0, i]))
        copies.append(pltpu.make_async_copy(before_ref.at[i], before_hbm.at[i], sems.at[1, i]))
        copies[-2].start()
        copies[-1].start()
    for copy in copies:
        copy.wait()


def chip_states(core, seg_first, own, sib, packs, et_sib, et_own):
    pieces = (CHUNKS, ROWS, LANE)
    before = (4, 4, 4, 64, LANE)
    return pl.pallas_call(
        states_kernel,
        in_specs=in_smem(2) + in_hbm(2) + in_vmem(3),
        out_specs=in_hbm(2) + in_vmem(2),
        out_shape=[
            hbm(pieces),
            hbm(before),
            jax.ShapeDtypeStruct((KERNEL + 1, GROUPS, GW), F32),
            jax.ShapeDtypeStruct((ENDS, GROUPS, GW), BF16),
        ],
        scratch_shapes=[
            pltpu.VMEM((TOK, GROUPS, GW), BF16),
            pltpu.VMEM((TOK, GROUPS, GW), BF16),
            pltpu.VMEM((GROUPS * PACK, LANE), F32),
            pltpu.VMEM((GW // LANE, TOK * GROUPS, LANE), F32),
            pltpu.VMEM(pieces, BF16),
            pltpu.VMEM(before, BF16),
            pltpu.SemaphoreType.DMA((2, 4)),
            pltpu.SemaphoreType.DMA((2, GW // LW)),
        ],
        compiler_params=params(20),
        name="chip_states",
    )(core, seg_first, from_hbm(own), from_hbm(sib), packs, et_sib, et_own)


def act_kernel(
    core_ref, conv_hbm, sib_hbm, own_halo_ref, sib_halo_ref, w_ref, x_hbm, bc_hbm,
    conv_ref, last_ref, act_ref, x_ref, bc_ref, sems, load_sems,
):
    core = core_ref[0]
    last = pltpu.make_async_copy(sib_hbm.at[pl.ds(TOK - ENDS, ENDS)], last_ref, load_sems.at[1, 0])
    last.start()
    loads = load_lanes((conv_hbm,), (conv_ref,), load_sems)
    last.wait()
    low = iota((1, GROUPS, LANE), 1) < 4
    for tile in range(GW // LANE):
        at = slice(tile * LANE, (tile + 1) * LANE)
        taps = [w_ref[k, :, at] for k in range(KERNEL + 1)]
        if tile % 2 == 0:
            loads[tile // 2][0].wait()

        def tokens(i, carry, at=at, tile=tile, taps=taps):
            window = conv_ref[pl.ds(i * PART - (KERNEL - 1), PART + KERNEL - 1), :, at].astype(F32)
            act_ref[tile, pl.ds(pl.multiple_of(i * PART * GROUPS, PART * GROUPS), PART * GROUPS), :] = convolve(window, taps)
            return carry

        halo = pltpu.roll(sib_halo_ref[:, :, at].astype(F32), 4, 1)
        halo = jnp.where(low, own_halo_ref[:, :, at].astype(F32), halo)
        halo = jnp.where(core == 0, halo, last_ref[:, :, at].astype(F32))
        window = jnp.concatenate([halo, conv_ref[0:PART, :, at].astype(F32)], axis=0)
        act_ref[tile, 0 : PART * GROUPS, :] = convolve(window, taps)
        lax.fori_loop(1, TOK // PART, tokens, 0, unroll=True)
    copies = []
    for g in range(GROUPS):
        for tile in range(GW // LANE):
            values = act_ref[tile, pl.ds(g, TOK, stride=GROUPS), :].astype(BF16)
            if tile < XW // LANE:
                x_ref[g, :, tile * LANE : (tile + 1) * LANE] = values
            else:
                bc_ref[g, :, tile * LANE - XW : (tile + 1) * LANE - XW] = values
        copies.append(pltpu.make_async_copy(x_ref.at[g], x_hbm.at[g], sems.at[0, g]))
        copies.append(pltpu.make_async_copy(bc_ref.at[g], bc_hbm.at[g], sems.at[1, g]))
        copies[-2].start()
        copies[-1].start()
    for copy in copies:
        copy.wait()


def activate(core, conv_input, sib, own_halo, sib_halo, weights):
    x, bc = (GROUPS, TOK, XW), (GROUPS, TOK, LW)
    return pl.pallas_call(
        act_kernel,
        in_specs=in_smem(1) + in_hbm(2) + in_vmem(3),
        out_specs=in_hbm(2),
        out_shape=[hbm(x), hbm(bc)],
        scratch_shapes=[
            pltpu.VMEM((TOK, GROUPS, GW), BF16),
            pltpu.VMEM((ENDS, GROUPS, GW), BF16),
            pltpu.VMEM((GW // LANE, TOK * GROUPS, LANE), F32),
            pltpu.VMEM(x, BF16),
            pltpu.VMEM(bc, BF16),
            pltpu.SemaphoreType.DMA((2, GROUPS)),
            pltpu.SemaphoreType.DMA((2, GW // LW)),
        ],
        compiler_params=params(18),
        cost_estimate=pl.CostEstimate(flops=20_000_000, bytes_accessed=8_000_000, transcendentals=1_400_000),
        name="activate",
    )(core, from_hbm(conv_input), from_hbm(sib), own_halo, sib_halo, weights)


def scan_kernel(chips, in_ref, out_hbm, out_ref, sems):
    each = CHUNKS // chips
    parts = 4
    size = CHUNKS // parts
    states = [jnp.zeros((64, LANE), F32) for _ in range(each)]
    stores = []
    for k in range(parts):
        for at in range(k * size, (k + 1) * size):
            i = at % each
            extra = in_ref[at, 64:ROWS].astype(F32)
            state = extra[3:4] * states[i]
            out_ref[at] = state.astype(BF16)
            states[i] = (extra[0:1] + extra[1:2] + extra[2:3]) * state + in_ref[at, 0:64].astype(F32)
        span = pl.ds(k * size, size)
        stores.append(pltpu.make_async_copy(out_ref.at[span], out_hbm.at[span], sems.at[k]))
        stores[-1].start()
    for store in stores:
        store.wait()


def scan(chips, pieces):
    return pl.pallas_call(
        functools.partial(scan_kernel, chips),
        in_specs=in_vmem(1),
        out_specs=in_hbm(1)[0],
        out_shape=hbm((CHUNKS, 64, LANE)),
        scratch_shapes=[pltpu.VMEM((CHUNKS, 64, LANE), BF16), pltpu.SemaphoreType.DMA((4,))],
        compiler_params=params(),
        name="scan",
    )(pieces)


def local_kernel(other, core_ref, len_ref, x_ref, bc_ref, tab_ref, before_ref, dts_ref, gate_ref, skip_ref, p_ref, q_ref):
    core = core_ref[0]
    group = ((core + other) % 2) * 4 + pl.program_id(0)
    inner, after, since = (tab_ref[k] for k in range(3))
    d_before = jnp.where(core == 1, dts_ref[TOK:], 1.0)
    spread = lambda table, j: jnp.concatenate([widen(table, group * 16 + j * 4 + 2 * k) for k in range(2)], axis=1)
    b = bc_ref[0, :, :LANE]
    c = bc_ref[0, :, LANE:]
    scores = lax.dot_general(c, b, (((1,), (1,)), ((), ())), preferred_element_type=F32)
    causal = iota((TOK, TOK), 0) >= iota((TOK, TOK), 1)
    scores = jnp.where(causal, scores, 0.0).astype(BF16)
    live = iota((TOK, LW), 0) < len_ref[0] - head_place() * TOK
    for j in range(4):
        at = slice(j * LW, (j + 1) * LW)
        x = x_ref[0, :, at].astype(F32)
        scaled = (x * spread(inner, j)).astype(BF16)
        y = spread(after, j) * jnp.dot(scores, scaled, preferred_element_type=F32)
        before = jnp.concatenate(
            [jnp.concatenate([before_ref[0, j, tile * 2], before_ref[0, j, tile * 2 + 1]], axis=0) for tile in range(2)],
            axis=1,
        )
        grown = spread(since, j)
        y = y + grown * (core.astype(F32) * jnp.dot(c, before, preferred_element_type=F32))
        y = y + skip_ref[:, at] * x
        half = gate_ref[:, at].astype(F32) * 0.5
        silu = half + half * jnp.tanh(half)
        p_ref[0, :, at] = jnp.where(live, y * silu, 0.0).astype(BF16)
        q_ref[0, :, at] = jnp.where(live, grown * spread(d_before, j)[0:1] * silu, 0.0).astype(BF16)


def local(other, core, seg_length, x, bc, tables, before, d_sib, gate_input, skip):
    group = lambda i, s: ((s[0] + other) % 2) * 4 + i
    out = hbm((4, TOK, XW))
    out_spec = pl.BlockSpec((1, TOK, XW), lambda i, s: (i, 0, 0))
    return pl.pallas_call(
        functools.partial(local_kernel, other),
        grid_spec=pltpu.PrefetchScalarGridSpec(
            num_scalar_prefetch=1,
            grid=(4,),
            in_specs=[
                pl.BlockSpec(memory_space=pltpu.SMEM),
                pl.BlockSpec((1, TOK, XW), lambda i, s: (group(i, s), 0, 0)),
                pl.BlockSpec((1, TOK, LW), lambda i, s: (group(i, s), 0, 0)),
                pl.BlockSpec((3, TOK, LANE), lambda i, s: (0, 0, 0)),
                pl.BlockSpec((1, 4, 4, 64, LANE), lambda i, s: (i, 0, 0, 0, 0)),
                pl.BlockSpec((TOK + 8, LANE), lambda i, s: (0, 0)),
                pl.BlockSpec((TOK, XW), lambda i, s: (0, group(i, s))),
                pl.BlockSpec((1, XW), lambda i, s: (0, group(i, s))),
            ],
            out_specs=[out_spec, out_spec],
        ),
        out_shape=[out, out],
        compiler_params=params(),
        cost_estimate=pl.CostEstimate(flops=400_000_000, bytes_accessed=8_000_000, transcendentals=600_000),
        name="local",
    )(core, seg_length, x, bc, tables, before, d_sib, gate_input, skip)


def finish_kernel(other, core_ref, p_ref, q_ref, bc_ref, state_ref, gain_ref, *rest):
    first = ((core_ref[0] + other) % 2) * 4
    if other:
        _, out_ref, rows_ref, sems = rest
    else:
        out_ref, rows_ref, sems, p_to, q_to, state_to, load_sems = rest
        loads = []
        for i in range(4):
            group = pl.ds(i * 16, 16)
            loads.append(pltpu.make_async_copy(state_ref.at[group], state_to.at[group], load_sems.at[0, i]))
            loads.append(pltpu.make_async_copy(p_ref.at[i], p_to.at[i], load_sems.at[1, i]))
            loads.append(pltpu.make_async_copy(q_ref.at[i], q_to.at[i], load_sems.at[2, i]))
        for load in loads:
            load.start()
        p_ref, q_ref, state_ref = p_to, q_to, state_to
    copies = []
    for i in range(4):
        if not other and i % 2 == 0:
            for load in loads[3 * i : 3 * i + 6]:
                load.wait()
        c = bc_ref[first + i, :, LANE:]
        gated = []
        for tile in range(0, 8, 2):
            state = jnp.concatenate(
                [
                    jnp.concatenate([state_ref[i * 16 + (tile + k) * 2], state_ref[i * 16 + (tile + k) * 2 + 1]], axis=0)
                    for k in range(2)
                ],
                axis=1,
            )
            at = slice(tile * LANE, (tile + 2) * LANE)
            read = jnp.dot(c, state, preferred_element_type=F32)
            gated.append(p_ref[i, :, at].astype(F32) + read * q_ref[i, :, at].astype(F32))
        total = sum(jnp.sum(v * v, axis=1, keepdims=True) for v in gated)
        scale = lax.rsqrt(total / XW + EPSILON)
        for j, v in enumerate(gated):
            at = slice(j * LW, (j + 1) * LW)
            rows_ref[i, :, at] = (v * scale * gain_ref[first + i, :, at]).astype(BF16)
        to = out_ref.at[:, pl.ds(pl.multiple_of((first + i) * XW, XW), XW)]
        copies.append(pltpu.make_async_copy(rows_ref.at[i], to, sems.at[i]))
        copies[-1].start()
    for copy in copies:
        copy.wait()


def finish(other, core, p, q, bc, states, gain, out=None):
    if other:
        operands = [core, p, q, bc, states, gain, out]
        in_specs = in_smem(1) + in_vmem(5) + [pl.BlockSpec(memory_space=pl.ANY)]
        loaded = []
    else:
        operands = [core, from_hbm(p), from_hbm(q), bc, from_hbm(states), gain]
        in_specs = in_smem(1) + in_hbm(2) + in_vmem(1) + in_hbm(1) + in_vmem(1)
        loaded = [
            pltpu.VMEM((4, TOK, XW), BF16),
            pltpu.VMEM((4, TOK, XW), BF16),
            pltpu.VMEM((CHUNKS, 64, LANE), BF16),
            pltpu.SemaphoreType.DMA((3, 4)),
        ]
    return pl.pallas_call(
        functools.partial(finish_kernel, other),
        in_specs=in_specs,
        out_specs=pl.BlockSpec(memory_space=pl.ANY),
        scratch_shapes=[pltpu.VMEM((4, TOK, XW), BF16), pltpu.SemaphoreType.DMA((4,))] + loaded,
        out_shape=jax.ShapeDtypeStruct((TOK, GROUPS * XW), BF16),
        input_output_aliases={6: 0} if other else {},
        compiler_params=params(),
        cost_estimate=pl.CostEstimate(flops=200_000_000, bytes_accessed=4_000_000, transcendentals=1000),
        name="finish",
    )(*operands)


def body(
    conv_input,
    gate_input,
    step_size,
    decay_log,
    conv_weight,
    conv_bias,
    skip_gain,
    norm_gain,
    seg_length,
    seg_first,
):
    segments = lax.axis_size("seq")
    in_segment = lax.axis_size("y") * lax.axis_size("core")
    chips = segments * in_segment // 2
    core = lax.axis_index("core").astype(jnp.int32).reshape(1)
    swap = [(0, 1), (1, 0)]

    sib = lax.ppermute(conv_input, "core", swap)
    tables, et_own, tail = start(seg_length, decay_log, step_size, conv_input)
    tail = lax.ppermute(tail, "seq", [(k, (k + 1) % segments) for k in range(segments)])
    et_sib = lax.ppermute(et_own, "core", swap)
    packs = pack(seg_first, conv_input, tail, conv_weight, conv_bias)
    packs = lax.all_to_all(packs, ("y", "core"), 0, 0, tiled=True)

    pieces, before_own, weights, halo = chip_states(core, seg_first, conv_input, sib, packs, et_sib, et_own)
    pieces = lax.all_to_all(pieces, CHIPS, 0, 0, tiled=True)
    before_oth = lax.ppermute(before_own, "core", swap[:1])
    halo_sib = lax.ppermute(halo, "core", swap)
    x, bc = activate(core, conv_input, sib, halo, halo_sib, weights)

    skip = jnp.repeat(skip_gain, HEAD_DIM)[None]
    pieces, x, bc = lax.optimization_barrier((pieces, x, bc))
    p_own, q_own = local(0, core, seg_length, x, bc, tables, before_own, et_sib, gate_input, skip)
    p_oth, q_oth = local(1, core, seg_length, x, bc, tables, before_oth, et_sib, gate_input, skip)
    states = lax.all_to_all(scan(chips, pieces), CHIPS, 0, 0, tiled=True)
    states, p_own, q_own, p_oth, q_oth = lax.optimization_barrier((states, p_own, q_own, p_oth, q_oth))
    states_oth = lax.ppermute(states, "core", swap)
    gain = norm_gain.reshape(GROUPS, 1, XW)
    out = finish(0, core, p_own, q_own, bc, states, gain)
    return finish(1, core, p_oth, q_oth, bc, states_oth, gain, out)


def solution(mesh):
    segments, in_segment = mesh.devices.shape
    fine = Mesh(mesh.devices.reshape(segments, in_segment // 2, 2), AXES)
    tokens = P(AXES, None)
    return jax.shard_map(
        body,
        mesh=fine,
        in_specs=(
            P(AXES, None, None),
            tokens,
            tokens,
            tokens,
            P(None, ("y", "core"), None),
            P(("y", "core"), None),
            P(),
            P(),
            P("seq"),
            P("seq"),
        ),
        out_specs=tokens,
        check_vma=False,
    )
```

time: 140 us -> 92.6 us (0.66)
  blocking collectives: 31.6 us -> 0 us
  Pallas kernels: 48 us -> 31.6 us
  waiting for transfers between devices: 17.3 us -> 29.1 us
  starting transfers between devices: 33.5 us -> 25.3 us
  local copies, waits for them, and re-layouts: 6.57 us -> 4.11 us
    all_to_all x1 -> x0, blocking collectives: 31.6 us -> none  [body(): pieces = lax.all_to_all(pieces, CHIPS, 0, 0, tiled=True)]
    all_to_all x1 -> x2, waiting for transfers between devices: 0.01 us -> 17.7 us  [the longest x1 9.85 us: body(): pieces = lax.all_to_all(pieces, CHIPS, 0, 0, tiled=True)]
    pallas_call x6 -> x7, Pallas kernels: 33.9 us -> 21.3 us  [the longest x1 7.04 us: chip_states(): pl.pallas_call(states_kernel, in_specs=in_smem(2) + in_hbm(2) + in_vmem(3...]
    ppermute x12 -> x5, starting transfers between devices: 18 us -> 5.68 us  [the longest x1 1.79 us: body(): lax.ppermute(tail, 'seq', [(k, (k + 1) % segments) for k in range(segment...]
    all_to_all x1, waiting for transfers between devices: 14.9 us -> 4.06 us  [body(): states = lax.all_to_all(scan(chips, pieces), CHIPS, 0, 0, tiled=True)]
    ppermute x12 -> x5, waiting for transfers between devices: 2.39 us -> 7.28 us  [the longest x1 6.02 us: body(): lax.ppermute(tail, 'seq', [(k, (k + 1) % segments) for k in range(segment...]
    pallas_call x2, Pallas kernels: 14.1 us -> 10.3 us  [local(): pl.pallas_call(functools.partial(local_kernel, other), grid_spec=pltpu.Pr...]
    all_to_all x1 -> x2, starting transfers between devices: 6.52 us -> 9.75 us  [the longest x1 5.08 us: body(): packs = lax.all_to_all(packs, ('y', 'core'), 0, 0, tiled=True)]
  transfers between devices with their start and end apart: 15 -> 9, of which waited for: 3 -> 5; matrix products, arithmetic and copies ran while one was open for 3% -> 0% of each run, Pallas kernels for 13% -> 25%
where the time goes in v2:
time: 92.6 us; the launch traced here: 91.8 us
  Pallas kernels  31.6 us (34%)
  waiting for transfers between devices  29.1 us (31%)
  starting transfers between devices  25.3 us (27%)
  local copies, waits for them, and re-layouts  4.11 us (4%)
  between operations  1.63 us (2%)
    pallas_call x2, Pallas kernels, local(): pl.pallas_call(functools.partial(local_kernel, other), grid_spec=pltpu.Pr...  10.3 us
    all_to_all x1, waiting for transfers between devices, body(): pieces = lax.all_to_all(pieces, CHIPS, 0, 0, tiled=True)  9.85 us
    all_to_all x1, waiting for transfers between devices, body(): packs = lax.all_to_all(packs, ('y', 'core'), 0, 0, tiled=True)  7.87 us
    pallas_call x1, Pallas kernels, chip_states(): pl.pallas_call(states_kernel, in_specs=in_smem(2) + in_hbm(2) + in_vmem(3...  7.04 us
    all_to_all x1, starting transfers between devices, body(): states = lax.all_to_all(scan(chips, pieces), CHIPS, 0, 0, tiled=True)  6.8 us
    ppermute x1, waiting for transfers between devices, body(): lax.ppermute(tail, 'seq', [(k, (k + 1) % segments) for k in range(segment...  6.02 us
    pallas_call x1, Pallas kernels, activate(): pl.pallas_call(act_kernel, in_specs=in_smem(1) + in_hbm(2) + in_vmem(3),...  5.42 us
    all_to_all x1, starting transfers between devices, body(): packs = lax.all_to_all(packs, ('y', 'core'), 0, 0, tiled=True)  5.08 us
  transfers between devices with their start and end apart: 9, of which 5 were waited for; matrix products, arithmetic and copies ran while one was open for 0% of the time, Pallas kernels for 25%

profile of v2, /device:TPU:1, one launch (start us, length us, event | category | flops | bytes accessed | tf_op | source)
XLA Modules:
  0.0 91.8 jit_solution(15833475618837101162)
XLA Ops:
  0.0 1.4 %collective-permute-start = (bf16[128,8,1280]{2,1,0:T(8,128)(2,1)}, bf16[128,8,1280]{2,1,0:T(8,128)(2,1)}, u32[]{:S(2)}, u32[]{:S(2)}) collective-permute-start(bf16[128,8,1280]{2,1,0:T(8,128)(2,1)} %conv_hbm.5), channel_id=1, source_target_pairs={{0,1},{1,0},{2,3},{3,2},{4,5},{5,4},{6,7},{7,6},{8,9},{9,8},{10,11... | collective-permute-start | bytes 7864328 | tf_op jit(solution)/shard_map/ppermute | solution.py:555
  2.1 1.1 %start.1 = (f32[3,128,128]{2,1,0:T(8,128)S(1)}, f32[136,128]{1,0:T(8,128)S(1)}, bf16[3,8,1280]{2,1,0:T(8,128)(2,1)S(1)}) custom-call(s32[1]{0:T(128)S(6)} %copy.13.len_ref, bf16[128,128]{1,0:T(8,128)(2,1)} %decay_hbm.1, bf16[128,128]{1,0:T(8,128)(2,1)} %step_hbm.1, bf16[128,8,1280]{2,1,0:T(8,128)(2,1)} %conv_hbm.5), custom_call_target="tpu_custom_call" | custom-call | tf_op jit(solution)/shard_map/start/pallas_call | solution.py:106
  3.2 1.8 %collective-permute-start.1 = (bf16[3,8,1280]{2,1,0:T(8,128)(2,1)S(1)}, bf16[3,8,1280]{2,1,0:T(8,128)(2,1)S(1)}, u32[]{:S(2)}, u32[]{:S(2)}) collective-permute-start(bf16[3,8,1280]{2,1,0:T(8,128)(2,1)S(1)} %get-tuple-element.26), channel_id=1, source_target_pairs={{0,8},{8,16},{16,24},{24,32},{32,40},{40,48},{48,56},{56,64},{64,7... | collective-permute-start | bytes 184328 | tf_op jit(solution)/shard_map/ppermute | solution.py:557
  5.6 6.0 %collective-permute-done.1.tail_ref = bf16[3,8,1280]{2,1,0:T(8,128)(2,1)S(1)} collective-permute-done((bf16[3,8,1280]{2,1,0:T(8,128)(2,1)S(1)}, bf16[3,8,1280]{2,1,0:T(8,128)(2,1)S(1)}, u32[]{:S(2)}, u32[]{:S(2)}) %collective-permute-start.1) | collective-permute-done | bytes 61472 | tf_op jit(solution)/shard_map/ppermute | solution.py:557
  11.6 1.8 %pack.1 = bf16[8,24,1280]{2,1,0:T(8,128)(2,1)} custom-call(s32[1]{0:T(128)S(6)} %copy.14.first_ref, bf16[128,8,1280]{2,1,0:T(8,128)(2,1)} %conv_hbm.5, bf16[3,8,1280]{2,1,0:T(8,128)(2,1)S(1)} %collective-permute-done.1.tail_ref, f32[4,1,1280]{2,1,0:T(1,128)S(1)} %copy-done.9, f32[1,1280]{1,0:T(1,128)S(1)} %copy-done.10), custom_call_target="tpu_custom_call" | custom-call | tf_op jit(solution)/shard_map/pack/pallas_call | solution.py:165
  13.4 5.1 %all-to-all-start = ((bf16[8,24,1280]{2,1,0:T(8,128)(2,1)}), bf16[8,24,1280]{2,1,0:T(8,128)(2,1)S(1)}, u32[]{:S(2)}, u32[]{:S(2)}) async-start(bf16[8,24,1280]{2,1,0:T(8,128)(2,1)} %pack.1), calls=%async_computation | async-start | bytes 983040 | tf_op jit(solution)/shard_map/all_to_all | solution.py:560
  18.5 1.3 %collective-permute-done.2.ets_ref.dts_ref = f32[136,128]{1,0:T(8,128)S(1)} collective-permute-done((f32[136,128]{1,0:T(8,128)S(1)}, f32[136,128]{1,0:T(8,128)S(1)}, u32[]{:S(2)}, u32[]{:S(2)}) %collective-permute-start.2) | collective-permute-done | bytes 69664 | tf_op jit(solution)/shard_map/ppermute | solution.py:558
  19.8 7.9 %all-to-all-done.pack_ref = bf16[8,24,1280]{2,1,0:T(8,128)(2,1)S(1)} async-done(((bf16[8,24,1280]{2,1,0:T(8,128)(2,1)}), bf16[8,24,1280]{2,1,0:T(8,128)(2,1)S(1)}, u32[]{:S(2)}, u32[]{:S(2)}) %all-to-all-start) | async-done | bytes 491552 | tf_op jit(solution)/shard_map/all_to_all | solution.py:560
  27.6 7.0 %chip_states.1 = (bf16[64,72,128]{2,1,0:T(8,128)(2,1)}, bf16[4,4,4,64,128]{4,3,2,1,0:T(8,128)(2,1)}, f32[5,8,1280]{2,1,0:T(8,128)S(1)}, bf16[3,8,1280]{2,1,0:T(8,128)(2,1)S(1)}) custom-call(s32[1]{0:T(128)} %bitcast.core_ref, s32[1]{0:T(128)S(6)} %copy.14.first_ref, bf16[128,8,1280]{2,1,0:T(8,128)(2,1)} %conv_hbm.5, ...), custom_call_target="tpu_custom_call" | custom-call | tf_op jit(solution)/shard_map/chip_states/pallas_call | solution.py:285
  34.7 4.7 %all-to-all-start.1 = ((bf16[64,72,128]{2,1,0:T(8,128)(2,1)}), bf16[64,72,128]{2,1,0:T(8,128)(2,1)S(1)}, u32[]{:S(2)}, u32[]{:S(2)}) async-start(bf16[64,72,128]{2,1,0:T(8,128)(2,1)} %get-tuple-element.28), calls=%async_computation.1 | async-start | bytes 2359296 | tf_op jit(solution)/shard_map/all_to_all | solution.py:563
  39.4 1.2 %collective-permute-start.3 = (bf16[3,8,1280]{2,1,0:T(8,128)(2,1)S(1)}, bf16[3,8,1280]{2,1,0:T(8,128)(2,1)S(1)}, u32[]{:S(2)}, u32[]{:S(2)}) collective-permute-start(bf16[3,8,1280]{2,1,0:T(8,128)(2,1)S(1)} %get-tuple-element.29.own_halo_ref), channel_id=1, source_target_pairs={{0,1},{1,0},{2,3},{3,2},{4,5},{5,4},{6,7},{7,6},{8,9},{9,8},{10,11... | collective-permute-start | bytes 184328 | tf_op jit(solution)/shard_map/ppermute | solution.py:565
  40.5 1.3 %collective-permute-start.4 = (bf16[4,4,4,64,128]{4,3,2,1,0:T(8,128)(2,1)}, bf16[4,4,4,64,128]{4,3,2,1,0:T(8,128)(2,1)}, u32[]{:S(2)}, u32[]{:S(2)}) collective-permute-start(bf16[4,4,4,64,128]{4,3,2,1,0:T(8,128)(2,1)} %get-tuple-element.37.before_ref), channel_id=1, source_target_pairs={{0,1},{2,3},{4,5},{6,7},{8,9},{10,11},{12,13},{14,15},{16,17},{18,... | collective-permute-start | bytes 3145736 | tf_op jit(solution)/shard_map/ppermute | solution.py:564
  41.8 5.4 %activate.1 = (bf16[8,128,1024]{2,1,0:T(8,128)(2,1)}, bf16[8,128,256]{2,1,0:T(8,128)(2,1)}) custom-call(s32[1]{0:T(128)} %bitcast.core_ref, bf16[128,8,1280]{2,1,0:T(8,128)(2,1)} %conv_hbm.5, bf16[128,8,1280]{2,1,0:T(8,128)(2,1)} %collective-permute-done.sib_hbm, bf16[3,8,1280]{2,1,0:T(8,128)(2,1)S(1)} %get-tuple-element.29.own_halo_ref, ...), custom_call_target="tpu_custom_call" | custom-call | flops 20000000 | bytes 8000000 | tf_op jit(solution)/shard_map/activate/pallas_call | solution.py:355
  47.3 9.9 %all-to-all-done.1.in_ref = bf16[64,72,128]{2,1,0:T(8,128)(2,1)S(1)} async-done(((bf16[64,72,128]{2,1,0:T(8,128)(2,1)}), bf16[64,72,128]{2,1,0:T(8,128)(2,1)S(1)}, u32[]{:S(2)}, u32[]{:S(2)}) %all-to-all-start.1) | async-done | bytes 1179680 | tf_op jit(solution)/shard_map/all_to_all | solution.py:563
  58.2 1.3 %copy-done.5 = bf16[64,72,128]{2,1,0:T(8,128)(2,1)S(1)} copy-done((bf16[64,72,128]{2,1,0:T(8,128)(2,1)S(1)}, bf16[64,72,128]{2,1,0:T(8,128)(2,1)}, u32[]{:S(2)}) %copy-start.5) | copy-done | bytes 1179672
  59.4 1.1 %scan.1 = bf16[64,64,128]{2,1,0:T(8,128)(2,1)} custom-call(bf16[64,72,128]{2,1,0:T(8,128)(2,1)S(1)} %copy-done.5), custom_call_target="tpu_custom_call" | custom-call | tf_op jit(solution)/shard_map/scan/pallas_call | solution.py:396
  60.5 6.8 %all-to-all-start.2 = ((bf16[64,64,128]{2,1,0:T(8,128)(2,1)}), bf16[64,64,128]{2,1,0:T(8,128)(2,1)}, u32[]{:S(2)}, u32[]{:S(2)}) async-start(bf16[64,64,128]{2,1,0:T(8,128)(2,1)} %scan.1), calls=%async_computation.2 | async-start | bytes 2097152 | tf_op jit(solution)/shard_map/all_to_all | solution.py:572
  67.6 1.6 %copy-done.2 = bf16[8,128,1024]{2,1,0:T(8,128)(2,1)S(1)} copy-done((bf16[8,128,1024]{2,1,0:T(8,128)(2,1)S(1)}, bf16[8,128,1024]{2,1,0:T(8,128)(2,1)}, u32[]{:S(2)}) %copy-start.2) | copy-done | bytes 2097176
  69.2 5.2 %local.2 = (bf16[4,128,1024]{2,1,0:T(8,128)(2,1)}, bf16[4,128,1024]{2,1,0:T(8,128)(2,1)}) custom-call(s32[1]{0:T(128)} %bitcast.core_ref, s32[1]{0:T(128)S(6)} %copy.13.len_ref, bf16[8,128,1024]{2,1,0:T(8,128)(2,1)S(1)} %copy-done.2, bf16[8,128,256]{2,1,0:T(8,128)(2,1)S(1)} %copy-done, f32[3,128,128]{2,1,0:T(8,128)S(1)} %get-tuple-element.36.tab_ref, ...), custom_call_target="tpu_custom_call" | custom-call | flops 400000000 | bytes 8000000 | tf_op jit(solution)/shard_map/local/pallas_call | solution.py:441
  74.4 5.1 %local.3 = (bf16[4,128,1024]{2,1,0:T(8,128)(2,1)}, bf16[4,128,1024]{2,1,0:T(8,128)(2,1)}) custom-call(s32[1]{0:T(128)} %bitcast.core_ref, s32[1]{0:T(128)S(6)} %copy.13.len_ref, bf16[8,128,1024]{2,1,0:T(8,128)(2,1)S(1)} %copy-done.3, bf16[8,128,256]{2,1,0:T(8,128)(2,1)S(1)} %copy-done, f32[3,128,128]{2,1,0:T(8,128)S(1)} %get-tuple-element.36.tab_ref, ...), custom_call_target="tpu_custom_call" | custom-call | flops 400000000 | bytes 8000000 | tf_op jit(solution)/shard_map/local/pallas_call | solution.py:441
  79.5 4.1 %all-to-all-done.2.state_ref = bf16[64,64,128]{2,1,0:T(8,128)(2,1)} async-done(((bf16[64,64,128]{2,1,0:T(8,128)(2,1)}), bf16[64,64,128]{2,1,0:T(8,128)(2,1)}, u32[]{:S(2)}, u32[]{:S(2)}) %all-to-all-start.2) | async-done | bytes 1048608 | tf_op jit(solution)/shard_map/all_to_all | solution.py:572
  83.6 3.1 %collective-permute-start.5 = (bf16[64,64,128]{2,1,0:T(8,128)(2,1)}, bf16[64,64,128]{2,1,0:T(8,128)(2,1)S(1)}, u32[]{:S(2)}, u32[]{:S(2)}) collective-permute-start(bf16[64,64,128]{2,1,0:T(8,128)(2,1)} %all-to-all-done.2.state_ref), channel_id=1, source_target_pairs={{0,1},{1,0},{2,3},{3,2},{4,5},{5,4},{6,7},{7,6},{8,9},{9,8},{10,11... | collective-permute-start | bytes 3145736 | tf_op jit(solution)/shard_map/ppermute | solution.py:574
  86.7 3.3 %finish.2.rest_0_ = bf16[128,8192]{1,0:T(8,128)(2,1)} custom-call(s32[1]{0:T(128)} %bitcast.core_ref, bf16[4,128,1024]{2,1,0:T(8,128)(2,1)} %get-tuple-element.45.p_ref, bf16[4,128,1024]{2,1,0:T(8,128)(2,1)} %get-tuple-element.46.q_ref, bf16[8,128,256]{2,1,0:T(8,128)(2,1)S(1)} %copy-done, bf16[64,64,128]{2,1,0:T(8,128)(2,1)} %all-to-all-done.2.state_ref, ...), custom_call_target="tpu_custom_call" | custom-call | flops 200000000 | bytes 4000000 | tf_op jit(solution)/shard_map/finish/pallas_call | solution.py:524
  90.0 1.5 %finish.3 = bf16[128,8192]{1,0:T(8,128)(2,1)} custom-call(s32[1]{0:T(128)} %bitcast.core_ref, bf16[4,128,1024]{2,1,0:T(8,128)(2,1)S(1)} %copy-done.6, bf16[4,128,1024]{2,1,0:T(8,128)(2,1)S(1)} %copy-done.7, bf16[8,128,256]{2,1,0:T(8,128)(2,1)S(1)} %copy-done, ...), custom_call_target="tpu_custom_call", output_to_operand_aliasing={{}: (6, {})} | custom-call | flops 200000000 | bytes 4000000 | tf_op jit(solution)/shard_map/finish/pallas_call | solution.py:524
  (29 shorter events, 1.3 us)
Async XLA Ops:
  0.0 11.6 %copy-start.9 = (f32[4,1,1280]{2,1,0:T(1,128)S(1)}, f32[4,1,1280]{2,1,0:T(1,128)}, u32[]{:S(2)}) copy-start(f32[4,1,1280]{2,1,0:T(1,128)} %weight_ref.1) | copy-start | bytes 61444
  0.0 11.6 %copy-start.10 = (f32[1,1280]{1,0:T(1,128)S(1)}, f32[1,1280]{1,0:T(1,128)}, u32[]{:S(2)}) copy-start(f32[1,1280]{1,0:T(1,128)} %bias_ref.1) | copy-start | bytes 15364
  0.0 27.6 %collective-permute-start = (bf16[128,8,1280]{2,1,0:T(8,128)(2,1)}, bf16[128,8,1280]{2,1,0:T(8,128)(2,1)}, u32[]{:S(2)}, u32[]{:S(2)}) collective-permute-start(bf16[128,8,1280]{2,1,0:T(8,128)(2,1)} %conv_hbm.5), channel_id=1, source_target_pairs={{0,1},{1,0},{2,3},{3,2},{4,5},{5,4},{6,7},{7,6},{8,9},{9,8},{10,11... | collective-permute-start | bytes 7864328 | tf_op jit(solution)/shard_map/ppermute | solution.py:555
  3.2 8.5 %collective-permute-start.1 = (bf16[3,8,1280]{2,1,0:T(8,128)(2,1)S(1)}, bf16[3,8,1280]{2,1,0:T(8,128)(2,1)S(1)}, u32[]{:S(2)}, u32[]{:S(2)}) collective-permute-start(bf16[3,8,1280]{2,1,0:T(8,128)(2,1)S(1)} %get-tuple-element.26), channel_id=1, source_target_pairs={{0,8},{8,16},{16,24},{24,32},{32,40},{40,48},{48,56},{56,64},{64,7... | collective-permute-start | bytes 184328 | tf_op jit(solution)/shard_map/ppermute | solution.py:557
  13.4 14.2 %all-to-all-start = ((bf16[8,24,1280]{2,1,0:T(8,128)(2,1)}), bf16[8,24,1280]{2,1,0:T(8,128)(2,1)S(1)}, u32[]{:S(2)}, u32[]{:S(2)}) async-start(bf16[8,24,1280]{2,1,0:T(8,128)(2,1)} %pack.1), calls=%async_computation | async-start | bytes 983040 | tf_op jit(solution)/shard_map/all_to_all | solution.py:560
  18.5 1.3 %collective-permute-start.2 = (f32[136,128]{1,0:T(8,128)S(1)}, f32[136,128]{1,0:T(8,128)S(1)}, u32[]{:S(2)}, u32[]{:S(2)}) collective-permute-start(f32[136,128]{1,0:T(8,128)S(1)} %get-tuple-element.27.eto_ref), channel_id=1, source_target_pairs={{0,1},{1,0},{2,3},{3,2},{4,5},{5,4},{6,7},{7,6},{8,9},{9,8},{10,11... | collective-permute-start | bytes 208904 | tf_op jit(solution)/shard_map/ppermute | solution.py:558
  34.7 22.4 %all-to-all-start.1 = ((bf16[64,72,128]{2,1,0:T(8,128)(2,1)}), bf16[64,72,128]{2,1,0:T(8,128)(2,1)S(1)}, u32[]{:S(2)}, u32[]{:S(2)}) async-start(bf16[64,72,128]{2,1,0:T(8,128)(2,1)} %get-tuple-element.28), calls=%async_computation.1 | async-start | bytes 2359296 | tf_op jit(solution)/shard_map/all_to_all | solution.py:563
  39.4 2.5 %collective-permute-start.3 = (bf16[3,8,1280]{2,1,0:T(8,128)(2,1)S(1)}, bf16[3,8,1280]{2,1,0:T(8,128)(2,1)S(1)}, u32[]{:S(2)}, u32[]{:S(2)}) collective-permute-start(bf16[3,8,1280]{2,1,0:T(8,128)(2,1)S(1)} %get-tuple-element.29.own_halo_ref), channel_id=1, source_target_pairs={{0,1},{1,0},{2,3},{3,2},{4,5},{5,4},{6,7},{7,6},{8,9},{9,8},{10,11... | collective-permute-start | bytes 184328 | tf_op jit(solution)/shard_map/ppermute | solution.py:565
  40.5 33.9 %collective-permute-start.4 = (bf16[4,4,4,64,128]{4,3,2,1,0:T(8,128)(2,1)}, bf16[4,4,4,64,128]{4,3,2,1,0:T(8,128)(2,1)}, u32[]{:S(2)}, u32[]{:S(2)}) collective-permute-start(bf16[4,4,4,64,128]{4,3,2,1,0:T(8,128)(2,1)} %get-tuple-element.37.before_ref), channel_id=1, source_target_pairs={{0,1},{2,3},{4,5},{6,7},{8,9},{10,11},{12,13},{14,15},{16,17},{18,... | collective-permute-start | bytes 3145736 | tf_op jit(solution)/shard_map/ppermute | solution.py:564
  57.1 1.0 %copy-start.4 = (bf16[64,72,128]{2,1,0:T(8,128)(2,1)}, bf16[64,72,128]{2,1,0:T(8,128)(2,1)S(1)}, u32[]{:S(2)}) copy-start(bf16[64,72,128]{2,1,0:T(8,128)(2,1)S(1)} %all-to-all-done.1.in_ref) | copy-start | bytes 3538948
  58.2 1.3 %copy-start.5 = (bf16[64,72,128]{2,1,0:T(8,128)(2,1)S(1)}, bf16[64,72,128]{2,1,0:T(8,128)(2,1)}, u32[]{:S(2)}) copy-start(bf16[64,72,128]{2,1,0:T(8,128)(2,1)} %copy-done.4) | copy-start | bytes 3538948
  59.4 7.9 %copy-start.11 = (f32[128]{0:T(128)S(1)}, f32[128]{0:T(128)}, u32[]{:S(2)}) copy-start(f32[128]{0:T(128)} %param.16) | copy-start | bytes 1540
  59.4 8.1 %copy-start = (bf16[8,128,256]{2,1,0:T(8,128)(2,1)S(1)}, bf16[8,128,256]{2,1,0:T(8,128)(2,1)}, u32[]{:S(2)}) copy-start(bf16[8,128,256]{2,1,0:T(8,128)(2,1)} %get-tuple-element.35.bc_ref) | copy-start | bytes 1572868
  59.4 8.1 %copy-start.1 = (bf16[128,8192]{1,0:T(8,128)(2,1)S(1)}, bf16[128,8192]{1,0:T(8,128)(2,1)}, u32[]{:S(2)}) copy-start(bf16[128,8192]{1,0:T(8,128)(2,1)} %gate_ref.3) | copy-start | bytes 6291460
  60.5 23.0 %all-to-all-start.2 = ((bf16[64,64,128]{2,1,0:T(8,128)(2,1)}), bf16[64,64,128]{2,1,0:T(8,128)(2,1)}, u32[]{:S(2)}, u32[]{:S(2)}) async-start(bf16[64,64,128]{2,1,0:T(8,128)(2,1)} %scan.1), calls=%async_computation.2 | async-start | bytes 2097152 | tf_op jit(solution)/shard_map/all_to_all | solution.py:572
  67.6 1.6 %copy-start.2 = (bf16[8,128,1024]{2,1,0:T(8,128)(2,1)S(1)}, bf16[8,128,1024]{2,1,0:T(8,128)(2,1)}, u32[]{:S(2)}) copy-start(bf16[8,128,1024]{2,1,0:T(8,128)(2,1)} %get-tuple-element.34.x_ref) | copy-start | bytes 6291460
  69.2 5.2 %copy-start.3 = (bf16[8,128,1024]{2,1,0:T(8,128)(2,1)S(1)}, bf16[8,128,1024]{2,1,0:T(8,128)(2,1)}, u32[]{:S(2)}) copy-start(bf16[8,128,1024]{2,1,0:T(8,128)(2,1)} %get-tuple-element.34.x_ref) | copy-start | bytes 6291460
  74.4 12.3 %copy-start.8 = (f32[8192]{0:T(1024)S(1)}, f32[8192]{0:T(1024)}, u32[]{:S(2)}) copy-start(f32[8192]{0:T(1024)} %param.17) | copy-start | bytes 98308
  83.6 6.4 %collective-permute-start.5 = (bf16[64,64,128]{2,1,0:T(8,128)(2,1)}, bf16[64,64,128]{2,1,0:T(8,128)(2,1)S(1)}, u32[]{:S(2)}, u32[]{:S(2)}) collective-permute-start(bf16[64,64,128]{2,1,0:T(8,128)(2,1)} %all-to-all-done.2.state_ref), channel_id=1, source_target_pairs={{0,1},{1,0},{2,3},{3,2},{4,5},{5,4},{6,7},{7,6},{8,9},{9,8},{10,11... | collective-permute-start | bytes 3145736 | tf_op jit(solution)/shard_map/ppermute | solution.py:574
  86.7 3.3 %copy-start.6 = (bf16[4,128,1024]{2,1,0:T(8,128)(2,1)S(1)}, bf16[4,128,1024]{2,1,0:T(8,128)(2,1)}, u32[]{:S(2)}) copy-start(bf16[4,128,1024]{2,1,0:T(8,128)(2,1)} %get-tuple-element.42.p_ref) | copy-start | bytes 3145732
  86.7 3.3 %copy-start.7 = (bf16[4,128,1024]{2,1,0:T(8,128)(2,1)S(1)}, bf16[4,128,1024]{2,1,0:T(8,128)(2,1)}, u32[]{:S(2)}) copy-start(bf16[4,128,1024]{2,1,0:T(8,128)(2,1)} %get-tuple-element.43.q_ref) | copy-start | bytes 3145732

commit v3 on v2

--- a/solution.py
+++ b/solution.py
@@ -24,6 +24,7 @@
 CHIPS = ("seq", "y")
 F32 = jnp.float32
 BF16 = jnp.bfloat16
+DONE = jax.ShapeDtypeStruct((8, LANE), F32)
 
 
 def iota(shape, dim):
@@ -70,7 +71,7 @@
 
 
 def start_kernel(
-    len_ref, decay_hbm, step_hbm, conv_hbm, tab_ref, et_ref, tail_ref, decay_ref, step_ref, rows_ref, sems
+    len_ref, decay_hbm, step_hbm, conv_hbm, tab_ref, et_ref, ends_ref, decay_ref, step_ref, rows_ref, sems
 ):
     first_row = len_ref[0] - head_place() * TOK
     copies = [
@@ -80,6 +81,7 @@
     for k in range(ENDS):
         row = jnp.clip(first_row - ENDS + k, 0, TOK - 1)
         copies.append(pltpu.make_async_copy(conv_hbm.at[pl.ds(row, 1)], rows_ref.at[pl.ds(k, 1)], sems.at[2 + k]))
+    copies.append(pltpu.make_async_copy(conv_hbm.at[pl.ds(TOK - ENDS, ENDS)], rows_ref.at[pl.ds(ENDS, ENDS)], sems.at[2 + ENDS]))
     for copy in copies:
         copy.start()
     for copy in copies:
@@ -87,7 +89,8 @@
     for k in range(ENDS):
         row = first_row - ENDS + k
         inside = jnp.where((row >= 0) & (row < TOK), 1.0, 0.0)
-        tail_ref[k] = (rows_ref[k].astype(F32) * inside).astype(BF16)
+        ends_ref[k] = (rows_ref[k].astype(F32) * inside).astype(BF16)
+        ends_ref[ENDS + k] = rows_ref[ENDS + k]
     live = iota((TOK, LANE), 0) < first_row
     log_rate = jnp.where(live, decay_ref[...].astype(F32), 0.0)
     gain = jnp.where(live, step_ref[...].astype(F32), 0.0)
@@ -110,13 +113,13 @@
         out_shape=[
             jax.ShapeDtypeStruct((3, TOK, LANE), F32),
             jax.ShapeDtypeStruct((TOK + 8, LANE), F32),
-            jax.ShapeDtypeStruct((ENDS, GROUPS, GW), BF16),
+            jax.ShapeDtypeStruct((2 * ENDS, GROUPS, GW), BF16),
         ],
         scratch_shapes=[
             pltpu.VMEM((TOK, LANE), BF16),
             pltpu.VMEM((TOK, LANE), BF16),
-            pltpu.VMEM((ENDS, GROUPS, GW), BF16),
-            pltpu.SemaphoreType.DMA((2 + ENDS,)),
+            pltpu.VMEM((2 * ENDS, GROUPS, GW), BF16),
+            pltpu.SemaphoreType.DMA((3 + ENDS,)),
         ],
         compiler_params=params(),
         name="start",
@@ -124,17 +127,13 @@
 
 
 def weight_row(m):
-    return m // 4 * 8 + 4 + m % 4
-
-
-def pack_kernel(first_ref, conv_hbm, tail_ref, weight_ref, bias_ref, out_hbm, last_ref, out_ref, sem, sems):
-    load = pltpu.make_async_copy(conv_hbm.at[pl.ds(TOK - ENDS, ENDS)], last_ref, sem)
-    load.start()
+    return m // 4 * 8 + m % 4 * 2 + 1
+
+
+def pack_kernel(own_ref, sib_ref, weight_ref, bias_ref, on_ref, tail_ref):
     place, core = lax.axis_index("y"), lax.axis_index("core")
-    keep = (1 - first_ref[0]).astype(F32)
     row = iota((GROUPS, LANE), 0)
-    low = row < 4
-    load.wait()
+    even = row % 2 == 0
     for tile in range(GW // LANE):
         at = slice(tile * LANE, (tile + 1) * LANE)
         rows = [weight_ref[k, :, at] for k in range(KERNEL)] + [bias_ref[:, at]]
@@ -142,40 +141,25 @@
         for k in range(ENDS):
             fill = jnp.zeros((GROUPS, LANE), F32)
             for m in range(4 * k, min(4 * k + 4, len(rows))):
-                fill = jnp.where(row == 4 + m % 4, rows[m], fill)
-            tail = tail_ref[k, :, at].astype(F32) * keep
-            last = last_ref[k, :, at].astype(F32)
-            for y in range(4):
-                if y == 0:
-                    value = tail
-                else:
-                    value = last * jnp.where((place == y - 1) & (core == 1), 1.0, 0.0)
-                for c in range(2):
-                    mine = value if c == 0 else pltpu.roll(value, 4, 0)
-                    out_ref[y * 2 + c, k * 8 : k * 8 + 8, at] = jnp.where(low, mine, fill).astype(BF16)
-    copies = [pltpu.make_async_copy(out_ref.at[pl.ds(4 * k, 4)], out_hbm.at[pl.ds(4 * k, 4)], sems.at[k]) for k in range(2)]
-    for copy in copies:
-        copy.start()
-    for copy in copies:
-        copy.wait()
-
-
-def pack(seg_first, conv_input, tail, weight, bias):
-    shape = (GROUPS, PACK, GW)
+                fill = jnp.where(row == weight_row(m % 4), rows[m], fill)
+            tail = own_ref[k, :, at].astype(F32) + sib_ref[k, :, at].astype(F32)
+            last = jnp.where(core == 0, sib_ref[ENDS + k, :, at].astype(F32), own_ref[ENDS + k, :, at].astype(F32))
+            onward = jnp.where(place == lax.axis_size("y") - 1, tail, last)
+            for value, ref in ((onward, on_ref), (tail, tail_ref)):
+                value = jnp.where(core == 0, value, pltpu.roll(value, GROUPS - 1, 0))
+                ref[k * 8 : k * 8 + 8, at] = jnp.where(even, value, fill).astype(BF16)
+
+
+def pack(own, sib, weight, bias):
+    shape = jax.ShapeDtypeStruct((PACK, GW), BF16)
     return pl.pallas_call(
         pack_kernel,
-        in_specs=in_smem(1) + in_hbm(1) + in_vmem(3),
-        out_specs=in_hbm(1)[0],
-        out_shape=hbm(shape),
-        scratch_shapes=[
-            pltpu.VMEM((ENDS, GROUPS, GW), BF16),
-            pltpu.VMEM(shape, BF16),
-            pltpu.SemaphoreType.DMA,
-            pltpu.SemaphoreType.DMA((2,)),
-        ],
+        in_specs=in_vmem(4),
+        out_specs=in_vmem(2),
+        out_shape=[shape, shape],
         compiler_params=params(),
         name="pack",
-    )(seg_first, from_hbm(conv_input), tail, weight, bias)
+    )(own, sib, weight, bias)
 
 
 PART = 16
@@ -202,25 +186,30 @@
 
 
 def states_kernel(
-    core_ref, first_ref, own_hbm, sib_hbm, pack_ref, ets_ref, eto_ref, out_hbm, before_hbm, w_ref, halo_ref,
+    core_ref, first_ref, own_hbm, sib_hbm, p0, p1, p2, p3, p4, ets_ref, eto_ref, out_hbm, before_hbm, w_ref, halo_ref,
     own_ref, sib_ref, packed_ref, act_ref, pieces_ref, before_ref, sems, load_sems,
 ):
     core = core_ref[0]
+    place = lax.axis_index("y")
     loads = load_lanes((own_hbm, sib_hbm), (own_ref, sib_ref), load_sems)
-    low = iota((1, GROUPS, LANE), 1) < 4
-    kept = low == (core == 0)
-    swap = lambda v: pltpu.roll(v, 4, v.ndim - 2)
+    keep = jnp.where(place == 0, 1 - first_ref[0], 1).astype(F32)
+    low = iota((1, GROUPS, LANE), 1) % 2 == 0
+    kept = iota((1, GROUPS, LANE), 1) % 2 == core
+    swap = lambda v: pltpu.roll(v, 1 + 6 * core, v.ndim - 2)
     for tile in range(GW // LANE):
         at = slice(tile * LANE, (tile + 1) * LANE)
-        packed_ref[...] = pack_ref[:, :, at].astype(F32).reshape(GROUPS * PACK, LANE)
-        before = [sum(packed_ref[d * PACK + k * 8 : d * PACK + k * 8 + 8] for d in range(GROUPS)) for k in range(ENDS)]
-        before = jnp.stack([jnp.where(low[0], v, 0.0) for v in before])
-        halo_ref[:, :, at] = before.astype(BF16)
+        packs = [ref[:, at].astype(F32) for ref in (p0, p1, p2, p3)]
+        for k, pack in enumerate(packs):
+            source = lax.rem(place - k + 4, 4)
+            for double in range(2):
+                packed_ref[pl.ds(pl.multiple_of((source * 2 + double) * PACK, 8), PACK), :] = pack
         halves = [packed_ref[pl.ds(weight_row(m), GROUPS, stride=PACK), :] * 0.5 for m in range(2 * KERNEL + 2)]
         taps = [halves[k] + halves[k + KERNEL + 1] for k in range(KERNEL + 1)]
         for k, v in enumerate(taps):
             w_ref[k, :, at] = v
-        taps = [jnp.where(kept[0], v, swap(v)) for v in taps]
+        before = packs[1] + jnp.where(place == 0, packs[2] + packs[3] + p4[:, at].astype(F32), 0.0)
+        before = jnp.where(low, before.reshape(ENDS, GROUPS, LANE) * keep, 0.0)
+        halo_ref[:, :, at] = before.astype(BF16)
         if tile % 2 == 0:
             for load in loads[tile // 2]:
                 load.wait()
@@ -243,23 +232,22 @@
     decay = [jnp.where(core == 0, own, sib), jnp.where(core == 0, sib, own)]
     d_last = decay[1][TOK:]
     d_chip = decay[0][TOK:] * d_last
-    keep = jnp.where(lax.axis_index("y") == 0, 1 - first_ref[0], 1).astype(F32)
     row = iota((8, LANE), 0)
     copies = []
     for i in range(4):
-        of_group = lambda half, tile: act_ref[tile, pl.ds(half * 4 + i, TOK, stride=GROUPS), :]
+        of_group = lambda half, tile: act_ref[tile, pl.ds(2 * i + half, TOK, stride=GROUPS), :]
         b_t = [of_group(half, 8).T.astype(BF16) for half in range(2)]
         for j in range(4):
             states = []
             for half in range(2):
                 carried = [
-                    (of_group(half, tile) * widen(decay[half][:TOK], core * 64 + i * 16 + tile * 2)).astype(BF16)
+                    (of_group(half, tile) * widen(decay[half][:TOK], core * 16 + i * 32 + tile * 2)).astype(BF16)
                     for tile in (2 * j, 2 * j + 1)
                 ]
                 states.append(jnp.dot(b_t[half], jnp.concatenate(carried, axis=1), preferred_element_type=F32))
             for tile in range(2):
                 lanes = slice(tile * LANE, (tile + 1) * LANE)
-                head = core * 64 + i * 16 + (2 * j + tile) * 2
+                head = core * 16 + i * 32 + (2 * j + tile) * 2
                 hi, mid, bottom = split3(widen(d_chip, head))
                 extra = jnp.where(row == 0, hi, jnp.where(row == 1, mid, jnp.where(row == 2, bottom, keep)))
                 first = states[0][:, lanes]
@@ -284,7 +272,7 @@
     before = (4, 4, 4, 64, LANE)
     return pl.pallas_call(
         states_kernel,
-        in_specs=in_smem(2) + in_hbm(2) + in_vmem(3),
+        in_specs=in_smem(2) + in_hbm(2) + in_vmem(7),
         out_specs=in_hbm(2) + in_vmem(2),
         out_shape=[
             hbm(pieces),
@@ -304,22 +292,24 @@
         ],
         compiler_params=params(20),
         name="chip_states",
-    )(core, seg_first, from_hbm(own), from_hbm(sib), packs, et_sib, et_own)
+    )(core, seg_first, from_hbm(own), from_hbm(sib), *packs, et_sib, et_own)
 
 
 def act_kernel(
-    core_ref, conv_hbm, sib_hbm, own_halo_ref, sib_halo_ref, w_ref, x_hbm, bc_hbm,
+    core_ref, conv_hbm, sib_hbm, own_halo_ref, sib_halo_ref, own_w_ref, sib_w_ref, x_hbm, bc_hbm, done_ref,
     conv_ref, last_ref, act_ref, x_ref, bc_ref, sems, load_sems,
 ):
+    done_ref[...] = jnp.zeros_like(done_ref)
     core = core_ref[0]
     last = pltpu.make_async_copy(sib_hbm.at[pl.ds(TOK - ENDS, ENDS)], last_ref, load_sems.at[1, 0])
     last.start()
     loads = load_lanes((conv_hbm,), (conv_ref,), load_sems)
     last.wait()
-    low = iota((1, GROUPS, LANE), 1) < 4
+    low = iota((1, GROUPS, LANE), 1) % 2 == 0
+    kept = iota((GROUPS, LANE), 0) % 2 == core
     for tile in range(GW // LANE):
         at = slice(tile * LANE, (tile + 1) * LANE)
-        taps = [w_ref[k, :, at] for k in range(KERNEL + 1)]
+        taps = [jnp.where(kept, own_w_ref[k, :, at], sib_w_ref[k, :, at]) for k in range(KERNEL + 1)]
         if tile % 2 == 0:
             loads[tile // 2][0].wait()
 
@@ -328,7 +318,7 @@
             act_ref[tile, pl.ds(pl.multiple_of(i * PART * GROUPS, PART * GROUPS), PART * GROUPS), :] = convolve(window, taps)
             return carry
 
-        halo = pltpu.roll(sib_halo_ref[:, :, at].astype(F32), 4, 1)
+        halo = pltpu.roll(sib_halo_ref[:, :, at].astype(F32), 1, 1)
         halo = jnp.where(low, own_halo_ref[:, :, at].astype(F32), halo)
         halo = jnp.where(core == 0, halo, last_ref[:, :, at].astype(F32))
         window = jnp.concatenate([halo, conv_ref[0:PART, :, at].astype(F32)], axis=0)
@@ -350,13 +340,13 @@
         copy.wait()
 
 
-def activate(core, conv_input, sib, own_halo, sib_halo, weights):
+def activate(core, conv_input, sib, own_halo, sib_halo, own_weights, sib_weights):
     x, bc = (GROUPS, TOK, XW), (GROUPS, TOK, LW)
     return pl.pallas_call(
         act_kernel,
-        in_specs=in_smem(1) + in_hbm(2) + in_vmem(3),
-        out_specs=in_hbm(2),
-        out_shape=[hbm(x), hbm(bc)],
+        in_specs=in_smem(1) + in_hbm(2) + in_vmem(4),
+        out_specs=in_hbm(2) + in_vmem(1),
+        out_shape=[hbm(x), hbm(bc), DONE],
         scratch_shapes=[
             pltpu.VMEM((TOK, GROUPS, GW), BF16),
             pltpu.VMEM((ENDS, GROUPS, GW), BF16),
@@ -369,44 +359,52 @@
         compiler_params=params(18),
         cost_estimate=pl.CostEstimate(flops=20_000_000, bytes_accessed=8_000_000, transcendentals=1_400_000),
         name="activate",
-    )(core, from_hbm(conv_input), from_hbm(sib), own_halo, sib_halo, weights)
-
-
-def scan_kernel(chips, in_ref, out_hbm, out_ref, sems):
+    )(core, from_hbm(conv_input), from_hbm(sib), own_halo, sib_halo, own_weights, sib_weights)
+
+
+def scan_kernel(chips, in_hbm, done_ref, out_hbm, in_ref, out_ref, sems):
     each = CHUNKS // chips
     parts = 4
     size = CHUNKS // parts
+    spans = [pl.ds(k * size, size) for k in range(parts)]
+    loads = [pltpu.make_async_copy(in_hbm.at[at], in_ref.at[at], sems.at[0, k]) for k, at in enumerate(spans)]
+    stores = [pltpu.make_async_copy(out_ref.at[at], out_hbm.at[at], sems.at[1, k]) for k, at in enumerate(spans)]
+    for load in loads:
+        load.start()
     states = [jnp.zeros((64, LANE), F32) for _ in range(each)]
-    stores = []
     for k in range(parts):
+        loads[k].wait()
         for at in range(k * size, (k + 1) * size):
             i = at % each
             extra = in_ref[at, 64:ROWS].astype(F32)
             state = extra[3:4] * states[i]
             out_ref[at] = state.astype(BF16)
             states[i] = (extra[0:1] + extra[1:2] + extra[2:3]) * state + in_ref[at, 0:64].astype(F32)
-        span = pl.ds(k * size, size)
-        stores.append(pltpu.make_async_copy(out_ref.at[span], out_hbm.at[span], sems.at[k]))
-        stores[-1].start()
+        stores[k].start()
     for store in stores:
         store.wait()
 
 
-def scan(chips, pieces):
+def scan(chips, pieces, done):
     return pl.pallas_call(
         functools.partial(scan_kernel, chips),
-        in_specs=in_vmem(1),
+        in_specs=in_hbm(1) + [pl.BlockSpec(memory_space=pl.ANY)],
         out_specs=in_hbm(1)[0],
         out_shape=hbm((CHUNKS, 64, LANE)),
-        scratch_shapes=[pltpu.VMEM((CHUNKS, 64, LANE), BF16), pltpu.SemaphoreType.DMA((4,))],
+        scratch_shapes=[
+            pltpu.VMEM((CHUNKS, ROWS, LANE), BF16),
+            pltpu.VMEM((CHUNKS, 64, LANE), BF16),
+            pltpu.SemaphoreType.DMA((2, 4)),
+        ],
         compiler_params=params(),
         name="scan",
-    )(pieces)
-
-
-def local_kernel(other, core_ref, len_ref, x_ref, bc_ref, tab_ref, before_ref, dts_ref, gate_ref, skip_ref, p_ref, q_ref):
+    )(from_hbm(pieces), done)
+
+
+def local_kernel(other, core_ref, len_ref, x_ref, bc_ref, tab_ref, before_ref, dts_ref, gate_ref, skip_ref, p_ref, q_ref, done_ref):
     core = core_ref[0]
-    group = ((core + other) % 2) * 4 + pl.program_id(0)
+    done_ref[...] = jnp.zeros_like(done_ref)
+    group = (core + other) % 2 + 2 * pl.program_id(0)
     inner, after, since = (tab_ref[k] for k in range(3))
     d_before = jnp.where(core == 1, dts_ref[TOK:], 1.0)
     spread = lambda table, j: jnp.concatenate([widen(table, group * 16 + j * 4 + 2 * k) for k in range(2)], axis=1)
@@ -435,7 +433,7 @@
 
 
 def local(other, core, seg_length, x, bc, tables, before, d_sib, gate_input, skip):
-    group = lambda i, s: ((s[0] + other) % 2) * 4 + i
+    group = lambda i, s: (s[0] + other) % 2 + 2 * i
     out = hbm((4, TOK, XW))
     out_spec = pl.BlockSpec((1, TOK, XW), lambda i, s: (i, 0, 0))
     return pl.pallas_call(
@@ -453,9 +451,9 @@
                 pl.BlockSpec((TOK, XW), lambda i, s: (0, group(i, s))),
                 pl.BlockSpec((1, XW), lambda i, s: (0, group(i, s))),
             ],
-            out_specs=[out_spec, out_spec],
+            out_specs=[out_spec, out_spec, pl.BlockSpec((8, LANE), lambda i, s: (0, 0))],
         ),
-        out_shape=[out, out],
+        out_shape=[out, out, DONE],
         compiler_params=params(),
         cost_estimate=pl.CostEstimate(flops=400_000_000, bytes_accessed=8_000_000, transcendentals=600_000),
         name="local",
@@ -463,11 +461,11 @@
 
 
 def finish_kernel(other, core_ref, p_ref, q_ref, bc_ref, state_ref, gain_ref, *rest):
-    first = ((core_ref[0] + other) % 2) * 4
+    first = (core_ref[0] + other) % 2
     if other:
         _, out_ref, rows_ref, sems = rest
     else:
-        out_ref, rows_ref, sems, p_to, q_to, state_to, load_sems = rest
+        _, out_ref, rows_ref, sems, p_to, q_to, state_to, load_sems = rest
         loads = []
         for i in range(4):
             group = pl.ds(i * 16, 16)
@@ -482,7 +480,7 @@
         if not other and i % 2 == 0:
             for load in loads[3 * i : 3 * i + 6]:
                 load.wait()
-        c = bc_ref[first + i, :, LANE:]
+        c = bc_ref[first + 2 * i, :, LANE:]
         gated = []
         for tile in range(0, 8, 2):
             state = jnp.concatenate(
@@ -499,22 +497,22 @@
         scale = lax.rsqrt(total / XW + EPSILON)
         for j, v in enumerate(gated):
             at = slice(j * LW, (j + 1) * LW)
-            rows_ref[i, :, at] = (v * scale * gain_ref[first + i, :, at]).astype(BF16)
-        to = out_ref.at[:, pl.ds(pl.multiple_of((first + i) * XW, XW), XW)]
+            rows_ref[i, :, at] = (v * scale * gain_ref[first + 2 * i, :, at]).astype(BF16)
+        to = out_ref.at[:, pl.ds(pl.multiple_of((first + 2 * i) * XW, XW), XW)]
         copies.append(pltpu.make_async_copy(rows_ref.at[i], to, sems.at[i]))
         copies[-1].start()
     for copy in copies:
         copy.wait()
 
 
-def finish(other, core, p, q, bc, states, gain, out=None):
+def finish(other, core, p, q, bc, states, gain, out):
     if other:
         operands = [core, p, q, bc, states, gain, out]
         in_specs = in_smem(1) + in_vmem(5) + [pl.BlockSpec(memory_space=pl.ANY)]
         loaded = []
     else:
-        operands = [core, from_hbm(p), from_hbm(q), bc, from_hbm(states), gain]
-        in_specs = in_smem(1) + in_hbm(2) + in_vmem(1) + in_hbm(1) + in_vmem(1)
+        operands = [core, from_hbm(p), from_hbm(q), bc, from_hbm(states), gain, out]
+        in_specs = in_smem(1) + in_hbm(2) + in_vmem(1) + in_hbm(1) + in_vmem(1) + [pl.BlockSpec(memory_space=pl.ANY)]
         loaded = [
             pltpu.VMEM((4, TOK, XW), BF16),
             pltpu.VMEM((4, TOK, XW), BF16),
@@ -553,27 +551,31 @@
     swap = [(0, 1), (1, 0)]
 
     sib = lax.ppermute(conv_input, "core", swap)
-    tables, et_own, tail = start(seg_length, decay_log, step_size, conv_input)
-    tail = lax.ppermute(tail, "seq", [(k, (k + 1) % segments) for k in range(segments)])
+    tables, et_own, ends = start(seg_length, decay_log, step_size, conv_input)
+    onward, tail = pack(ends, lax.ppermute(ends, "core", swap), conv_weight, conv_bias)
+    packs = [
+        lax.ppermute(tail if k > 1 else onward, CHIPS, [(c, (c + k) % chips) for c in range(chips)]) for k in range(1, 5)
+    ]
     et_sib = lax.ppermute(et_own, "core", swap)
-    packs = pack(seg_first, conv_input, tail, conv_weight, conv_bias)
-    packs = lax.all_to_all(packs, ("y", "core"), 0, 0, tiled=True)
-
-    pieces, before_own, weights, halo = chip_states(core, seg_first, conv_input, sib, packs, et_sib, et_own)
+
+    pieces, before_own, weights, halo = chip_states(
+        core, seg_first, conv_input, sib, [tail] + packs, et_sib, et_own
+    )
     pieces = lax.all_to_all(pieces, CHIPS, 0, 0, tiled=True)
     before_oth = lax.ppermute(before_own, "core", swap[:1])
     halo_sib = lax.ppermute(halo, "core", swap)
-    x, bc = activate(core, conv_input, sib, halo, halo_sib, weights)
+    weights_sib = lax.ppermute(weights, "core", swap)
+    x, bc, done = activate(core, conv_input, sib, halo, halo_sib, weights, weights_sib)
 
     skip = jnp.repeat(skip_gain, HEAD_DIM)[None]
-    pieces, x, bc = lax.optimization_barrier((pieces, x, bc))
-    p_own, q_own = local(0, core, seg_length, x, bc, tables, before_own, et_sib, gate_input, skip)
-    p_oth, q_oth = local(1, core, seg_length, x, bc, tables, before_oth, et_sib, gate_input, skip)
-    states = lax.all_to_all(scan(chips, pieces), CHIPS, 0, 0, tiled=True)
-    states, p_own, q_own, p_oth, q_oth = lax.optimization_barrier((states, p_own, q_own, p_oth, q_oth))
+    p_own, q_own, done_own = local(0, core, seg_length, x, bc, tables, before_own, et_sib, gate_input, skip)
+    p_oth, q_oth, done_oth = local(1, core, seg_length, x, bc, tables, before_oth, et_sib, gate_input, skip)
+    pieces, done = lax.optimization_barrier((pieces, done))
+    states = lax.all_to_all(scan(chips, pieces, done), CHIPS, 0, 0, tiled=True)
+    states, done = lax.optimization_barrier((states, done_own + done_oth))
     states_oth = lax.ppermute(states, "core", swap)
     gain = norm_gain.reshape(GROUPS, 1, XW)
-    out = finish(0, core, p_own, q_own, bc, states, gain)
+    out = finish(0, core, p_own, q_own, bc, states, gain, done)
     return finish(1, core, p_oth, q_oth, bc, states_oth, gain, out)
 
 

time: 92.6 us -> 84.1 us (0.908)
  waiting for transfers between devices: 29.1 us -> 19.6 us
  starting transfers between devices: 25.3 us -> 28 us
  local copies, waits for them, and re-layouts: 4.11 us -> 2.84 us
    all_to_all x2 -> x1, waiting for transfers between devices: 11.9 us -> 2.87 us  [body(): states = lax.all_to_all(scan(chips, pieces, done), CHIPS, 0, 0, tiled=True)]
    ppermute x1 -> x6, starting transfers between devices: 1.79 us -> 10.1 us  [the longest x4 7.52 us: body(): lax.ppermute(tail if k > 1 else onward, CHIPS, [(c, (c + k) % chips) for...]
    all_to_all x2 -> x1, starting transfers between devices: 11.9 us -> 5.52 us  [body(): states = lax.all_to_all(scan(chips, pieces, done), CHIPS, 0, 0, tiled=True)]
    ppermute x1 -> x6, waiting for transfers between devices: 6.02 us -> 8.66 us  [the longest x4 6.44 us: body(): lax.ppermute(tail if k > 1 else onward, CHIPS, [(c, (c + k) % chips) for...]
    all_to_all x1, waiting for transfers between devices: 9.85 us -> 8.09 us  [body(): pieces = lax.all_to_all(pieces, CHIPS, 0, 0, tiled=True)]
    unnamed x24 -> x22, local copies, waits for them, and re-layouts: 3.93 us -> 2.66 us
    ppermute x1, waiting for transfers between devices: 1.26 us -> 0.01 us  [body(): et_sib = lax.ppermute(et_own, 'core', swap)]
    ppermute x1, starting transfers between devices: 3.1 us -> 4.24 us  [body(): states_oth = lax.ppermute(states, 'core', swap)]
  transfers between devices with their start and end apart: 9 -> 13, of which waited for: 5 -> 6; matrix products, arithmetic and copies ran while one was open for 0% -> 0% of each run, Pallas kernels for 25% -> 27%
where the time goes in v3:
time: 84.1 us; the launch traced here: 83.5 us
  Pallas kernels  31.4 us (37%)
  starting transfers between devices  28 us (33%)
  waiting for transfers between devices  19.6 us (23%)
  local copies, waits for them, and re-layouts  2.84 us (3%)
  between operations  1.64 us (2%)
    pallas_call x2, Pallas kernels, local(): pl.pallas_call(functools.partial(local_kernel, other), grid_spec=pltpu.Pr...  10.4 us
    all_to_all x1, waiting for transfers between devices, body(): pieces = lax.all_to_all(pieces, CHIPS, 0, 0, tiled=True)  8.09 us
    ppermute x4, starting transfers between devices, body(): lax.ppermute(tail if k > 1 else onward, CHIPS, [(c, (c + k) % chips) for...  7.52 us
    pallas_call x1, Pallas kernels, chip_states(): pl.pallas_call(states_kernel, in_specs=in_smem(2) + in_hbm(2) + in_vmem(7...  7.06 us
    ppermute x4, waiting for transfers between devices, body(): lax.ppermute(tail if k > 1 else onward, CHIPS, [(c, (c + k) % chips) for...  6.44 us
    all_to_all x1, starting transfers between devices, body(): states = lax.all_to_all(scan(chips, pieces, done), CHIPS, 0, 0, tiled=True)  5.52 us
    pallas_call x1, Pallas kernels, activate(): pl.pallas_call(act_kernel, in_specs=in_smem(1) + in_hbm(2) + in_vmem(4),...  5.44 us
    pallas_call x2, Pallas kernels, finish(): pl.pallas_call(functools.partial(finish_kernel, other), in_specs=in_specs...  4.87 us
  transfers between devices with their start and end apart: 13, of which 6 were waited for; matrix products, arithmetic and copies ran while one was open for 0% of the time, Pallas kernels for 27%

profile of v3, /device:TPU:1, one launch (start us, length us, event | category | flops | bytes accessed | tf_op | source)
XLA Modules:
  0.0 83.5 jit_solution(4232133364316962577)
XLA Ops:
  0.0 1.4 %collective-permute-start = (bf16[128,8,1280]{2,1,0:T(8,128)(2,1)}, bf16[128,8,1280]{2,1,0:T(8,128)(2,1)}, u32[]{:S(2)}, u32[]{:S(2)}) collective-permute-start(bf16[128,8,1280]{2,1,0:T(8,128)(2,1)} %conv_hbm.3), channel_id=1, source_target_pairs={{0,1},{1,0},{2,3},{3,2},{4,5},{5,4},{6,7},{7,6},{8,9},{9,8},{10,11... | collective-permute-start | bytes 7864328 | tf_op jit(solution)/shard_map/ppermute | solution.py:553
  2.1 1.2 %start.1 = (f32[3,128,128]{2,1,0:T(8,128)S(1)}, f32[136,128]{1,0:T(8,128)S(1)}, bf16[6,8,1280]{2,1,0:T(8,128)(2,1)S(1)}) custom-call(s32[1]{0:T(128)S(6)} %copy.13.len_ref, bf16[128,128]{1,0:T(8,128)(2,1)} %decay_hbm.1, bf16[128,128]{1,0:T(8,128)(2,1)} %step_hbm.1, bf16[128,8,1280]{2,1,0:T(8,128)(2,1)} %conv_hbm.3), custom_call_target="tpu_custom_call" | custom-call | tf_op jit(solution)/shard_map/start/pallas_call | solution.py:109
  3.9 2.2 %collective-permute-done.1.sib_ref = bf16[6,8,1280]{2,1,0:T(8,128)(2,1)S(1)} collective-permute-done((bf16[6,8,1280]{2,1,0:T(8,128)(2,1)S(1)}, bf16[6,8,1280]{2,1,0:T(8,128)(2,1)S(1)}, u32[]{:S(2)}, u32[]{:S(2)}) %collective-permute-start.1) | collective-permute-done | bytes 122912 | tf_op jit(solution)/shard_map/ppermute | solution.py:555
  6.3 1.4 %collective-permute-start.2 = (bf16[24,1280]{1,0:T(8,128)(2,1)S(1)}, bf16[24,1280]{1,0:T(8,128)(2,1)S(1)}, u32[]{:S(2)}, u32[]{:S(2)}) collective-permute-start(bf16[24,1280]{1,0:T(8,128)(2,1)S(1)} %get-tuple-element.29), channel_id=1, source_target_pairs={{0,2},{2,4},{4,6},{6,8},{8,10},{10,12},{12,14},{14,16},{16,18},{18... | collective-permute-start | bytes 184328 | tf_op jit(solution)/shard_map/ppermute | solution.py:557
  7.7 1.6 %collective-permute-start.5 = (bf16[24,1280]{1,0:T(8,128)(2,1)S(1)}, bf16[24,1280]{1,0:T(8,128)(2,1)S(1)}, u32[]{:S(2)}, u32[]{:S(2)}) collective-permute-start(bf16[24,1280]{1,0:T(8,128)(2,1)S(1)} %get-tuple-element.28.p0), channel_id=1, source_target_pairs={{0,8},{2,10},{4,12},{6,14},{8,16},{10,18},{12,20},{14,22},{16,24},... | collective-permute-start | bytes 184328 | tf_op jit(solution)/shard_map/ppermute | solution.py:557
  9.3 2.7 %collective-permute-start.4 = (bf16[24,1280]{1,0:T(8,128)(2,1)S(1)}, bf16[24,1280]{1,0:T(8,128)(2,1)S(1)}, u32[]{:S(2)}, u32[]{:S(2)}) collective-permute-start(bf16[24,1280]{1,0:T(8,128)(2,1)S(1)} %get-tuple-element.28.p0), channel_id=1, source_target_pairs={{0,6},{2,8},{4,10},{6,12},{8,14},{10,16},{12,18},{14,20},{16,22},{... | collective-permute-start | bytes 184328 | tf_op jit(solution)/shard_map/ppermute | solution.py:557
  12.1 1.7 %collective-permute-start.3 = (bf16[24,1280]{1,0:T(8,128)(2,1)S(1)}, bf16[24,1280]{1,0:T(8,128)(2,1)S(1)}, u32[]{:S(2)}, u32[]{:S(2)}) collective-permute-start(bf16[24,1280]{1,0:T(8,128)(2,1)S(1)} %get-tuple-element.28.p0), channel_id=1, source_target_pairs={{0,4},{2,6},{4,8},{6,10},{8,12},{10,14},{12,16},{14,18},{16,20},{1... | collective-permute-start | bytes 184328 | tf_op jit(solution)/shard_map/ppermute | solution.py:557
  14.4 2.7 %collective-permute-done.2.p1 = bf16[24,1280]{1,0:T(8,128)(2,1)S(1)} collective-permute-done((bf16[24,1280]{1,0:T(8,128)(2,1)S(1)}, bf16[24,1280]{1,0:T(8,128)(2,1)S(1)}, u32[]{:S(2)}, u32[]{:S(2)}) %collective-permute-start.2) | collective-permute-done | bytes 61472 | tf_op jit(solution)/shard_map/ppermute | solution.py:557
  18.0 2.9 %collective-permute-done.3.p2 = bf16[24,1280]{1,0:T(8,128)(2,1)S(1)} collective-permute-done((bf16[24,1280]{1,0:T(8,128)(2,1)S(1)}, bf16[24,1280]{1,0:T(8,128)(2,1)S(1)}, u32[]{:S(2)}, u32[]{:S(2)}) %collective-permute-start.3) | collective-permute-done | bytes 61472 | tf_op jit(solution)/shard_map/ppermute | solution.py:557
  20.9 7.1 %chip_states.1 = (bf16[64,72,128]{2,1,0:T(8,128)(2,1)}, bf16[4,4,4,64,128]{4,3,2,1,0:T(8,128)(2,1)}, f32[5,8,1280]{2,1,0:T(8,128)S(1)}, bf16[3,8,1280]{2,1,0:T(8,128)(2,1)S(1)}) custom-call(s32[1]{0:T(128)} %bitcast.core_ref, s32[1]{0:T(128)S(6)} %copy.14.first_ref, bf16[128,8,1280]{2,1,0:T(8,128)(2,1)} %conv_hbm.3, ...), custom_call_target="tpu_custom_call" | custom-call | tf_op jit(solution)/shard_map/chip_states/pallas_call | solution.py:273
  28.0 4.7 %all-to-all-start = ((bf16[64,72,128]{2,1,0:T(8,128)(2,1)}), bf16[64,72,128]{2,1,0:T(8,128)(2,1)S(1)}, u32[]{:S(2)}, u32[]{:S(2)}) async-start(bf16[64,72,128]{2,1,0:T(8,128)(2,1)} %get-tuple-element.39), calls=%async_computation | async-start | bytes 2359296 | tf_op jit(solution)/shard_map/all_to_all | solution.py:564
  32.6 2.4 %collective-permute-start.8 = (f32[5,8,1280]{2,1,0:T(8,128)S(1)}, f32[5,8,1280]{2,1,0:T(8,128)S(1)}, u32[]{:S(2)}, u32[]{:S(2)}) collective-permute-start(f32[5,8,1280]{2,1,0:T(8,128)S(1)} %get-tuple-element.32.own_w_ref), channel_id=1, source_target_pairs={{0,1},{1,0},{2,3},{3,2},{4,5},{5,4},{6,7},{7,6},{8,9},{9,8},{10,11... | collective-permute-start | bytes 614408 | tf_op jit(solution)/shard_map/ppermute | solution.py:567
  35.2 1.5 %collective-permute-start.9 = (bf16[4,4,4,64,128]{4,3,2,1,0:T(8,128)(2,1)}, bf16[4,4,4,64,128]{4,3,2,1,0:T(8,128)(2,1)}, u32[]{:S(2)}, u32[]{:S(2)}) collective-permute-start(bf16[4,4,4,64,128]{4,3,2,1,0:T(8,128)(2,1)} %get-tuple-element.36.before_ref), channel_id=1, source_target_pairs={{0,1},{2,3},{4,5},{6,7},{8,9},{10,11},{12,13},{14,15},{16,17},{18,... | collective-permute-start | bytes 3145736 | tf_op jit(solution)/shard_map/ppermute | solution.py:565
  36.7 5.4 %activate.1 = (bf16[8,128,1024]{2,1,0:T(8,128)(2,1)}, bf16[8,128,256]{2,1,0:T(8,128)(2,1)}, f32[8,128]{1,0:T(8,128)S(1)}) custom-call(s32[1]{0:T(128)} %bitcast.core_ref, bf16[128,8,1280]{2,1,0:T(8,128)(2,1)} %conv_hbm.3, bf16[128,8,1280]{2,1,0:T(8,128)(2,1)} %collective-permute-done.sib_hbm, bf16[3,8,1280]{2,1,0:T(8,128)(2,1)S(1)} %get-tuple-element.31.own_halo_ref, ...), custom_call_target="tpu_custom_call" | custom-call | flops 20000000 | bytes 8000000 | tf_op jit(solution)/shard_map/activate/pallas_call | solution.py:345
  42.1 8.1 %all-to-all-done.in_hbm = bf16[64,72,128]{2,1,0:T(8,128)(2,1)S(1)} async-done(((bf16[64,72,128]{2,1,0:T(8,128)(2,1)}), bf16[64,72,128]{2,1,0:T(8,128)(2,1)S(1)}, u32[]{:S(2)}, u32[]{:S(2)}) %all-to-all-start) | async-done | bytes 1179680 | tf_op jit(solution)/shard_map/all_to_all | solution.py:564
  51.2 2.3 %scan.1 = bf16[64,64,128]{2,1,0:T(8,128)(2,1)} custom-call(bf16[64,72,128]{2,1,0:T(8,128)(2,1)} %copy-done.9, f32[8,128]{1,0:T(8,128)S(1)} %get-tuple-element.42.done_ref), custom_call_target="tpu_custom_call" | custom-call | tf_op jit(solution)/shard_map/scan/pallas_call | solution.py:389
  53.5 5.5 %all-to-all-start.1 = ((bf16[64,64,128]{2,1,0:T(8,128)(2,1)}), bf16[64,64,128]{2,1,0:T(8,128)(2,1)}, u32[]{:S(2)}, u32[]{:S(2)}) async-start(bf16[64,64,128]{2,1,0:T(8,128)(2,1)} %scan.1), calls=%async_computation.1 | async-start | bytes 2097152 | tf_op jit(solution)/shard_map/all_to_all | solution.py:574
  59.3 1.6 %copy-done.2 = bf16[8,128,1024]{2,1,0:T(8,128)(2,1)S(1)} copy-done((bf16[8,128,1024]{2,1,0:T(8,128)(2,1)S(1)}, bf16[8,128,1024]{2,1,0:T(8,128)(2,1)}, u32[]{:S(2)}) %copy-start.2) | copy-done | bytes 2097176
  60.9 5.2 %local.3 = (bf16[4,128,1024]{2,1,0:T(8,128)(2,1)}, bf16[4,128,1024]{2,1,0:T(8,128)(2,1)}, f32[8,128]{1,0:T(8,128)S(1)}) custom-call(s32[1]{0:T(128)} %bitcast.core_ref, s32[1]{0:T(128)S(6)} %copy.13.len_ref, bf16[8,128,1024]{2,1,0:T(8,128)(2,1)S(1)} %copy-done.2, bf16[8,128,256]{2,1,0:T(8,128)(2,1)S(1)} %copy-done, ...), custom_call_target="tpu_custom_call" | custom-call | flops 400000000 | bytes 8000000 | tf_op jit(solution)/shard_map/local/pallas_call | solution.py:439
  66.1 5.2 %local.2 = (bf16[4,128,1024]{2,1,0:T(8,128)(2,1)}, bf16[4,128,1024]{2,1,0:T(8,128)(2,1)}, f32[8,128]{1,0:T(8,128)S(1)}) custom-call(s32[1]{0:T(128)} %bitcast.core_ref, s32[1]{0:T(128)S(6)} %copy.13.len_ref, bf16[8,128,1024]{2,1,0:T(8,128)(2,1)S(1)} %copy-done.3, bf16[8,128,256]{2,1,0:T(8,128)(2,1)S(1)} %copy-done, ...), custom_call_target="tpu_custom_call" | custom-call | flops 400000000 | bytes 8000000 | tf_op jit(solution)/shard_map/local/pallas_call | solution.py:439
  71.3 2.9 %all-to-all-done.1.state_ref = bf16[64,64,128]{2,1,0:T(8,128)(2,1)} async-done(((bf16[64,64,128]{2,1,0:T(8,128)(2,1)}), bf16[64,64,128]{2,1,0:T(8,128)(2,1)}, u32[]{:S(2)}, u32[]{:S(2)}) %all-to-all-start.1) | async-done | bytes 1048608 | tf_op jit(solution)/shard_map/all_to_all | solution.py:574
  74.1 4.2 %collective-permute-start.10 = (bf16[64,64,128]{2,1,0:T(8,128)(2,1)}, bf16[64,64,128]{2,1,0:T(8,128)(2,1)S(1)}, u32[]{:S(2)}, u32[]{:S(2)}) collective-permute-start(bf16[64,64,128]{2,1,0:T(8,128)(2,1)} %all-to-all-done.1.state_ref), channel_id=1, source_target_pairs={{0,1},{1,0},{2,3},{3,2},{4,5},{5,4},{6,7},{7,6},{8,9},{9,8},{10,11... | collective-permute-start | bytes 3145736 | tf_op jit(solution)/shard_map/ppermute | solution.py:576
  78.4 3.3 %finish.2.rest_0_ = bf16[128,8192]{1,0:T(8,128)(2,1)} custom-call(s32[1]{0:T(128)} %bitcast.core_ref, bf16[4,128,1024]{2,1,0:T(8,128)(2,1)} %get-tuple-element.46.p_ref, bf16[4,128,1024]{2,1,0:T(8,128)(2,1)} %get-tuple-element.47.q_ref, bf16[8,128,256]{2,1,0:T(8,128)(2,1)S(1)} %copy-done, bf16[64,64,128]{2,1,0:T(8,128)(2,1)} %all-to-all-done.1.state_ref, ...), custom_call_target="tpu_custom_call" | custom-call | flops 200000000 | bytes 4000000 | tf_op jit(solution)/shard_map/finish/pallas_call | solution.py:522
  81.7 1.6 %finish.3 = bf16[128,8192]{1,0:T(8,128)(2,1)} custom-call(s32[1]{0:T(128)} %bitcast.core_ref, bf16[4,128,1024]{2,1,0:T(8,128)(2,1)S(1)} %copy-done.4, bf16[4,128,1024]{2,1,0:T(8,128)(2,1)S(1)} %copy-done.5, bf16[8,128,256]{2,1,0:T(8,128)(2,1)S(1)} %copy-done, ...), custom_call_target="tpu_custom_call", output_to_operand_aliasing={{}: (6, {})} | custom-call | flops 200000000 | bytes 4000000 | tf_op jit(solution)/shard_map/finish/pallas_call | solution.py:522
  (36 shorter events, 2.9 us)
Async XLA Ops:
  0.0 6.1 %copy-start.8 = (f32[1,1280]{1,0:T(1,128)S(1)}, f32[1,1280]{1,0:T(1,128)}, u32[]{:S(2)}) copy-start(f32[1,1280]{1,0:T(1,128)} %bias_ref.1) | copy-start | bytes 15364
  0.0 6.1 %copy-start.7 = (f32[4,1,1280]{2,1,0:T(1,128)S(1)}, f32[4,1,1280]{2,1,0:T(1,128)}, u32[]{:S(2)}) copy-start(f32[4,1,1280]{2,1,0:T(1,128)} %weight_ref.1) | copy-start | bytes 61444
  0.0 20.9 %collective-permute-start = (bf16[128,8,1280]{2,1,0:T(8,128)(2,1)}, bf16[128,8,1280]{2,1,0:T(8,128)(2,1)}, u32[]{:S(2)}, u32[]{:S(2)}) collective-permute-start(bf16[128,8,1280]{2,1,0:T(8,128)(2,1)} %conv_hbm.3), channel_id=1, source_target_pairs={{0,1},{1,0},{2,3},{3,2},{4,5},{5,4},{6,7},{7,6},{8,9},{9,8},{10,11... | collective-permute-start | bytes 7864328 | tf_op jit(solution)/shard_map/ppermute | solution.py:553
  3.3 2.8 %collective-permute-start.1 = (bf16[6,8,1280]{2,1,0:T(8,128)(2,1)S(1)}, bf16[6,8,1280]{2,1,0:T(8,128)(2,1)S(1)}, u32[]{:S(2)}, u32[]{:S(2)}) collective-permute-start(bf16[6,8,1280]{2,1,0:T(8,128)(2,1)S(1)} %get-tuple-element.27.own_ref), channel_id=1, source_target_pairs={{0,1},{1,0},{2,3},{3,2},{4,5},{5,4},{6,7},{7,6},{8,9},{9,8},{10,11... | collective-permute-start | bytes 368648 | tf_op jit(solution)/shard_map/ppermute | solution.py:555
  3.4 8.6 %collective-permute-start.6 = (f32[136,128]{1,0:T(8,128)S(1)}, f32[136,128]{1,0:T(8,128)S(1)}, u32[]{:S(2)}, u32[]{:S(2)}) collective-permute-start(f32[136,128]{1,0:T(8,128)S(1)} %get-tuple-element.30.eto_ref), channel_id=1, source_target_pairs={{0,1},{1,0},{2,3},{3,2},{4,5},{5,4},{6,7},{7,6},{8,9},{9,8},{10,11... | collective-permute-start | bytes 208904 | tf_op jit(solution)/shard_map/ppermute | solution.py:559
  6.3 10.9 %collective-permute-start.2 = (bf16[24,1280]{1,0:T(8,128)(2,1)S(1)}, bf16[24,1280]{1,0:T(8,128)(2,1)S(1)}, u32[]{:S(2)}, u32[]{:S(2)}) collective-permute-start(bf16[24,1280]{1,0:T(8,128)(2,1)S(1)} %get-tuple-element.29), channel_id=1, source_target_pairs={{0,2},{2,4},{4,6},{6,8},{8,10},{10,12},{12,14},{14,16},{16,18},{18... | collective-permute-start | bytes 184328 | tf_op jit(solution)/shard_map/ppermute | solution.py:557
  7.7 9.5 %collective-permute-start.5 = (bf16[24,1280]{1,0:T(8,128)(2,1)S(1)}, bf16[24,1280]{1,0:T(8,128)(2,1)S(1)}, u32[]{:S(2)}, u32[]{:S(2)}) collective-permute-start(bf16[24,1280]{1,0:T(8,128)(2,1)S(1)} %get-tuple-element.28.p0), channel_id=1, source_target_pairs={{0,8},{2,10},{4,12},{6,14},{8,16},{10,18},{12,20},{14,22},{16,24},... | collective-permute-start | bytes 184328 | tf_op jit(solution)/shard_map/ppermute | solution.py:557
  9.3 8.7 %collective-permute-start.4 = (bf16[24,1280]{1,0:T(8,128)(2,1)S(1)}, bf16[24,1280]{1,0:T(8,128)(2,1)S(1)}, u32[]{:S(2)}, u32[]{:S(2)}) collective-permute-start(bf16[24,1280]{1,0:T(8,128)(2,1)S(1)} %get-tuple-element.28.p0), channel_id=1, source_target_pairs={{0,6},{2,8},{4,10},{6,12},{8,14},{10,16},{12,18},{14,20},{16,22},{... | collective-permute-start | bytes 184328 | tf_op jit(solution)/shard_map/ppermute | solution.py:557
  12.1 8.8 %collective-permute-start.3 = (bf16[24,1280]{1,0:T(8,128)(2,1)S(1)}, bf16[24,1280]{1,0:T(8,128)(2,1)S(1)}, u32[]{:S(2)}, u32[]{:S(2)}) collective-permute-start(bf16[24,1280]{1,0:T(8,128)(2,1)S(1)} %get-tuple-element.28.p0), channel_id=1, source_target_pairs={{0,4},{2,6},{4,8},{6,10},{8,12},{10,14},{12,16},{14,18},{16,20},{1... | collective-permute-start | bytes 184328 | tf_op jit(solution)/shard_map/ppermute | solution.py:557
  28.0 22.2 %all-to-all-start = ((bf16[64,72,128]{2,1,0:T(8,128)(2,1)}), bf16[64,72,128]{2,1,0:T(8,128)(2,1)S(1)}, u32[]{:S(2)}, u32[]{:S(2)}) async-start(bf16[64,72,128]{2,1,0:T(8,128)(2,1)} %get-tuple-element.39), calls=%async_computation | async-start | bytes 2359296 | tf_op jit(solution)/shard_map/all_to_all | solution.py:564
  32.6 4.0 %collective-permute-start.8 = (f32[5,8,1280]{2,1,0:T(8,128)S(1)}, f32[5,8,1280]{2,1,0:T(8,128)S(1)}, u32[]{:S(2)}, u32[]{:S(2)}) collective-permute-start(f32[5,8,1280]{2,1,0:T(8,128)S(1)} %get-tuple-element.32.own_w_ref), channel_id=1, source_target_pairs={{0,1},{1,0},{2,3},{3,2},{4,5},{5,4},{6,7},{7,6},{8,9},{9,8},{10,11... | collective-permute-start | bytes 614408 | tf_op jit(solution)/shard_map/ppermute | solution.py:567
  35.1 1.6 %collective-permute-start.7 = (bf16[3,8,1280]{2,1,0:T(8,128)(2,1)S(1)}, bf16[3,8,1280]{2,1,0:T(8,128)(2,1)S(1)}, u32[]{:S(2)}, u32[]{:S(2)}) collective-permute-start(bf16[3,8,1280]{2,1,0:T(8,128)(2,1)S(1)} %get-tuple-element.31.own_halo_ref), channel_id=1, source_target_pairs={{0,1},{1,0},{2,3},{3,2},{4,5},{5,4},{6,7},{7,6},{8,9},{9,8},{10,11... | collective-permute-start | bytes 184328 | tf_op jit(solution)/shard_map/ppermute | solution.py:566
  35.2 30.9 %collective-permute-start.9 = (bf16[4,4,4,64,128]{4,3,2,1,0:T(8,128)(2,1)}, bf16[4,4,4,64,128]{4,3,2,1,0:T(8,128)(2,1)}, u32[]{:S(2)}, u32[]{:S(2)}) collective-permute-start(bf16[4,4,4,64,128]{4,3,2,1,0:T(8,128)(2,1)} %get-tuple-element.36.before_ref), channel_id=1, source_target_pairs={{0,1},{2,3},{4,5},{6,7},{8,9},{10,11},{12,13},{14,15},{16,17},{18,... | collective-permute-start | bytes 3145736 | tf_op jit(solution)/shard_map/ppermute | solution.py:565
  50.2 1.0 %copy-start.9 = (bf16[64,72,128]{2,1,0:T(8,128)(2,1)}, bf16[64,72,128]{2,1,0:T(8,128)(2,1)S(1)}, u32[]{:S(2)}) copy-start(bf16[64,72,128]{2,1,0:T(8,128)(2,1)S(1)} %all-to-all-done.in_hbm) | copy-start | bytes 3538948
  51.2 7.8 %copy-start.10 = (f32[128]{0:T(128)S(1)}, f32[128]{0:T(128)}, u32[]{:S(2)}) copy-start(f32[128]{0:T(128)} %param.16) | copy-start | bytes 1540
  51.2 8.0 %copy-start = (bf16[8,128,256]{2,1,0:T(8,128)(2,1)S(1)}, bf16[8,128,256]{2,1,0:T(8,128)(2,1)}, u32[]{:S(2)}) copy-start(bf16[8,128,256]{2,1,0:T(8,128)(2,1)} %get-tuple-element.34.bc_ref) | copy-start | bytes 1572868
  51.2 8.0 %copy-start.1 = (bf16[128,8192]{1,0:T(8,128)(2,1)S(1)}, bf16[128,8192]{1,0:T(8,128)(2,1)}, u32[]{:S(2)}) copy-start(bf16[128,8192]{1,0:T(8,128)(2,1)} %gate_ref.3) | copy-start | bytes 6291460
  53.5 20.6 %all-to-all-start.1 = ((bf16[64,64,128]{2,1,0:T(8,128)(2,1)}), bf16[64,64,128]{2,1,0:T(8,128)(2,1)}, u32[]{:S(2)}, u32[]{:S(2)}) async-start(bf16[64,64,128]{2,1,0:T(8,128)(2,1)} %scan.1), calls=%async_computation.1 | async-start | bytes 2097152 | tf_op jit(solution)/shard_map/all_to_all | solution.py:574
  59.3 1.6 %copy-start.2 = (bf16[8,128,1024]{2,1,0:T(8,128)(2,1)S(1)}, bf16[8,128,1024]{2,1,0:T(8,128)(2,1)}, u32[]{:S(2)}) copy-start(bf16[8,128,1024]{2,1,0:T(8,128)(2,1)} %get-tuple-element.33.x_ref) | copy-start | bytes 6291460
  60.9 5.2 %copy-start.3 = (bf16[8,128,1024]{2,1,0:T(8,128)(2,1)S(1)}, bf16[8,128,1024]{2,1,0:T(8,128)(2,1)}, u32[]{:S(2)}) copy-start(bf16[8,128,1024]{2,1,0:T(8,128)(2,1)} %get-tuple-element.33.x_ref) | copy-start | bytes 6291460
  66.1 12.3 %copy-start.6 = (f32[8192]{0:T(1024)S(1)}, f32[8192]{0:T(1024)}, u32[]{:S(2)}) copy-start(f32[8192]{0:T(1024)} %param.17) | copy-start | bytes 98308
  74.1 7.6 %collective-permute-start.10 = (bf16[64,64,128]{2,1,0:T(8,128)(2,1)}, bf16[64,64,128]{2,1,0:T(8,128)(2,1)S(1)}, u32[]{:S(2)}, u32[]{:S(2)}) collective-permute-start(bf16[64,64,128]{2,1,0:T(8,128)(2,1)} %all-to-all-done.1.state_ref), channel_id=1, source_target_pairs={{0,1},{1,0},{2,3},{3,2},{4,5},{5,4},{6,7},{7,6},{8,9},{9,8},{10,11... | collective-permute-start | bytes 3145736 | tf_op jit(solution)/shard_map/ppermute | solution.py:576
  78.4 3.3 %copy-start.4 = (bf16[4,128,1024]{2,1,0:T(8,128)(2,1)S(1)}, bf16[4,128,1024]{2,1,0:T(8,128)(2,1)}, u32[]{:S(2)}) copy-start(bf16[4,128,1024]{2,1,0:T(8,128)(2,1)} %get-tuple-element.37.p_ref) | copy-start | bytes 3145732
  78.4 3.3 %copy-start.5 = (bf16[4,128,1024]{2,1,0:T(8,128)(2,1)S(1)}, bf16[4,128,1024]{2,1,0:T(8,128)(2,1)}, u32[]{:S(2)}) copy-start(bf16[4,128,1024]{2,1,0:T(8,128)(2,1)} %get-tuple-element.38.q_ref) | copy-start | bytes 3145732

commit v4 on v3

--- a/solution.py
+++ b/solution.py
@@ -362,25 +362,22 @@
     )(core, from_hbm(conv_input), from_hbm(sib), own_halo, sib_halo, own_weights, sib_weights)
 
 
-def scan_kernel(chips, in_hbm, done_ref, out_hbm, in_ref, out_ref, sems):
+def scan_kernel(chips, in_ref, done_ref, out_hbm, out_ref, sems):
     each = CHUNKS // chips
     parts = 4
     size = CHUNKS // parts
-    spans = [pl.ds(k * size, size) for k in range(parts)]
-    loads = [pltpu.make_async_copy(in_hbm.at[at], in_ref.at[at], sems.at[0, k]) for k, at in enumerate(spans)]
-    stores = [pltpu.make_async_copy(out_ref.at[at], out_hbm.at[at], sems.at[1, k]) for k, at in enumerate(spans)]
-    for load in loads:
-        load.start()
     states = [jnp.zeros((64, LANE), F32) for _ in range(each)]
+    stores = []
     for k in range(parts):
-        loads[k].wait()
         for at in range(k * size, (k + 1) * size):
             i = at % each
             extra = in_ref[at, 64:ROWS].astype(F32)
             state = extra[3:4] * states[i]
             out_ref[at] = state.astype(BF16)
             states[i] = (extra[0:1] + extra[1:2] + extra[2:3]) * state + in_ref[at, 0:64].astype(F32)
-        stores[k].start()
+        span = pl.ds(k * size, size)
+        stores.append(pltpu.make_async_copy(out_ref.at[span], out_hbm.at[span], sems.at[k]))
+        stores[-1].start()
     for store in stores:
         store.wait()
 
@@ -388,17 +385,13 @@
 def scan(chips, pieces, done):
     return pl.pallas_call(
         functools.partial(scan_kernel, chips),
-        in_specs=in_hbm(1) + [pl.BlockSpec(memory_space=pl.ANY)],
+        in_specs=in_vmem(1) + [pl.BlockSpec(memory_space=pl.ANY)],
         out_specs=in_hbm(1)[0],
         out_shape=hbm((CHUNKS, 64, LANE)),
-        scratch_shapes=[
-            pltpu.VMEM((CHUNKS, ROWS, LANE), BF16),
-            pltpu.VMEM((CHUNKS, 64, LANE), BF16),
-            pltpu.SemaphoreType.DMA((2, 4)),
-        ],
-        compiler_params=params(),
+        scratch_shapes=[pltpu.VMEM((CHUNKS, 64, LANE), BF16), pltpu.SemaphoreType.DMA((4,))],
+        compiler_params=params(4),
         name="scan",
-    )(from_hbm(pieces), done)
+    )(pieces, done)
 
 
 def local_kernel(other, core_ref, len_ref, x_ref, bc_ref, tab_ref, before_ref, dts_ref, gate_ref, skip_ref, p_ref, q_ref, done_ref):
@@ -406,7 +399,9 @@
     done_ref[...] = jnp.zeros_like(done_ref)
     group = (core + other) % 2 + 2 * pl.program_id(0)
     inner, after, since = (tab_ref[k] for k in range(3))
-    d_before = jnp.where(core == 1, dts_ref[TOK:], 1.0)
+    since = since * jnp.where(core == 1, dts_ref[TOK : TOK + 1], 1.0)
+    rise = jnp.where(core == 1, tab_ref[2, TOK // 2 - 1 : TOK // 2], 0.0)
+    rise = jnp.broadcast_to(rise, (8, LANE))
     spread = lambda table, j: jnp.concatenate([widen(table, group * 16 + j * 4 + 2 * k) for k in range(2)], axis=1)
     b = bc_ref[0, :, :LANE]
     c = bc_ref[0, :, LANE:]
@@ -418,18 +413,17 @@
         at = slice(j * LW, (j + 1) * LW)
         x = x_ref[0, :, at].astype(F32)
         scaled = (x * spread(inner, j)).astype(BF16)
-        y = spread(after, j) * jnp.dot(scores, scaled, preferred_element_type=F32)
         before = jnp.concatenate(
             [jnp.concatenate([before_ref[0, j, tile * 2], before_ref[0, j, tile * 2 + 1]], axis=0) for tile in range(2)],
             axis=1,
         )
-        grown = spread(since, j)
-        y = y + grown * (core.astype(F32) * jnp.dot(c, before, preferred_element_type=F32))
-        y = y + skip_ref[:, at] * x
+        read = jnp.dot(scores, scaled, preferred_element_type=F32)
+        read = read + spread(rise, j)[0:1] * jnp.dot(c, before, preferred_element_type=F32)
+        y = spread(after, j) * read + skip_ref[:, at] * x
         half = gate_ref[:, at].astype(F32) * 0.5
         silu = half + half * jnp.tanh(half)
         p_ref[0, :, at] = jnp.where(live, y * silu, 0.0).astype(BF16)
-        q_ref[0, :, at] = jnp.where(live, grown * spread(d_before, j)[0:1] * silu, 0.0).astype(BF16)
+        q_ref[0, :, at] = jnp.where(live, spread(since, j) * silu, 0.0).astype(BF16)
 
 
 def local(other, core, seg_length, x, bc, tables, before, d_sib, gate_input, skip):
@@ -457,7 +451,7 @@
         compiler_params=params(),
         cost_estimate=pl.CostEstimate(flops=400_000_000, bytes_accessed=8_000_000, transcendentals=600_000),
         name="local",
-    )(core, seg_length, x, bc, tables, before, d_sib, gate_input, skip)
+    )(core, seg_length, from_hbm(x), from_hbm(bc), tables, from_hbm(before), d_sib, from_hbm(gate_input), skip)
 
 
 def finish_kernel(other, core_ref, p_ref, q_ref, bc_ref, state_ref, gain_ref, *rest):
@@ -570,7 +564,6 @@
     skip = jnp.repeat(skip_gain, HEAD_DIM)[None]
     p_own, q_own, done_own = local(0, core, seg_length, x, bc, tables, before_own, et_sib, gate_input, skip)
     p_oth, q_oth, done_oth = local(1, core, seg_length, x, bc, tables, before_oth, et_sib, gate_input, skip)
-    pieces, done = lax.optimization_barrier((pieces, done))
     states = lax.all_to_all(scan(chips, pieces, done), CHIPS, 0, 0, tiled=True)
     states, done = lax.optimization_barrier((states, done_own + done_oth))
     states_oth = lax.ppermute(states, "core", swap)

time: 84.1 us -> 81.3 us (0.967)
  local copies, waits for them, and re-layouts: 2.84 us -> 0.21 us
  waiting for transfers between devices: 19.6 us -> 20.7 us
    unnamed x22 -> x18, local copies, waits for them, and re-layouts: 2.66 us -> 0.03 us
    pallas_call x1, Pallas kernels: 2.25 us -> 1.13 us  [scan(): pl.pallas_call(functools.partial(scan_kernel, chips), in_specs=in_vmem(1)...]
    all_to_all x1, waiting for transfers between devices: 2.87 us -> 3.91 us  [body(): states = lax.all_to_all(scan(chips, pieces, done), CHIPS, 0, 0, tiled=True)]
    all_to_all x1, starting transfers between devices: 5.52 us -> 4.66 us  [body(): states = lax.all_to_all(scan(chips, pieces, done), CHIPS, 0, 0, tiled=True)]
where the time goes in v4:
time: 81.3 us; the launch traced here: 80.7 us
  Pallas kernels  30.8 us (38%)
  starting transfers between devices  27.4 us (34%)
  waiting for transfers between devices  20.7 us (25%)
  between operations  1.64 us (2%)
    pallas_call x2, Pallas kernels, local(): pl.pallas_call(functools.partial(local_kernel, other), grid_spec=pltpu.Pr...  11 us
    all_to_all x1, waiting for transfers between devices, body(): pieces = lax.all_to_all(pieces, CHIPS, 0, 0, tiled=True)  8.08 us
    ppermute x4, starting transfers between devices, body(): lax.ppermute(tail if k > 1 else onward, CHIPS, [(c, (c + k) % chips) for...  7.52 us
    pallas_call x1, Pallas kernels, chip_states(): pl.pallas_call(states_kernel, in_specs=in_smem(2) + in_hbm(2) + in_vmem(7...  7.05 us
    ppermute x4, waiting for transfers between devices, body(): lax.ppermute(tail if k > 1 else onward, CHIPS, [(c, (c + k) % chips) for...  6.44 us
    pallas_call x1, Pallas kernels, activate(): pl.pallas_call(act_kernel, in_specs=in_smem(1) + in_hbm(2) + in_vmem(4),...  5.45 us
    pallas_call x2, Pallas kernels, finish(): pl.pallas_call(functools.partial(finish_kernel, other), in_specs=in_specs...  4.87 us
    all_to_all x1, starting transfers between devices, body(): pieces = lax.all_to_all(pieces, CHIPS, 0, 0, tiled=True)  4.8 us
  transfers between devices with their start and end apart: 13, of which 6 were waited for; matrix products, arithmetic and copies ran while one was open for 0% of the time, Pallas kernels for 27%

profile of v4, /device:TPU:1, one launch (start us, length us, event | category | flops | bytes accessed | tf_op | source)
XLA Modules:
  0.0 80.7 jit_solution(17150752380757144254)
XLA Ops:
  0.0 1.4 %collective-permute-start = (bf16[128,8,1280]{2,1,0:T(8,128)(2,1)}, bf16[128,8,1280]{2,1,0:T(8,128)(2,1)}, u32[]{:S(2)}, u32[]{:S(2)}) collective-permute-start(bf16[128,8,1280]{2,1,0:T(8,128)(2,1)} %conv_hbm.3), channel_id=1, source_target_pairs={{0,1},{1,0},{2,3},{3,2},{4,5},{5,4},{6,7},{7,6},{8,9},{9,8},{10,11... | collective-permute-start | bytes 7864328 | tf_op jit(solution)/shard_map/ppermute | solution.py:547
  2.1 1.2 %start.1 = (f32[3,128,128]{2,1,0:T(8,128)S(1)}, f32[136,128]{1,0:T(8,128)S(1)}, bf16[6,8,1280]{2,1,0:T(8,128)(2,1)S(1)}) custom-call(s32[1]{0:T(128)S(6)} %copy.13.len_ref, bf16[128,128]{1,0:T(8,128)(2,1)} %decay_hbm.1, bf16[128,128]{1,0:T(8,128)(2,1)} %step_hbm.1, bf16[128,8,1280]{2,1,0:T(8,128)(2,1)} %conv_hbm.3), custom_call_target="tpu_custom_call" | custom-call | tf_op jit(solution)/shard_map/start/pallas_call | solution.py:109
  3.9 2.2 %collective-permute-done.1.sib_ref = bf16[6,8,1280]{2,1,0:T(8,128)(2,1)S(1)} collective-permute-done((bf16[6,8,1280]{2,1,0:T(8,128)(2,1)S(1)}, bf16[6,8,1280]{2,1,0:T(8,128)(2,1)S(1)}, u32[]{:S(2)}, u32[]{:S(2)}) %collective-permute-start.1) | collective-permute-done | bytes 122912 | tf_op jit(solution)/shard_map/ppermute | solution.py:549
  6.3 1.4 %collective-permute-start.2 = (bf16[24,1280]{1,0:T(8,128)(2,1)S(1)}, bf16[24,1280]{1,0:T(8,128)(2,1)S(1)}, u32[]{:S(2)}, u32[]{:S(2)}) collective-permute-start(bf16[24,1280]{1,0:T(8,128)(2,1)S(1)} %get-tuple-element.27), channel_id=1, source_target_pairs={{0,2},{2,4},{4,6},{6,8},{8,10},{10,12},{12,14},{14,16},{16,18},{18... | collective-permute-start | bytes 184328 | tf_op jit(solution)/shard_map/ppermute | solution.py:551
  7.7 1.6 %collective-permute-start.5 = (bf16[24,1280]{1,0:T(8,128)(2,1)S(1)}, bf16[24,1280]{1,0:T(8,128)(2,1)S(1)}, u32[]{:S(2)}, u32[]{:S(2)}) collective-permute-start(bf16[24,1280]{1,0:T(8,128)(2,1)S(1)} %get-tuple-element.26.p0), channel_id=1, source_target_pairs={{0,8},{2,10},{4,12},{6,14},{8,16},{10,18},{12,20},{14,22},{16,24},... | collective-permute-start | bytes 184328 | tf_op jit(solution)/shard_map/ppermute | solution.py:551
  9.3 2.7 %collective-permute-start.4 = (bf16[24,1280]{1,0:T(8,128)(2,1)S(1)}, bf16[24,1280]{1,0:T(8,128)(2,1)S(1)}, u32[]{:S(2)}, u32[]{:S(2)}) collective-permute-start(bf16[24,1280]{1,0:T(8,128)(2,1)S(1)} %get-tuple-element.26.p0), channel_id=1, source_target_pairs={{0,6},{2,8},{4,10},{6,12},{8,14},{10,16},{12,18},{14,20},{16,22},{... | collective-permute-start | bytes 184328 | tf_op jit(solution)/shard_map/ppermute | solution.py:551
  12.1 1.7 %collective-permute-start.3 = (bf16[24,1280]{1,0:T(8,128)(2,1)S(1)}, bf16[24,1280]{1,0:T(8,128)(2,1)S(1)}, u32[]{:S(2)}, u32[]{:S(2)}) collective-permute-start(bf16[24,1280]{1,0:T(8,128)(2,1)S(1)} %get-tuple-element.26.p0), channel_id=1, source_target_pairs={{0,4},{2,6},{4,8},{6,10},{8,12},{10,14},{12,16},{14,18},{16,20},{1... | collective-permute-start | bytes 184328 | tf_op jit(solution)/shard_map/ppermute | solution.py:551
  14.4 2.7 %collective-permute-done.2.p1 = bf16[24,1280]{1,0:T(8,128)(2,1)S(1)} collective-permute-done((bf16[24,1280]{1,0:T(8,128)(2,1)S(1)}, bf16[24,1280]{1,0:T(8,128)(2,1)S(1)}, u32[]{:S(2)}, u32[]{:S(2)}) %collective-permute-start.2) | collective-permute-done | bytes 61472 | tf_op jit(solution)/shard_map/ppermute | solution.py:551
  17.2 0.9 %collective-permute-done.4.p3 = bf16[24,1280]{1,0:T(8,128)(2,1)S(1)} collective-permute-done((bf16[24,1280]{1,0:T(8,128)(2,1)S(1)}, bf16[24,1280]{1,0:T(8,128)(2,1)S(1)}, u32[]{:S(2)}, u32[]{:S(2)}) %collective-permute-start.4) | collective-permute-done | bytes 61472 | tf_op jit(solution)/shard_map/ppermute | solution.py:551
  18.0 2.9 %collective-permute-done.3.p2 = bf16[24,1280]{1,0:T(8,128)(2,1)S(1)} collective-permute-done((bf16[24,1280]{1,0:T(8,128)(2,1)S(1)}, bf16[24,1280]{1,0:T(8,128)(2,1)S(1)}, u32[]{:S(2)}, u32[]{:S(2)}) %collective-permute-start.3) | collective-permute-done | bytes 61472 | tf_op jit(solution)/shard_map/ppermute | solution.py:551
  20.9 7.0 %chip_states.1 = (bf16[64,72,128]{2,1,0:T(8,128)(2,1)}, bf16[4,4,4,64,128]{4,3,2,1,0:T(8,128)(2,1)}, f32[5,8,1280]{2,1,0:T(8,128)S(1)}, bf16[3,8,1280]{2,1,0:T(8,128)(2,1)S(1)}) custom-call(s32[1]{0:T(128)} %bitcast.core_ref, s32[1]{0:T(128)S(6)} %copy.14.first_ref, bf16[128,8,1280]{2,1,0:T(8,128)(2,1)} %conv_hbm.3, ...), custom_call_target="tpu_custom_call" | custom-call | tf_op jit(solution)/shard_map/chip_states/pallas_call | solution.py:273
  27.9 4.8 %all-to-all-start = ((bf16[64,72,128]{2,1,0:T(8,128)(2,1)}), bf16[64,72,128]{2,1,0:T(8,128)(2,1)S(1)}, u32[]{:S(2)}, u32[]{:S(2)}) async-start(bf16[64,72,128]{2,1,0:T(8,128)(2,1)} %get-tuple-element.37), calls=%async_computation | async-start | bytes 2359296 | tf_op jit(solution)/shard_map/all_to_all | solution.py:558
  32.8 2.4 %collective-permute-start.8 = (f32[5,8,1280]{2,1,0:T(8,128)S(1)}, f32[5,8,1280]{2,1,0:T(8,128)S(1)}, u32[]{:S(2)}, u32[]{:S(2)}) collective-permute-start(f32[5,8,1280]{2,1,0:T(8,128)S(1)} %get-tuple-element.30.own_w_ref), channel_id=1, source_target_pairs={{0,1},{1,0},{2,3},{3,2},{4,5},{5,4},{6,7},{7,6},{8,9},{9,8},{10,11... | collective-permute-start | bytes 614408 | tf_op jit(solution)/shard_map/ppermute | solution.py:561
  35.3 1.5 %collective-permute-start.9 = (bf16[4,4,4,64,128]{4,3,2,1,0:T(8,128)(2,1)S(1)}, bf16[4,4,4,64,128]{4,3,2,1,0:T(8,128)(2,1)}, u32[]{:S(2)}, u32[]{:S(2)}) collective-permute-start(bf16[4,4,4,64,128]{4,3,2,1,0:T(8,128)(2,1)S(1)} %copy-done.7), channel_id=1, source_target_pairs={{0,1},{2,3},{4,5},{6,7},{8,9},{10,11},{12,13},{14,15},{16,17},{18,... | collective-permute-start | bytes 3145736 | tf_op jit(solution)/shard_map/ppermute | solution.py:559
  36.8 5.4 %activate.1 = (bf16[8,128,1024]{2,1,0:T(8,128)(2,1)}, bf16[8,128,256]{2,1,0:T(8,128)(2,1)}, f32[8,128]{1,0:T(8,128)S(1)}) custom-call(s32[1]{0:T(128)} %bitcast.core_ref, bf16[128,8,1280]{2,1,0:T(8,128)(2,1)} %conv_hbm.3, bf16[128,8,1280]{2,1,0:T(8,128)(2,1)} %collective-permute-done.sib_hbm, bf16[3,8,1280]{2,1,0:T(8,128)(2,1)S(1)} %get-tuple-element.29.own_halo_ref, ...), custom_call_target="tpu_custom_call" | custom-call | flops 20000000 | bytes 8000000 | tf_op jit(solution)/shard_map/activate/pallas_call | solution.py:345
  42.2 8.1 %all-to-all-done.in_ref = bf16[64,72,128]{2,1,0:T(8,128)(2,1)S(1)} async-done(((bf16[64,72,128]{2,1,0:T(8,128)(2,1)}), bf16[64,72,128]{2,1,0:T(8,128)(2,1)S(1)}, u32[]{:S(2)}, u32[]{:S(2)}) %all-to-all-start) | async-done | bytes 1179680 | tf_op jit(solution)/shard_map/all_to_all | solution.py:558
  50.3 1.1 %scan.1 = bf16[64,64,128]{2,1,0:T(8,128)(2,1)} custom-call(bf16[64,72,128]{2,1,0:T(8,128)(2,1)S(1)} %all-to-all-done.in_ref, f32[8,128]{1,0:T(8,128)S(1)} %get-tuple-element.38.done_ref), custom_call_target="tpu_custom_call" | custom-call | tf_op jit(solution)/shard_map/scan/pallas_call | solution.py:386
  51.5 4.7 %all-to-all-start.1 = ((bf16[64,64,128]{2,1,0:T(8,128)(2,1)}), bf16[64,64,128]{2,1,0:T(8,128)(2,1)S(1)}, u32[]{:S(2)}, u32[]{:S(2)}) async-start(bf16[64,64,128]{2,1,0:T(8,128)(2,1)} %scan.1), calls=%async_computation.1 | async-start | bytes 2097152 | tf_op jit(solution)/shard_map/all_to_all | solution.py:567
  56.3 5.5 %local.3 = (bf16[4,128,1024]{2,1,0:T(8,128)(2,1)}, bf16[4,128,1024]{2,1,0:T(8,128)(2,1)}, f32[8,128]{1,0:T(8,128)S(1)}) custom-call(s32[1]{0:T(128)} %bitcast.core_ref, s32[1]{0:T(128)S(6)} %copy.13.len_ref, bf16[8,128,1024]{2,1,0:T(8,128)(2,1)} %get-tuple-element.31.x_ref, bf16[8,128,256]{2,1,0:T(8,128)(2,1)} %get-tuple-element.32.bc_ref, ...), custom_call_target="tpu_custom_call" | custom-call | flops 400000000 | bytes 8000000 | tf_op jit(solution)/shard_map/local/pallas_call | solution.py:433
  61.8 5.5 %local.2 = (bf16[4,128,1024]{2,1,0:T(8,128)(2,1)}, bf16[4,128,1024]{2,1,0:T(8,128)(2,1)}, f32[8,128]{1,0:T(8,128)S(1)}) custom-call(s32[1]{0:T(128)} %bitcast.core_ref, s32[1]{0:T(128)S(6)} %copy.13.len_ref, bf16[8,128,1024]{2,1,0:T(8,128)(2,1)} %get-tuple-element.31.x_ref, bf16[8,128,256]{2,1,0:T(8,128)(2,1)} %get-tuple-element.32.bc_ref, ...), custom_call_target="tpu_custom_call" | custom-call | flops 400000000 | bytes 8000000 | tf_op jit(solution)/shard_map/local/pallas_call | solution.py:433
  67.3 3.9 %all-to-all-done.1.state_ref = bf16[64,64,128]{2,1,0:T(8,128)(2,1)S(1)} async-done(((bf16[64,64,128]{2,1,0:T(8,128)(2,1)}), bf16[64,64,128]{2,1,0:T(8,128)(2,1)S(1)}, u32[]{:S(2)}, u32[]{:S(2)}) %all-to-all-start.1) | async-done | bytes 1048608 | tf_op jit(solution)/shard_map/all_to_all | solution.py:567
  71.2 4.4 %collective-permute-start.10 = (bf16[64,64,128]{2,1,0:T(8,128)(2,1)S(1)}, bf16[64,64,128]{2,1,0:T(8,128)(2,1)S(1)}, u32[]{:S(2)}, u32[]{:S(2)}) collective-permute-start(bf16[64,64,128]{2,1,0:T(8,128)(2,1)S(1)} %all-to-all-done.1.state_ref), channel_id=1, source_target_pairs={{0,1},{1,0},{2,3},{3,2},{4,5},{5,4},{6,7},{7,6},{8,9},{9,8},{10,11... | collective-permute-start | bytes 3145736 | tf_op jit(solution)/shard_map/ppermute | solution.py:569
  75.6 3.3 %finish.2.rest_0_ = bf16[128,8192]{1,0:T(8,128)(2,1)} custom-call(s32[1]{0:T(128)} %bitcast.core_ref, bf16[4,128,1024]{2,1,0:T(8,128)(2,1)} %get-tuple-element.42.p_ref, bf16[4,128,1024]{2,1,0:T(8,128)(2,1)} %get-tuple-element.43.q_ref, bf16[8,128,256]{2,1,0:T(8,128)(2,1)S(1)} %copy-done, bf16[64,64,128]{2,1,0:T(8,128)(2,1)} %copy-done.6, ...), custom_call_target="tpu_custom_call" | custom-call | flops 200000000 | bytes 4000000 | tf_op jit(solution)/shard_map/finish/pallas_call | solution.py:516
  79.0 1.6 %finish.3 = bf16[128,8192]{1,0:T(8,128)(2,1)} custom-call(s32[1]{0:T(128)} %bitcast.core_ref, bf16[4,128,1024]{2,1,0:T(8,128)(2,1)S(1)} %copy-done.1, bf16[4,128,1024]{2,1,0:T(8,128)(2,1)S(1)} %copy-done.2, bf16[8,128,256]{2,1,0:T(8,128)(2,1)S(1)} %copy-done, ...), custom_call_target="tpu_custom_call", output_to_operand_aliasing={{}: (6, {})} | custom-call | flops 200000000 | bytes 4000000 | tf_op jit(solution)/shard_map/finish/pallas_call | solution.py:516
  (32 shorter events, 1.0 us)
Async XLA Ops:
  0.0 6.1 %copy-start.5 = (f32[1,1280]{1,0:T(1,128)S(1)}, f32[1,1280]{1,0:T(1,128)}, u32[]{:S(2)}) copy-start(f32[1,1280]{1,0:T(1,128)} %bias_ref.1) | copy-start | bytes 15364
  0.0 6.1 %copy-start.4 = (f32[4,1,1280]{2,1,0:T(1,128)S(1)}, f32[4,1,1280]{2,1,0:T(1,128)}, u32[]{:S(2)}) copy-start(f32[4,1,1280]{2,1,0:T(1,128)} %weight_ref.1) | copy-start | bytes 61444
  0.0 20.9 %collective-permute-start = (bf16[128,8,1280]{2,1,0:T(8,128)(2,1)}, bf16[128,8,1280]{2,1,0:T(8,128)(2,1)}, u32[]{:S(2)}, u32[]{:S(2)}) collective-permute-start(bf16[128,8,1280]{2,1,0:T(8,128)(2,1)} %conv_hbm.3), channel_id=1, source_target_pairs={{0,1},{1,0},{2,3},{3,2},{4,5},{5,4},{6,7},{7,6},{8,9},{9,8},{10,11... | collective-permute-start | bytes 7864328 | tf_op jit(solution)/shard_map/ppermute | solution.py:547
  3.3 2.8 %collective-permute-start.1 = (bf16[6,8,1280]{2,1,0:T(8,128)(2,1)S(1)}, bf16[6,8,1280]{2,1,0:T(8,128)(2,1)S(1)}, u32[]{:S(2)}, u32[]{:S(2)}) collective-permute-start(bf16[6,8,1280]{2,1,0:T(8,128)(2,1)S(1)} %get-tuple-element.25.own_ref), channel_id=1, source_target_pairs={{0,1},{1,0},{2,3},{3,2},{4,5},{5,4},{6,7},{7,6},{8,9},{9,8},{10,11... | collective-permute-start | bytes 368648 | tf_op jit(solution)/shard_map/ppermute | solution.py:549
  3.4 8.6 %collective-permute-start.6 = (f32[136,128]{1,0:T(8,128)S(1)}, f32[136,128]{1,0:T(8,128)S(1)}, u32[]{:S(2)}, u32[]{:S(2)}) collective-permute-start(f32[136,128]{1,0:T(8,128)S(1)} %get-tuple-element.28.eto_ref), channel_id=1, source_target_pairs={{0,1},{1,0},{2,3},{3,2},{4,5},{5,4},{6,7},{7,6},{8,9},{9,8},{10,11... | collective-permute-start | bytes 208904 | tf_op jit(solution)/shard_map/ppermute | solution.py:553
  6.3 10.9 %collective-permute-start.2 = (bf16[24,1280]{1,0:T(8,128)(2,1)S(1)}, bf16[24,1280]{1,0:T(8,128)(2,1)S(1)}, u32[]{:S(2)}, u32[]{:S(2)}) collective-permute-start(bf16[24,1280]{1,0:T(8,128)(2,1)S(1)} %get-tuple-element.27), channel_id=1, source_target_pairs={{0,2},{2,4},{4,6},{6,8},{8,10},{10,12},{12,14},{14,16},{16,18},{18... | collective-permute-start | bytes 184328 | tf_op jit(solution)/shard_map/ppermute | solution.py:551
  7.7 9.5 %collective-permute-start.5 = (bf16[24,1280]{1,0:T(8,128)(2,1)S(1)}, bf16[24,1280]{1,0:T(8,128)(2,1)S(1)}, u32[]{:S(2)}, u32[]{:S(2)}) collective-permute-start(bf16[24,1280]{1,0:T(8,128)(2,1)S(1)} %get-tuple-element.26.p0), channel_id=1, source_target_pairs={{0,8},{2,10},{4,12},{6,14},{8,16},{10,18},{12,20},{14,22},{16,24},... | collective-permute-start | bytes 184328 | tf_op jit(solution)/shard_map/ppermute | solution.py:551
  9.3 8.7 %collective-permute-start.4 = (bf16[24,1280]{1,0:T(8,128)(2,1)S(1)}, bf16[24,1280]{1,0:T(8,128)(2,1)S(1)}, u32[]{:S(2)}, u32[]{:S(2)}) collective-permute-start(bf16[24,1280]{1,0:T(8,128)(2,1)S(1)} %get-tuple-element.26.p0), channel_id=1, source_target_pairs={{0,6},{2,8},{4,10},{6,12},{8,14},{10,16},{12,18},{14,20},{16,22},{... | collective-permute-start | bytes 184328 | tf_op jit(solution)/shard_map/ppermute | solution.py:551
  12.1 8.8 %collective-permute-start.3 = (bf16[24,1280]{1,0:T(8,128)(2,1)S(1)}, bf16[24,1280]{1,0:T(8,128)(2,1)S(1)}, u32[]{:S(2)}, u32[]{:S(2)}) collective-permute-start(bf16[24,1280]{1,0:T(8,128)(2,1)S(1)} %get-tuple-element.26.p0), channel_id=1, source_target_pairs={{0,4},{2,6},{4,8},{6,10},{8,12},{10,14},{12,16},{14,18},{16,20},{1... | collective-permute-start | bytes 184328 | tf_op jit(solution)/shard_map/ppermute | solution.py:551
  27.9 7.4 %copy-start.7 = (bf16[4,4,4,64,128]{4,3,2,1,0:T(8,128)(2,1)S(1)}, bf16[4,4,4,64,128]{4,3,2,1,0:T(8,128)(2,1)}, u32[]{:S(2)}) copy-start(bf16[4,4,4,64,128]{4,3,2,1,0:T(8,128)(2,1)} %get-tuple-element.34.before_ref) | copy-start | bytes 3145732
  27.9 22.4 %all-to-all-start = ((bf16[64,72,128]{2,1,0:T(8,128)(2,1)}), bf16[64,72,128]{2,1,0:T(8,128)(2,1)S(1)}, u32[]{:S(2)}, u32[]{:S(2)}) async-start(bf16[64,72,128]{2,1,0:T(8,128)(2,1)} %get-tuple-element.37), calls=%async_computation | async-start | bytes 2359296 | tf_op jit(solution)/shard_map/all_to_all | solution.py:558
  32.8 4.0 %collective-permute-start.8 = (f32[5,8,1280]{2,1,0:T(8,128)S(1)}, f32[5,8,1280]{2,1,0:T(8,128)S(1)}, u32[]{:S(2)}, u32[]{:S(2)}) collective-permute-start(f32[5,8,1280]{2,1,0:T(8,128)S(1)} %get-tuple-element.30.own_w_ref), channel_id=1, source_target_pairs={{0,1},{1,0},{2,3},{3,2},{4,5},{5,4},{6,7},{7,6},{8,9},{9,8},{10,11... | collective-permute-start | bytes 614408 | tf_op jit(solution)/shard_map/ppermute | solution.py:561
  35.2 1.6 %collective-permute-start.7 = (bf16[3,8,1280]{2,1,0:T(8,128)(2,1)S(1)}, bf16[3,8,1280]{2,1,0:T(8,128)(2,1)S(1)}, u32[]{:S(2)}, u32[]{:S(2)}) collective-permute-start(bf16[3,8,1280]{2,1,0:T(8,128)(2,1)S(1)} %get-tuple-element.29.own_halo_ref), channel_id=1, source_target_pairs={{0,1},{1,0},{2,3},{3,2},{4,5},{5,4},{6,7},{7,6},{8,9},{9,8},{10,11... | collective-permute-start | bytes 184328 | tf_op jit(solution)/shard_map/ppermute | solution.py:560
  35.3 26.5 %collective-permute-start.9 = (bf16[4,4,4,64,128]{4,3,2,1,0:T(8,128)(2,1)S(1)}, bf16[4,4,4,64,128]{4,3,2,1,0:T(8,128)(2,1)}, u32[]{:S(2)}, u32[]{:S(2)}) collective-permute-start(bf16[4,4,4,64,128]{4,3,2,1,0:T(8,128)(2,1)S(1)} %copy-done.7), channel_id=1, source_target_pairs={{0,1},{2,3},{4,5},{6,7},{8,9},{10,11},{12,13},{14,15},{16,17},{18,... | collective-permute-start | bytes 3145736 | tf_op jit(solution)/shard_map/ppermute | solution.py:559
  50.3 5.8 %copy-start.8 = (f32[128]{0:T(128)S(1)}, f32[128]{0:T(128)}, u32[]{:S(2)}) copy-start(f32[128]{0:T(128)} %param.16) | copy-start | bytes 1540
  51.5 19.8 %all-to-all-start.1 = ((bf16[64,64,128]{2,1,0:T(8,128)(2,1)}), bf16[64,64,128]{2,1,0:T(8,128)(2,1)S(1)}, u32[]{:S(2)}, u32[]{:S(2)}) async-start(bf16[64,64,128]{2,1,0:T(8,128)(2,1)} %scan.1), calls=%async_computation.1 | async-start | bytes 2097152 | tf_op jit(solution)/shard_map/all_to_all | solution.py:567
  61.8 13.8 %copy-start = (bf16[8,128,256]{2,1,0:T(8,128)(2,1)S(1)}, bf16[8,128,256]{2,1,0:T(8,128)(2,1)}, u32[]{:S(2)}) copy-start(bf16[8,128,256]{2,1,0:T(8,128)(2,1)} %get-tuple-element.32.bc_ref) | copy-start | bytes 1572868
  61.8 13.8 %copy-start.3 = (f32[8192]{0:T(1024)S(1)}, f32[8192]{0:T(1024)}, u32[]{:S(2)}) copy-start(f32[8192]{0:T(1024)} %param.17) | copy-start | bytes 98308
  71.2 4.4 %copy-start.6 = (bf16[64,64,128]{2,1,0:T(8,128)(2,1)}, bf16[64,64,128]{2,1,0:T(8,128)(2,1)S(1)}, u32[]{:S(2)}) copy-start(bf16[64,64,128]{2,1,0:T(8,128)(2,1)S(1)} %all-to-all-done.1.state_ref) | copy-start | bytes 3145732
  71.2 7.8 %collective-permute-start.10 = (bf16[64,64,128]{2,1,0:T(8,128)(2,1)S(1)}, bf16[64,64,128]{2,1,0:T(8,128)(2,1)S(1)}, u32[]{:S(2)}, u32[]{:S(2)}) collective-permute-start(bf16[64,64,128]{2,1,0:T(8,128)(2,1)S(1)} %all-to-all-done.1.state_ref), channel_id=1, source_target_pairs={{0,1},{1,0},{2,3},{3,2},{4,5},{5,4},{6,7},{7,6},{8,9},{9,8},{10,11... | collective-permute-start | bytes 3145736 | tf_op jit(solution)/shard_map/ppermute | solution.py:569
  75.6 3.3 %copy-start.1 = (bf16[4,128,1024]{2,1,0:T(8,128)(2,1)S(1)}, bf16[4,128,1024]{2,1,0:T(8,128)(2,1)}, u32[]{:S(2)}) copy-start(bf16[4,128,1024]{2,1,0:T(8,128)(2,1)} %get-tuple-element.35.p_ref) | copy-start | bytes 3145732
  75.6 3.4 %copy-start.2 = (bf16[4,128,1024]{2,1,0:T(8,128)(2,1)S(1)}, bf16[4,128,1024]{2,1,0:T(8,128)(2,1)}, u32[]{:S(2)}) copy-start(bf16[4,128,1024]{2,1,0:T(8,128)(2,1)} %get-tuple-element.36.q_ref) | copy-start | bytes 3145732

commit v5 on v4

--- a/solution.py
+++ b/solution.py
@@ -456,10 +456,20 @@
 
 def finish_kernel(other, core_ref, p_ref, q_ref, bc_ref, state_ref, gain_ref, *rest):
     first = (core_ref[0] + other) % 2
+    copies = []
+
+    def send(half, i, rows_ref, sems):
+        group = (core_ref[0] + half) % 2 + 2 * i
+        to = out_ref.at[:, pl.ds(pl.multiple_of(group * XW, XW), XW)]
+        copies.append(pltpu.make_async_copy(rows_ref.at[i], to, sems.at[half, i]))
+        copies[-1].start()
+
     if other:
-        _, out_ref, rows_ref, sems = rest
+        own_rows_ref, out_ref, rows_ref, sems = rest
+        for i in range(4):
+            send(0, i, own_rows_ref, sems)
     else:
-        _, out_ref, rows_ref, sems, p_to, q_to, state_to, load_sems = rest
+        _, rows_ref, p_to, q_to, state_to, load_sems = rest
         loads = []
         for i in range(4):
             group = pl.ds(i * 16, 16)
@@ -469,10 +479,9 @@
         for load in loads:
             load.start()
         p_ref, q_ref, state_ref = p_to, q_to, state_to
-    copies = []
     for i in range(4):
-        if not other and i % 2 == 0:
-            for load in loads[3 * i : 3 * i + 6]:
+        if not other:
+            for load in loads[3 * i : 3 * i + 6 if i % 2 == 0 else 3 * i]:
                 load.wait()
         c = bc_ref[first + 2 * i, :, LANE:]
         gated = []
@@ -492,34 +501,32 @@
         for j, v in enumerate(gated):
             at = slice(j * LW, (j + 1) * LW)
             rows_ref[i, :, at] = (v * scale * gain_ref[first + 2 * i, :, at]).astype(BF16)
-        to = out_ref.at[:, pl.ds(pl.multiple_of((first + 2 * i) * XW, XW), XW)]
-        copies.append(pltpu.make_async_copy(rows_ref.at[i], to, sems.at[i]))
-        copies[-1].start()
+        if other:
+            send(1, i, rows_ref, sems)
     for copy in copies:
         copy.wait()
 
 
 def finish(other, core, p, q, bc, states, gain, out):
+    rows = pltpu.VMEM((4, TOK, XW), BF16)
     if other:
         operands = [core, p, q, bc, states, gain, out]
         in_specs = in_smem(1) + in_vmem(5) + [pl.BlockSpec(memory_space=pl.ANY)]
-        loaded = []
+        out_shape = jax.ShapeDtypeStruct((TOK, GROUPS * XW), BF16)
+        out_spec = pl.BlockSpec(memory_space=pl.ANY)
+        scratch = [rows, pltpu.SemaphoreType.DMA((2, 4))]
     else:
         operands = [core, from_hbm(p), from_hbm(q), bc, from_hbm(states), gain, out]
         in_specs = in_smem(1) + in_hbm(2) + in_vmem(1) + in_hbm(1) + in_vmem(1) + [pl.BlockSpec(memory_space=pl.ANY)]
-        loaded = [
-            pltpu.VMEM((4, TOK, XW), BF16),
-            pltpu.VMEM((4, TOK, XW), BF16),
-            pltpu.VMEM((CHUNKS, 64, LANE), BF16),
-            pltpu.SemaphoreType.DMA((3, 4)),
-        ]
+        out_shape = jax.ShapeDtypeStruct((4, TOK, XW), BF16)
+        out_spec = in_vmem(1)[0]
+        scratch = [rows, rows, pltpu.VMEM((CHUNKS, 64, LANE), BF16), pltpu.SemaphoreType.DMA((3, 4))]
     return pl.pallas_call(
         functools.partial(finish_kernel, other),
         in_specs=in_specs,
-        out_specs=pl.BlockSpec(memory_space=pl.ANY),
-        scratch_shapes=[pltpu.VMEM((4, TOK, XW), BF16), pltpu.SemaphoreType.DMA((4,))] + loaded,
-        out_shape=jax.ShapeDtypeStruct((TOK, GROUPS * XW), BF16),
-        input_output_aliases={6: 0} if other else {},
+        out_specs=out_spec,
+        scratch_shapes=scratch,
+        out_shape=out_shape,
         compiler_params=params(),
         cost_estimate=pl.CostEstimate(flops=200_000_000, bytes_accessed=4_000_000, transcendentals=1000),
         name="finish",

time: 81.3 us -> 80.7 us (level)
  no operation moved by 1% of the time
where the time goes in v5:
time: 80.7 us; the launch traced here: 80.1 us
  Pallas kernels  30.1 us (37%)
  starting transfers between devices  27.4 us (34%)
  waiting for transfers between devices  20.7 us (26%)
  between operations  1.64 us (2%)
    pallas_call x2, Pallas kernels, local(): pl.pallas_call(functools.partial(local_kernel, other), grid_spec=pltpu.Pr...  11 us
    all_to_all x1, waiting for transfers between devices, body(): pieces = lax.all_to_all(pieces, CHIPS, 0, 0, tiled=True)  8.08 us
    ppermute x4, starting transfers between devices, body(): lax.ppermute(tail if k > 1 else onward, CHIPS, [(c, (c + k) % chips) for...  7.52 us
    pallas_call x1, Pallas kernels, chip_states(): pl.pallas_call(states_kernel, in_specs=in_smem(2) + in_hbm(2) + in_vmem(7...  7.05 us
    ppermute x4, waiting for transfers between devices, body(): lax.ppermute(tail if k > 1 else onward, CHIPS, [(c, (c + k) % chips) for...  6.44 us
    pallas_call x1, Pallas kernels, activate(): pl.pallas_call(act_kernel, in_specs=in_smem(1) + in_hbm(2) + in_vmem(4),...  5.45 us
    all_to_all x1, starting transfers between devices, body(): pieces = lax.all_to_all(pieces, CHIPS, 0, 0, tiled=True)  4.8 us
    all_to_all x1, starting transfers between devices, body(): states = lax.all_to_all(scan(chips, pieces, done), CHIPS, 0, 0, tiled=True)  4.66 us
  transfers between devices with their start and end apart: 13, of which 6 were waited for; matrix products, arithmetic and copies ran while one was open for 0% of the time, Pallas kernels for 27%

profile of v5, /device:TPU:1, one launch (start us, length us, event | category | flops | bytes accessed | tf_op | source)
XLA Modules:
  0.0 80.1 jit_solution(16437312501583223375)
XLA Ops:
  0.0 1.4 %collective-permute-start = (bf16[128,8,1280]{2,1,0:T(8,128)(2,1)}, bf16[128,8,1280]{2,1,0:T(8,128)(2,1)}, u32[]{:S(2)}, u32[]{:S(2)}) collective-permute-start(bf16[128,8,1280]{2,1,0:T(8,128)(2,1)} %conv_hbm.3), channel_id=1, source_target_pairs={{0,1},{1,0},{2,3},{3,2},{4,5},{5,4},{6,7},{7,6},{8,9},{9,8},{10,11... | collective-permute-start | bytes 7864328 | tf_op jit(solution)/shard_map/ppermute | solution.py:554
  2.1 1.2 %start.1 = (f32[3,128,128]{2,1,0:T(8,128)S(1)}, f32[136,128]{1,0:T(8,128)S(1)}, bf16[6,8,1280]{2,1,0:T(8,128)(2,1)S(1)}) custom-call(s32[1]{0:T(128)S(6)} %copy.11.len_ref, bf16[128,128]{1,0:T(8,128)(2,1)} %decay_hbm.1, bf16[128,128]{1,0:T(8,128)(2,1)} %step_hbm.1, bf16[128,8,1280]{2,1,0:T(8,128)(2,1)} %conv_hbm.3), custom_call_target="tpu_custom_call" | custom-call | tf_op jit(solution)/shard_map/start/pallas_call | solution.py:109
  3.8 2.3 %collective-permute-done.1.sib_ref = bf16[6,8,1280]{2,1,0:T(8,128)(2,1)S(1)} collective-permute-done((bf16[6,8,1280]{2,1,0:T(8,128)(2,1)S(1)}, bf16[6,8,1280]{2,1,0:T(8,128)(2,1)S(1)}, u32[]{:S(2)}, u32[]{:S(2)}) %collective-permute-start.1) | collective-permute-done | bytes 122912 | tf_op jit(solution)/shard_map/ppermute | solution.py:556
  6.3 1.4 %collective-permute-start.2 = (bf16[24,1280]{1,0:T(8,128)(2,1)S(1)}, bf16[24,1280]{1,0:T(8,128)(2,1)S(1)}, u32[]{:S(2)}, u32[]{:S(2)}) collective-permute-start(bf16[24,1280]{1,0:T(8,128)(2,1)S(1)} %get-tuple-element.27), channel_id=1, source_target_pairs={{0,2},{2,4},{4,6},{6,8},{8,10},{10,12},{12,14},{14,16},{16,18},{18... | collective-permute-start | bytes 184328 | tf_op jit(solution)/shard_map/ppermute | solution.py:558
  7.7 1.6 %collective-permute-start.5 = (bf16[24,1280]{1,0:T(8,128)(2,1)S(1)}, bf16[24,1280]{1,0:T(8,128)(2,1)S(1)}, u32[]{:S(2)}, u32[]{:S(2)}) collective-permute-start(bf16[24,1280]{1,0:T(8,128)(2,1)S(1)} %get-tuple-element.26.p0), channel_id=1, source_target_pairs={{0,8},{2,10},{4,12},{6,14},{8,16},{10,18},{12,20},{14,22},{16,24},... | collective-permute-start | bytes 184328 | tf_op jit(solution)/shard_map/ppermute | solution.py:558
  9.3 2.7 %collective-permute-start.4 = (bf16[24,1280]{1,0:T(8,128)(2,1)S(1)}, bf16[24,1280]{1,0:T(8,128)(2,1)S(1)}, u32[]{:S(2)}, u32[]{:S(2)}) collective-permute-start(bf16[24,1280]{1,0:T(8,128)(2,1)S(1)} %get-tuple-element.26.p0), channel_id=1, source_target_pairs={{0,6},{2,8},{4,10},{6,12},{8,14},{10,16},{12,18},{14,20},{16,22},{... | collective-permute-start | bytes 184328 | tf_op jit(solution)/shard_map/ppermute | solution.py:558
  12.1 1.7 %collective-permute-start.3 = (bf16[24,1280]{1,0:T(8,128)(2,1)S(1)}, bf16[24,1280]{1,0:T(8,128)(2,1)S(1)}, u32[]{:S(2)}, u32[]{:S(2)}) collective-permute-start(bf16[24,1280]{1,0:T(8,128)(2,1)S(1)} %get-tuple-element.26.p0), channel_id=1, source_target_pairs={{0,4},{2,6},{4,8},{6,10},{8,12},{10,14},{12,16},{14,18},{16,20},{1... | collective-permute-start | bytes 184328 | tf_op jit(solution)/shard_map/ppermute | solution.py:558
  14.4 2.7 %collective-permute-done.2.p1 = bf16[24,1280]{1,0:T(8,128)(2,1)S(1)} collective-permute-done((bf16[24,1280]{1,0:T(8,128)(2,1)S(1)}, bf16[24,1280]{1,0:T(8,128)(2,1)S(1)}, u32[]{:S(2)}, u32[]{:S(2)}) %collective-permute-start.2) | collective-permute-done | bytes 61472 | tf_op jit(solution)/shard_map/ppermute | solution.py:558
  17.2 0.9 %collective-permute-done.4.p3 = bf16[24,1280]{1,0:T(8,128)(2,1)S(1)} collective-permute-done((bf16[24,1280]{1,0:T(8,128)(2,1)S(1)}, bf16[24,1280]{1,0:T(8,128)(2,1)S(1)}, u32[]{:S(2)}, u32[]{:S(2)}) %collective-permute-start.4) | collective-permute-done | bytes 61472 | tf_op jit(solution)/shard_map/ppermute | solution.py:558
  18.0 2.9 %collective-permute-done.3.p2 = bf16[24,1280]{1,0:T(8,128)(2,1)S(1)} collective-permute-done((bf16[24,1280]{1,0:T(8,128)(2,1)S(1)}, bf16[24,1280]{1,0:T(8,128)(2,1)S(1)}, u32[]{:S(2)}, u32[]{:S(2)}) %collective-permute-start.3) | collective-permute-done | bytes 61472 | tf_op jit(solution)/shard_map/ppermute | solution.py:558
  20.9 7.0 %chip_states.1 = (bf16[64,72,128]{2,1,0:T(8,128)(2,1)}, bf16[4,4,4,64,128]{4,3,2,1,0:T(8,128)(2,1)}, f32[5,8,1280]{2,1,0:T(8,128)S(1)}, bf16[3,8,1280]{2,1,0:T(8,128)(2,1)S(1)}) custom-call(s32[1]{0:T(128)} %bitcast.core_ref, s32[1]{0:T(128)S(6)} %copy.12.first_ref, bf16[128,8,1280]{2,1,0:T(8,128)(2,1)} %conv_hbm.3, ...), custom_call_target="tpu_custom_call" | custom-call | tf_op jit(solution)/shard_map/chip_states/pallas_call | solution.py:273
  27.9 4.8 %all-to-all-start = ((bf16[64,72,128]{2,1,0:T(8,128)(2,1)}), bf16[64,72,128]{2,1,0:T(8,128)(2,1)S(1)}, u32[]{:S(2)}, u32[]{:S(2)}) async-start(bf16[64,72,128]{2,1,0:T(8,128)(2,1)} %get-tuple-element.37), calls=%async_computation | async-start | bytes 2359296 | tf_op jit(solution)/shard_map/all_to_all | solution.py:565
  32.8 2.4 %collective-permute-start.8 = (f32[5,8,1280]{2,1,0:T(8,128)S(1)}, f32[5,8,1280]{2,1,0:T(8,128)S(1)}, u32[]{:S(2)}, u32[]{:S(2)}) collective-permute-start(f32[5,8,1280]{2,1,0:T(8,128)S(1)} %get-tuple-element.30.own_w_ref), channel_id=1, source_target_pairs={{0,1},{1,0},{2,3},{3,2},{4,5},{5,4},{6,7},{7,6},{8,9},{9,8},{10,11... | collective-permute-start | bytes 614408 | tf_op jit(solution)/shard_map/ppermute | solution.py:568
  35.3 1.5 %collective-permute-start.9 = (bf16[4,4,4,64,128]{4,3,2,1,0:T(8,128)(2,1)S(1)}, bf16[4,4,4,64,128]{4,3,2,1,0:T(8,128)(2,1)}, u32[]{:S(2)}, u32[]{:S(2)}) collective-permute-start(bf16[4,4,4,64,128]{4,3,2,1,0:T(8,128)(2,1)S(1)} %copy-done.7), channel_id=1, source_target_pairs={{0,1},{2,3},{4,5},{6,7},{8,9},{10,11},{12,13},{14,15},{16,17},{18,... | collective-permute-start | bytes 3145736 | tf_op jit(solution)/shard_map/ppermute | solution.py:566
  36.8 5.4 %activate.1 = (bf16[8,128,1024]{2,1,0:T(8,128)(2,1)}, bf16[8,128,256]{2,1,0:T(8,128)(2,1)}, f32[8,128]{1,0:T(8,128)S(1)}) custom-call(s32[1]{0:T(128)} %bitcast.core_ref, bf16[128,8,1280]{2,1,0:T(8,128)(2,1)} %conv_hbm.3, bf16[128,8,1280]{2,1,0:T(8,128)(2,1)} %collective-permute-done.sib_hbm, bf16[3,8,1280]{2,1,0:T(8,128)(2,1)S(1)} %get-tuple-element.29.own_halo_ref, ...), custom_call_target="tpu_custom_call" | custom-call | flops 20000000 | bytes 8000000 | tf_op jit(solution)/shard_map/activate/pallas_call | solution.py:345
  42.2 8.1 %all-to-all-done.in_ref = bf16[64,72,128]{2,1,0:T(8,128)(2,1)S(1)} async-done(((bf16[64,72,128]{2,1,0:T(8,128)(2,1)}), bf16[64,72,128]{2,1,0:T(8,128)(2,1)S(1)}, u32[]{:S(2)}, u32[]{:S(2)}) %all-to-all-start) | async-done | bytes 1179680 | tf_op jit(solution)/shard_map/all_to_all | solution.py:565
  50.3 1.1 %scan.1 = bf16[64,64,128]{2,1,0:T(8,128)(2,1)} custom-call(bf16[64,72,128]{2,1,0:T(8,128)(2,1)S(1)} %all-to-all-done.in_ref, f32[8,128]{1,0:T(8,128)S(1)} %get-tuple-element.38.done_ref), custom_call_target="tpu_custom_call" | custom-call | tf_op jit(solution)/shard_map/scan/pallas_call | solution.py:386
  51.5 4.7 %all-to-all-start.1 = ((bf16[64,64,128]{2,1,0:T(8,128)(2,1)}), bf16[64,64,128]{2,1,0:T(8,128)(2,1)S(1)}, u32[]{:S(2)}, u32[]{:S(2)}) async-start(bf16[64,64,128]{2,1,0:T(8,128)(2,1)} %scan.1), calls=%async_computation.1 | async-start | bytes 2097152 | tf_op jit(solution)/shard_map/all_to_all | solution.py:574
  56.3 5.5 %local.3 = (bf16[4,128,1024]{2,1,0:T(8,128)(2,1)}, bf16[4,128,1024]{2,1,0:T(8,128)(2,1)}, f32[8,128]{1,0:T(8,128)S(1)}) custom-call(s32[1]{0:T(128)} %bitcast.core_ref, s32[1]{0:T(128)S(6)} %copy.11.len_ref, bf16[8,128,1024]{2,1,0:T(8,128)(2,1)} %get-tuple-element.31.x_ref, bf16[8,128,256]{2,1,0:T(8,128)(2,1)} %get-tuple-element.32.bc_ref, ...), custom_call_target="tpu_custom_call" | custom-call | flops 400000000 | bytes 8000000 | tf_op jit(solution)/shard_map/local/pallas_call | solution.py:433
  61.8 5.5 %local.2 = (bf16[4,128,1024]{2,1,0:T(8,128)(2,1)}, bf16[4,128,1024]{2,1,0:T(8,128)(2,1)}, f32[8,128]{1,0:T(8,128)S(1)}) custom-call(s32[1]{0:T(128)} %bitcast.core_ref, s32[1]{0:T(128)S(6)} %copy.11.len_ref, bf16[8,128,1024]{2,1,0:T(8,128)(2,1)} %get-tuple-element.31.x_ref, bf16[8,128,256]{2,1,0:T(8,128)(2,1)} %get-tuple-element.32.bc_ref, ...), custom_call_target="tpu_custom_call" | custom-call | flops 400000000 | bytes 8000000 | tf_op jit(solution)/shard_map/local/pallas_call | solution.py:433
  67.3 3.9 %all-to-all-done.1.state_ref = bf16[64,64,128]{2,1,0:T(8,128)(2,1)S(1)} async-done(((bf16[64,64,128]{2,1,0:T(8,128)(2,1)}), bf16[64,64,128]{2,1,0:T(8,128)(2,1)S(1)}, u32[]{:S(2)}, u32[]{:S(2)}) %all-to-all-start.1) | async-done | bytes 1048608 | tf_op jit(solution)/shard_map/all_to_all | solution.py:574
  71.2 4.4 %collective-permute-start.10 = (bf16[64,64,128]{2,1,0:T(8,128)(2,1)S(1)}, bf16[64,64,128]{2,1,0:T(8,128)(2,1)S(1)}, u32[]{:S(2)}, u32[]{:S(2)}) collective-permute-start(bf16[64,64,128]{2,1,0:T(8,128)(2,1)S(1)} %all-to-all-done.1.state_ref), channel_id=1, source_target_pairs={{0,1},{1,0},{2,3},{3,2},{4,5},{5,4},{6,7},{7,6},{8,9},{9,8},{10,11... | collective-permute-start | bytes 3145736 | tf_op jit(solution)/shard_map/ppermute | solution.py:576
  75.6 2.6 %finish.2.rest_0_ = bf16[4,128,1024]{2,1,0:T(8,128)(2,1)S(1)} custom-call(s32[1]{0:T(128)} %bitcast.core_ref, bf16[4,128,1024]{2,1,0:T(8,128)(2,1)} %get-tuple-element.42.p_ref, bf16[4,128,1024]{2,1,0:T(8,128)(2,1)} %get-tuple-element.43.q_ref, bf16[8,128,256]{2,1,0:T(8,128)(2,1)S(1)} %copy-done, bf16[64,64,128]{2,1,0:T(8,128)(2,1)} %copy-done.6, ...), custom_call_target="tpu_custom_call" | custom-call | flops 200000000 | bytes 4000000 | tf_op jit(solution)/shard_map/finish/pallas_call | solution.py:524
  78.2 1.7 %finish.3 = bf16[128,8192]{1,0:T(8,128)(2,1)} custom-call(s32[1]{0:T(128)} %bitcast.core_ref, bf16[4,128,1024]{2,1,0:T(8,128)(2,1)S(1)} %copy-done.1, bf16[4,128,1024]{2,1,0:T(8,128)(2,1)S(1)} %copy-done.2, bf16[8,128,256]{2,1,0:T(8,128)(2,1)S(1)} %copy-done, bf16[64,64,128]{2,1,0:T(8,128)(2,1)S(1)} %collective-permute-done.10.state_ref, ...), custom_call_target="tpu_custom_call" | custom-call | flops 200000000 | bytes 4000000 | tf_op jit(solution)/shard_map/finish/pallas_call | solution.py:524
  (32 shorter events, 1.0 us)
Async XLA Ops:
  0.0 6.1 %copy-start.5 = (f32[1,1280]{1,0:T(1,128)S(1)}, f32[1,1280]{1,0:T(1,128)}, u32[]{:S(2)}) copy-start(f32[1,1280]{1,0:T(1,128)} %bias_ref.1) | copy-start | bytes 15364
  0.0 6.1 %copy-start.4 = (f32[4,1,1280]{2,1,0:T(1,128)S(1)}, f32[4,1,1280]{2,1,0:T(1,128)}, u32[]{:S(2)}) copy-start(f32[4,1,1280]{2,1,0:T(1,128)} %weight_ref.1) | copy-start | bytes 61444
  0.0 20.9 %collective-permute-start = (bf16[128,8,1280]{2,1,0:T(8,128)(2,1)}, bf16[128,8,1280]{2,1,0:T(8,128)(2,1)}, u32[]{:S(2)}, u32[]{:S(2)}) collective-permute-start(bf16[128,8,1280]{2,1,0:T(8,128)(2,1)} %conv_hbm.3), channel_id=1, source_target_pairs={{0,1},{1,0},{2,3},{3,2},{4,5},{5,4},{6,7},{7,6},{8,9},{9,8},{10,11... | collective-permute-start | bytes 7864328 | tf_op jit(solution)/shard_map/ppermute | solution.py:554
  3.2 2.9 %collective-permute-start.1 = (bf16[6,8,1280]{2,1,0:T(8,128)(2,1)S(1)}, bf16[6,8,1280]{2,1,0:T(8,128)(2,1)S(1)}, u32[]{:S(2)}, u32[]{:S(2)}) collective-permute-start(bf16[6,8,1280]{2,1,0:T(8,128)(2,1)S(1)} %get-tuple-element.25.own_ref), channel_id=1, source_target_pairs={{0,1},{1,0},{2,3},{3,2},{4,5},{5,4},{6,7},{7,6},{8,9},{9,8},{10,11... | collective-permute-start | bytes 368648 | tf_op jit(solution)/shard_map/ppermute | solution.py:556
  3.4 8.6 %collective-permute-start.6 = (f32[136,128]{1,0:T(8,128)S(1)}, f32[136,128]{1,0:T(8,128)S(1)}, u32[]{:S(2)}, u32[]{:S(2)}) collective-permute-start(f32[136,128]{1,0:T(8,128)S(1)} %get-tuple-element.28.eto_ref), channel_id=1, source_target_pairs={{0,1},{1,0},{2,3},{3,2},{4,5},{5,4},{6,7},{7,6},{8,9},{9,8},{10,11... | collective-permute-start | bytes 208904 | tf_op jit(solution)/shard_map/ppermute | solution.py:560
  6.3 10.9 %collective-permute-start.2 = (bf16[24,1280]{1,0:T(8,128)(2,1)S(1)}, bf16[24,1280]{1,0:T(8,128)(2,1)S(1)}, u32[]{:S(2)}, u32[]{:S(2)}) collective-permute-start(bf16[24,1280]{1,0:T(8,128)(2,1)S(1)} %get-tuple-element.27), channel_id=1, source_target_pairs={{0,2},{2,4},{4,6},{6,8},{8,10},{10,12},{12,14},{14,16},{16,18},{18... | collective-permute-start | bytes 184328 | tf_op jit(solution)/shard_map/ppermute | solution.py:558
  7.7 9.5 %collective-permute-start.5 = (bf16[24,1280]{1,0:T(8,128)(2,1)S(1)}, bf16[24,1280]{1,0:T(8,128)(2,1)S(1)}, u32[]{:S(2)}, u32[]{:S(2)}) collective-permute-start(bf16[24,1280]{1,0:T(8,128)(2,1)S(1)} %get-tuple-element.26.p0), channel_id=1, source_target_pairs={{0,8},{2,10},{4,12},{6,14},{8,16},{10,18},{12,20},{14,22},{16,24},... | collective-permute-start | bytes 184328 | tf_op jit(solution)/shard_map/ppermute | solution.py:558
  9.3 8.7 %collective-permute-start.4 = (bf16[24,1280]{1,0:T(8,128)(2,1)S(1)}, bf16[24,1280]{1,0:T(8,128)(2,1)S(1)}, u32[]{:S(2)}, u32[]{:S(2)}) collective-permute-start(bf16[24,1280]{1,0:T(8,128)(2,1)S(1)} %get-tuple-element.26.p0), channel_id=1, source_target_pairs={{0,6},{2,8},{4,10},{6,12},{8,14},{10,16},{12,18},{14,20},{16,22},{... | collective-permute-start | bytes 184328 | tf_op jit(solution)/shard_map/ppermute | solution.py:558
  12.1 8.8 %collective-permute-start.3 = (bf16[24,1280]{1,0:T(8,128)(2,1)S(1)}, bf16[24,1280]{1,0:T(8,128)(2,1)S(1)}, u32[]{:S(2)}, u32[]{:S(2)}) collective-permute-start(bf16[24,1280]{1,0:T(8,128)(2,1)S(1)} %get-tuple-element.26.p0), channel_id=1, source_target_pairs={{0,4},{2,6},{4,8},{6,10},{8,12},{10,14},{12,16},{14,18},{16,20},{1... | collective-permute-start | bytes 184328 | tf_op jit(solution)/shard_map/ppermute | solution.py:558
  27.9 7.4 %copy-start.7 = (bf16[4,4,4,64,128]{4,3,2,1,0:T(8,128)(2,1)S(1)}, bf16[4,4,4,64,128]{4,3,2,1,0:T(8,128)(2,1)}, u32[]{:S(2)}) copy-start(bf16[4,4,4,64,128]{4,3,2,1,0:T(8,128)(2,1)} %get-tuple-element.34.before_ref) | copy-start | bytes 3145732
  27.9 22.4 %all-to-all-start = ((bf16[64,72,128]{2,1,0:T(8,128)(2,1)}), bf16[64,72,128]{2,1,0:T(8,128)(2,1)S(1)}, u32[]{:S(2)}, u32[]{:S(2)}) async-start(bf16[64,72,128]{2,1,0:T(8,128)(2,1)} %get-tuple-element.37), calls=%async_computation | async-start | bytes 2359296 | tf_op jit(solution)/shard_map/all_to_all | solution.py:565
  32.8 4.0 %collective-permute-start.8 = (f32[5,8,1280]{2,1,0:T(8,128)S(1)}, f32[5,8,1280]{2,1,0:T(8,128)S(1)}, u32[]{:S(2)}, u32[]{:S(2)}) collective-permute-start(f32[5,8,1280]{2,1,0:T(8,128)S(1)} %get-tuple-element.30.own_w_ref), channel_id=1, source_target_pairs={{0,1},{1,0},{2,3},{3,2},{4,5},{5,4},{6,7},{7,6},{8,9},{9,8},{10,11... | collective-permute-start | bytes 614408 | tf_op jit(solution)/shard_map/ppermute | solution.py:568
  35.2 1.6 %collective-permute-start.7 = (bf16[3,8,1280]{2,1,0:T(8,128)(2,1)S(1)}, bf16[3,8,1280]{2,1,0:T(8,128)(2,1)S(1)}, u32[]{:S(2)}, u32[]{:S(2)}) collective-permute-start(bf16[3,8,1280]{2,1,0:T(8,128)(2,1)S(1)} %get-tuple-element.29.own_halo_ref), channel_id=1, source_target_pairs={{0,1},{1,0},{2,3},{3,2},{4,5},{5,4},{6,7},{7,6},{8,9},{9,8},{10,11... | collective-permute-start | bytes 184328 | tf_op jit(solution)/shard_map/ppermute | solution.py:567
  35.3 26.5 %collective-permute-start.9 = (bf16[4,4,4,64,128]{4,3,2,1,0:T(8,128)(2,1)S(1)}, bf16[4,4,4,64,128]{4,3,2,1,0:T(8,128)(2,1)}, u32[]{:S(2)}, u32[]{:S(2)}) collective-permute-start(bf16[4,4,4,64,128]{4,3,2,1,0:T(8,128)(2,1)S(1)} %copy-done.7), channel_id=1, source_target_pairs={{0,1},{2,3},{4,5},{6,7},{8,9},{10,11},{12,13},{14,15},{16,17},{18,... | collective-permute-start | bytes 3145736 | tf_op jit(solution)/shard_map/ppermute | solution.py:566
  50.3 5.8 %copy-start.8 = (f32[128]{0:T(128)S(1)}, f32[128]{0:T(128)}, u32[]{:S(2)}) copy-start(f32[128]{0:T(128)} %param.16) | copy-start | bytes 1540
  51.5 19.8 %all-to-all-start.1 = ((bf16[64,64,128]{2,1,0:T(8,128)(2,1)}), bf16[64,64,128]{2,1,0:T(8,128)(2,1)S(1)}, u32[]{:S(2)}, u32[]{:S(2)}) async-start(bf16[64,64,128]{2,1,0:T(8,128)(2,1)} %scan.1), calls=%async_computation.1 | async-start | bytes 2097152 | tf_op jit(solution)/shard_map/all_to_all | solution.py:574
  61.8 13.9 %copy-start = (bf16[8,128,256]{2,1,0:T(8,128)(2,1)S(1)}, bf16[8,128,256]{2,1,0:T(8,128)(2,1)}, u32[]{:S(2)}) copy-start(bf16[8,128,256]{2,1,0:T(8,128)(2,1)} %get-tuple-element.32.bc_ref) | copy-start | bytes 1572868
  61.8 13.9 %copy-start.3 = (f32[8192]{0:T(1024)S(1)}, f32[8192]{0:T(1024)}, u32[]{:S(2)}) copy-start(f32[8192]{0:T(1024)} %param.17) | copy-start | bytes 98308
  71.2 4.4 %copy-start.6 = (bf16[64,64,128]{2,1,0:T(8,128)(2,1)}, bf16[64,64,128]{2,1,0:T(8,128)(2,1)S(1)}, u32[]{:S(2)}) copy-start(bf16[64,64,128]{2,1,0:T(8,128)(2,1)S(1)} %all-to-all-done.1.state_ref) | copy-start | bytes 3145732
  71.2 7.0 %collective-permute-start.10 = (bf16[64,64,128]{2,1,0:T(8,128)(2,1)S(1)}, bf16[64,64,128]{2,1,0:T(8,128)(2,1)S(1)}, u32[]{:S(2)}, u32[]{:S(2)}) collective-permute-start(bf16[64,64,128]{2,1,0:T(8,128)(2,1)S(1)} %all-to-all-done.1.state_ref), channel_id=1, source_target_pairs={{0,1},{1,0},{2,3},{3,2},{4,5},{5,4},{6,7},{7,6},{8,9},{9,8},{10,11... | collective-permute-start | bytes 3145736 | tf_op jit(solution)/shard_map/ppermute | solution.py:576
  75.6 2.6 %copy-start.1 = (bf16[4,128,1024]{2,1,0:T(8,128)(2,1)S(1)}, bf16[4,128,1024]{2,1,0:T(8,128)(2,1)}, u32[]{:S(2)}) copy-start(bf16[4,128,1024]{2,1,0:T(8,128)(2,1)} %get-tuple-element.35.p_ref) | copy-start | bytes 3145732
  75.6 2.6 %copy-start.2 = (bf16[4,128,1024]{2,1,0:T(8,128)(2,1)S(1)}, bf16[4,128,1024]{2,1,0:T(8,128)(2,1)}, u32[]{:S(2)}) copy-start(bf16[4,128,1024]{2,1,0:T(8,128)(2,1)} %get-tuple-element.36.q_ref) | copy-start | bytes 3145732

commit v6 on v5

--- a/solution.py
+++ b/solution.py
@@ -237,27 +237,26 @@
     for i in range(4):
         of_group = lambda half, tile: act_ref[tile, pl.ds(2 * i + half, TOK, stride=GROUPS), :]
         b_t = [of_group(half, 8).T.astype(BF16) for half in range(2)]
-        for j in range(4):
-            states = []
-            for half in range(2):
-                carried = [
-                    (of_group(half, tile) * widen(decay[half][:TOK], core * 16 + i * 32 + tile * 2)).astype(BF16)
-                    for tile in (2 * j, 2 * j + 1)
-                ]
-                states.append(jnp.dot(b_t[half], jnp.concatenate(carried, axis=1), preferred_element_type=F32))
-            for tile in range(2):
-                lanes = slice(tile * LANE, (tile + 1) * LANE)
-                head = core * 16 + i * 32 + (2 * j + tile) * 2
-                hi, mid, bottom = split3(widen(d_chip, head))
-                extra = jnp.where(row == 0, hi, jnp.where(row == 1, mid, jnp.where(row == 2, bottom, keep)))
-                first = states[0][:, lanes]
-                both = (first * widen(d_last, head)[0:1] + states[1][:, lanes]).astype(BF16)
-                first = first.astype(BF16)
-                for rows in range(2):
-                    piece = (i * 8 + 2 * j + tile) * 2 + rows
-                    before_ref[i, j, tile * 2 + rows] = first[rows * 64 : rows * 64 + 64]
-                    pieces_ref[piece, 0:64] = both[rows * 64 : rows * 64 + 64]
-                    pieces_ref[piece, 64:ROWS] = extra.astype(BF16)
+        states = []
+        for half in range(2):
+            carried = [
+                (of_group(half, tile) * widen(decay[half][:TOK], core * 16 + i * 32 + tile * 2)).astype(BF16)
+                for tile in range(8)
+            ]
+            states.append(jnp.dot(b_t[half], jnp.concatenate(carried, axis=1), preferred_element_type=F32))
+        for tile in range(8):
+            lanes = slice(tile * LANE, (tile + 1) * LANE)
+            head = core * 16 + i * 32 + tile * 2
+            hi, mid, bottom = split3(widen(d_chip, head))
+            extra = jnp.where(row == 0, hi, jnp.where(row == 1, mid, jnp.where(row == 2, bottom, keep)))
+            first = states[0][:, lanes]
+            both = (first * widen(d_last, head)[0:1] + states[1][:, lanes]).astype(BF16)
+            first = first.astype(BF16)
+            for rows in range(2):
+                piece = (i * 8 + tile) * 2 + rows
+                before_ref[i, tile // 2, tile % 2 * 2 + rows] = first[rows * 64 : rows * 64 + 64]
+                pieces_ref[piece, 0:64] = both[rows * 64 : rows * 64 + 64]
+                pieces_ref[piece, 64:ROWS] = extra.astype(BF16)
         group = pl.ds(i * 16, 16)
         copies.append(pltpu.make_async_copy(pieces_ref.at[group], out_hbm.at[group], sems.at[0, i]))
         copies.append(pltpu.make_async_copy(before_ref.at[i], before_hbm.at[i], sems.at[1, i]))

time: 80.7 us -> 80.6 us (level)
  no operation moved by 1% of the time
where the time goes in v6:
time: 80.6 us; the launch traced here: 80 us
  Pallas kernels  30 us (37%)
  starting transfers between devices  27.4 us (34%)
  waiting for transfers between devices  20.7 us (26%)
  between operations  1.64 us (2%)
    pallas_call x2, Pallas kernels, local(): pl.pallas_call(functools.partial(local_kernel, other), grid_spec=pltpu.Pr...  11 us
    all_to_all x1, waiting for transfers between devices, body(): pieces = lax.all_to_all(pieces, CHIPS, 0, 0, tiled=True)  8.07 us
    ppermute x4, starting transfers between devices, body(): lax.ppermute(tail if k > 1 else onward, CHIPS, [(c, (c + k) % chips) for...  7.52 us
    pallas_call x1, Pallas kernels, chip_states(): pl.pallas_call(states_kernel, in_specs=in_smem(2) + in_hbm(2) + in_vmem(7...  6.97 us
    ppermute x4, waiting for transfers between devices, body(): lax.ppermute(tail if k > 1 else onward, CHIPS, [(c, (c + k) % chips) for...  6.44 us
    pallas_call x1, Pallas kernels, activate(): pl.pallas_call(act_kernel, in_specs=in_smem(1) + in_hbm(2) + in_vmem(4),...  5.45 us
    all_to_all x1, starting transfers between devices, body(): pieces = lax.all_to_all(pieces, CHIPS, 0, 0, tiled=True)  4.8 us
    all_to_all x1, starting transfers between devices, body(): states = lax.all_to_all(scan(chips, pieces, done), CHIPS, 0, 0, tiled=True)  4.66 us
  transfers between devices with their start and end apart: 13, of which 6 were waited for; matrix products, arithmetic and copies ran while one was open for 0% of the time, Pallas kernels for 27%

profile of v6, /device:TPU:1, one launch (start us, length us, event | category | flops | bytes accessed | tf_op | source)
XLA Modules:
  0.0 80.0 jit_solution(72074326469192955)
XLA Ops:
  0.0 1.4 %collective-permute-start = (bf16[128,8,1280]{2,1,0:T(8,128)(2,1)}, bf16[128,8,1280]{2,1,0:T(8,128)(2,1)}, u32[]{:S(2)}, u32[]{:S(2)}) collective-permute-start(bf16[128,8,1280]{2,1,0:T(8,128)(2,1)} %conv_hbm.3), channel_id=1, source_target_pairs={{0,1},{1,0},{2,3},{3,2},{4,5},{5,4},{6,7},{7,6},{8,9},{9,8},{10,11... | collective-permute-start | bytes 7864328 | tf_op jit(solution)/shard_map/ppermute | solution.py:553
  2.1 1.2 %start.1 = (f32[3,128,128]{2,1,0:T(8,128)S(1)}, f32[136,128]{1,0:T(8,128)S(1)}, bf16[6,8,1280]{2,1,0:T(8,128)(2,1)S(1)}) custom-call(s32[1]{0:T(128)S(6)} %copy.11.len_ref, bf16[128,128]{1,0:T(8,128)(2,1)} %decay_hbm.1, bf16[128,128]{1,0:T(8,128)(2,1)} %step_hbm.1, bf16[128,8,1280]{2,1,0:T(8,128)(2,1)} %conv_hbm.3), custom_call_target="tpu_custom_call" | custom-call | tf_op jit(solution)/shard_map/start/pallas_call | solution.py:109
  3.8 2.3 %collective-permute-done.1.sib_ref = bf16[6,8,1280]{2,1,0:T(8,128)(2,1)S(1)} collective-permute-done((bf16[6,8,1280]{2,1,0:T(8,128)(2,1)S(1)}, bf16[6,8,1280]{2,1,0:T(8,128)(2,1)S(1)}, u32[]{:S(2)}, u32[]{:S(2)}) %collective-permute-start.1) | collective-permute-done | bytes 122912 | tf_op jit(solution)/shard_map/ppermute | solution.py:555
  6.3 1.4 %collective-permute-start.2 = (bf16[24,1280]{1,0:T(8,128)(2,1)S(1)}, bf16[24,1280]{1,0:T(8,128)(2,1)S(1)}, u32[]{:S(2)}, u32[]{:S(2)}) collective-permute-start(bf16[24,1280]{1,0:T(8,128)(2,1)S(1)} %get-tuple-element.27), channel_id=1, source_target_pairs={{0,2},{2,4},{4,6},{6,8},{8,10},{10,12},{12,14},{14,16},{16,18},{18... | collective-permute-start | bytes 184328 | tf_op jit(solution)/shard_map/ppermute | solution.py:557
  7.7 1.6 %collective-permute-start.5 = (bf16[24,1280]{1,0:T(8,128)(2,1)S(1)}, bf16[24,1280]{1,0:T(8,128)(2,1)S(1)}, u32[]{:S(2)}, u32[]{:S(2)}) collective-permute-start(bf16[24,1280]{1,0:T(8,128)(2,1)S(1)} %get-tuple-element.26.p0), channel_id=1, source_target_pairs={{0,8},{2,10},{4,12},{6,14},{8,16},{10,18},{12,20},{14,22},{16,24},... | collective-permute-start | bytes 184328 | tf_op jit(solution)/shard_map/ppermute | solution.py:557
  9.3 2.7 %collective-permute-start.4 = (bf16[24,1280]{1,0:T(8,128)(2,1)S(1)}, bf16[24,1280]{1,0:T(8,128)(2,1)S(1)}, u32[]{:S(2)}, u32[]{:S(2)}) collective-permute-start(bf16[24,1280]{1,0:T(8,128)(2,1)S(1)} %get-tuple-element.26.p0), channel_id=1, source_target_pairs={{0,6},{2,8},{4,10},{6,12},{8,14},{10,16},{12,18},{14,20},{16,22},{... | collective-permute-start | bytes 184328 | tf_op jit(solution)/shard_map/ppermute | solution.py:557
  12.1 1.7 %collective-permute-start.3 = (bf16[24,1280]{1,0:T(8,128)(2,1)S(1)}, bf16[24,1280]{1,0:T(8,128)(2,1)S(1)}, u32[]{:S(2)}, u32[]{:S(2)}) collective-permute-start(bf16[24,1280]{1,0:T(8,128)(2,1)S(1)} %get-tuple-element.26.p0), channel_id=1, source_target_pairs={{0,4},{2,6},{4,8},{6,10},{8,12},{10,14},{12,16},{14,18},{16,20},{1... | collective-permute-start | bytes 184328 | tf_op jit(solution)/shard_map/ppermute | solution.py:557
  14.4 2.7 %collective-permute-done.2.p1 = bf16[24,1280]{1,0:T(8,128)(2,1)S(1)} collective-permute-done((bf16[24,1280]{1,0:T(8,128)(2,1)S(1)}, bf16[24,1280]{1,0:T(8,128)(2,1)S(1)}, u32[]{:S(2)}, u32[]{:S(2)}) %collective-permute-start.2) | collective-permute-done | bytes 61472 | tf_op jit(solution)/shard_map/ppermute | solution.py:557
  17.2 0.9 %collective-permute-done.4.p3 = bf16[24,1280]{1,0:T(8,128)(2,1)S(1)} collective-permute-done((bf16[24,1280]{1,0:T(8,128)(2,1)S(1)}, bf16[24,1280]{1,0:T(8,128)(2,1)S(1)}, u32[]{:S(2)}, u32[]{:S(2)}) %collective-permute-start.4) | collective-permute-done | bytes 61472 | tf_op jit(solution)/shard_map/ppermute | solution.py:557
  18.0 2.9 %collective-permute-done.3.p2 = bf16[24,1280]{1,0:T(8,128)(2,1)S(1)} collective-permute-done((bf16[24,1280]{1,0:T(8,128)(2,1)S(1)}, bf16[24,1280]{1,0:T(8,128)(2,1)S(1)}, u32[]{:S(2)}, u32[]{:S(2)}) %collective-permute-start.3) | collective-permute-done | bytes 61472 | tf_op jit(solution)/shard_map/ppermute | solution.py:557
  20.9 7.0 %chip_states.1 = (bf16[64,72,128]{2,1,0:T(8,128)(2,1)}, bf16[4,4,4,64,128]{4,3,2,1,0:T(8,128)(2,1)}, f32[5,8,1280]{2,1,0:T(8,128)S(1)}, bf16[3,8,1280]{2,1,0:T(8,128)(2,1)S(1)}) custom-call(s32[1]{0:T(128)} %bitcast.core_ref, s32[1]{0:T(128)S(6)} %copy.12.first_ref, bf16[128,8,1280]{2,1,0:T(8,128)(2,1)} %conv_hbm.3, ...), custom_call_target="tpu_custom_call" | custom-call | tf_op jit(solution)/shard_map/chip_states/pallas_call | solution.py:272
  27.9 4.8 %all-to-all-start = ((bf16[64,72,128]{2,1,0:T(8,128)(2,1)}), bf16[64,72,128]{2,1,0:T(8,128)(2,1)S(1)}, u32[]{:S(2)}, u32[]{:S(2)}) async-start(bf16[64,72,128]{2,1,0:T(8,128)(2,1)} %get-tuple-element.37), calls=%async_computation | async-start | bytes 2359296 | tf_op jit(solution)/shard_map/all_to_all | solution.py:564
  32.7 2.5 %collective-permute-start.8 = (f32[5,8,1280]{2,1,0:T(8,128)S(1)}, f32[5,8,1280]{2,1,0:T(8,128)S(1)}, u32[]{:S(2)}, u32[]{:S(2)}) collective-permute-start(f32[5,8,1280]{2,1,0:T(8,128)S(1)} %get-tuple-element.30.own_w_ref), channel_id=1, source_target_pairs={{0,1},{1,0},{2,3},{3,2},{4,5},{5,4},{6,7},{7,6},{8,9},{9,8},{10,11... | collective-permute-start | bytes 614408 | tf_op jit(solution)/shard_map/ppermute | solution.py:567
  35.2 1.5 %collective-permute-start.9 = (bf16[4,4,4,64,128]{4,3,2,1,0:T(8,128)(2,1)S(1)}, bf16[4,4,4,64,128]{4,3,2,1,0:T(8,128)(2,1)}, u32[]{:S(2)}, u32[]{:S(2)}) collective-permute-start(bf16[4,4,4,64,128]{4,3,2,1,0:T(8,128)(2,1)S(1)} %copy-done.7), channel_id=1, source_target_pairs={{0,1},{2,3},{4,5},{6,7},{8,9},{10,11},{12,13},{14,15},{16,17},{18,... | collective-permute-start | bytes 3145736 | tf_op jit(solution)/shard_map/ppermute | solution.py:565
  36.7 5.4 %activate.1 = (bf16[8,128,1024]{2,1,0:T(8,128)(2,1)}, bf16[8,128,256]{2,1,0:T(8,128)(2,1)}, f32[8,128]{1,0:T(8,128)S(1)}) custom-call(s32[1]{0:T(128)} %bitcast.core_ref, bf16[128,8,1280]{2,1,0:T(8,128)(2,1)} %conv_hbm.3, bf16[128,8,1280]{2,1,0:T(8,128)(2,1)} %collective-permute-done.sib_hbm, bf16[3,8,1280]{2,1,0:T(8,128)(2,1)S(1)} %get-tuple-element.29.own_halo_ref, ...), custom_call_target="tpu_custom_call" | custom-call | flops 20000000 | bytes 8000000 | tf_op jit(solution)/shard_map/activate/pallas_call | solution.py:344
  42.2 8.1 %all-to-all-done.in_ref = bf16[64,72,128]{2,1,0:T(8,128)(2,1)S(1)} async-done(((bf16[64,72,128]{2,1,0:T(8,128)(2,1)}), bf16[64,72,128]{2,1,0:T(8,128)(2,1)S(1)}, u32[]{:S(2)}, u32[]{:S(2)}) %all-to-all-start) | async-done | bytes 1179680 | tf_op jit(solution)/shard_map/all_to_all | solution.py:564
  50.2 1.1 %scan.1 = bf16[64,64,128]{2,1,0:T(8,128)(2,1)} custom-call(bf16[64,72,128]{2,1,0:T(8,128)(2,1)S(1)} %all-to-all-done.in_ref, f32[8,128]{1,0:T(8,128)S(1)} %get-tuple-element.38.done_ref), custom_call_target="tpu_custom_call" | custom-call | tf_op jit(solution)/shard_map/scan/pallas_call | solution.py:385
  51.4 4.7 %all-to-all-start.1 = ((bf16[64,64,128]{2,1,0:T(8,128)(2,1)}), bf16[64,64,128]{2,1,0:T(8,128)(2,1)S(1)}, u32[]{:S(2)}, u32[]{:S(2)}) async-start(bf16[64,64,128]{2,1,0:T(8,128)(2,1)} %scan.1), calls=%async_computation.1 | async-start | bytes 2097152 | tf_op jit(solution)/shard_map/all_to_all | solution.py:573
  56.2 5.5 %local.3 = (bf16[4,128,1024]{2,1,0:T(8,128)(2,1)}, bf16[4,128,1024]{2,1,0:T(8,128)(2,1)}, f32[8,128]{1,0:T(8,128)S(1)}) custom-call(s32[1]{0:T(128)} %bitcast.core_ref, s32[1]{0:T(128)S(6)} %copy.11.len_ref, bf16[8,128,1024]{2,1,0:T(8,128)(2,1)} %get-tuple-element.31.x_ref, bf16[8,128,256]{2,1,0:T(8,128)(2,1)} %get-tuple-element.32.bc_ref, ...), custom_call_target="tpu_custom_call" | custom-call | flops 400000000 | bytes 8000000 | tf_op jit(solution)/shard_map/local/pallas_call | solution.py:432
  61.7 5.5 %local.2 = (bf16[4,128,1024]{2,1,0:T(8,128)(2,1)}, bf16[4,128,1024]{2,1,0:T(8,128)(2,1)}, f32[8,128]{1,0:T(8,128)S(1)}) custom-call(s32[1]{0:T(128)} %bitcast.core_ref, s32[1]{0:T(128)S(6)} %copy.11.len_ref, bf16[8,128,1024]{2,1,0:T(8,128)(2,1)} %get-tuple-element.31.x_ref, bf16[8,128,256]{2,1,0:T(8,128)(2,1)} %get-tuple-element.32.bc_ref, ...), custom_call_target="tpu_custom_call" | custom-call | flops 400000000 | bytes 8000000 | tf_op jit(solution)/shard_map/local/pallas_call | solution.py:432
  67.2 3.9 %all-to-all-done.1.state_ref = bf16[64,64,128]{2,1,0:T(8,128)(2,1)S(1)} async-done(((bf16[64,64,128]{2,1,0:T(8,128)(2,1)}), bf16[64,64,128]{2,1,0:T(8,128)(2,1)S(1)}, u32[]{:S(2)}, u32[]{:S(2)}) %all-to-all-start.1) | async-done | bytes 1048608 | tf_op jit(solution)/shard_map/all_to_all | solution.py:573
  71.1 4.4 %collective-permute-start.10 = (bf16[64,64,128]{2,1,0:T(8,128)(2,1)S(1)}, bf16[64,64,128]{2,1,0:T(8,128)(2,1)S(1)}, u32[]{:S(2)}, u32[]{:S(2)}) collective-permute-start(bf16[64,64,128]{2,1,0:T(8,128)(2,1)S(1)} %all-to-all-done.1.state_ref), channel_id=1, source_target_pairs={{0,1},{1,0},{2,3},{3,2},{4,5},{5,4},{6,7},{7,6},{8,9},{9,8},{10,11... | collective-permute-start | bytes 3145736 | tf_op jit(solution)/shard_map/ppermute | solution.py:575
  75.6 2.6 %finish.2.rest_0_ = bf16[4,128,1024]{2,1,0:T(8,128)(2,1)S(1)} custom-call(s32[1]{0:T(128)} %bitcast.core_ref, bf16[4,128,1024]{2,1,0:T(8,128)(2,1)} %get-tuple-element.42.p_ref, bf16[4,128,1024]{2,1,0:T(8,128)(2,1)} %get-tuple-element.43.q_ref, bf16[8,128,256]{2,1,0:T(8,128)(2,1)S(1)} %copy-done, bf16[64,64,128]{2,1,0:T(8,128)(2,1)} %copy-done.6, ...), custom_call_target="tpu_custom_call" | custom-call | flops 200000000 | bytes 4000000 | tf_op jit(solution)/shard_map/finish/pallas_call | solution.py:523
  78.2 1.7 %finish.3 = bf16[128,8192]{1,0:T(8,128)(2,1)} custom-call(s32[1]{0:T(128)} %bitcast.core_ref, bf16[4,128,1024]{2,1,0:T(8,128)(2,1)S(1)} %copy-done.1, bf16[4,128,1024]{2,1,0:T(8,128)(2,1)S(1)} %copy-done.2, bf16[8,128,256]{2,1,0:T(8,128)(2,1)S(1)} %copy-done, bf16[64,64,128]{2,1,0:T(8,128)(2,1)S(1)} %collective-permute-done.10.state_ref, ...), custom_call_target="tpu_custom_call" | custom-call | flops 200000000 | bytes 4000000 | tf_op jit(solution)/shard_map/finish/pallas_call | solution.py:523
  (32 shorter events, 1.0 us)
Async XLA Ops:
  0.0 6.1 %copy-start.5 = (f32[1,1280]{1,0:T(1,128)S(1)}, f32[1,1280]{1,0:T(1,128)}, u32[]{:S(2)}) copy-start(f32[1,1280]{1,0:T(1,128)} %bias_ref.1) | copy-start | bytes 15364
  0.0 6.1 %copy-start.4 = (f32[4,1,1280]{2,1,0:T(1,128)S(1)}, f32[4,1,1280]{2,1,0:T(1,128)}, u32[]{:S(2)}) copy-start(f32[4,1,1280]{2,1,0:T(1,128)} %weight_ref.1) | copy-start | bytes 61444
  0.0 20.9 %collective-permute-start = (bf16[128,8,1280]{2,1,0:T(8,128)(2,1)}, bf16[128,8,1280]{2,1,0:T(8,128)(2,1)}, u32[]{:S(2)}, u32[]{:S(2)}) collective-permute-start(bf16[128,8,1280]{2,1,0:T(8,128)(2,1)} %conv_hbm.3), channel_id=1, source_target_pairs={{0,1},{1,0},{2,3},{3,2},{4,5},{5,4},{6,7},{7,6},{8,9},{9,8},{10,11... | collective-permute-start | bytes 7864328 | tf_op jit(solution)/shard_map/ppermute | solution.py:553
  3.2 2.9 %collective-permute-start.1 = (bf16[6,8,1280]{2,1,0:T(8,128)(2,1)S(1)}, bf16[6,8,1280]{2,1,0:T(8,128)(2,1)S(1)}, u32[]{:S(2)}, u32[]{:S(2)}) collective-permute-start(bf16[6,8,1280]{2,1,0:T(8,128)(2,1)S(1)} %get-tuple-element.25.own_ref), channel_id=1, source_target_pairs={{0,1},{1,0},{2,3},{3,2},{4,5},{5,4},{6,7},{7,6},{8,9},{9,8},{10,11... | collective-permute-start | bytes 368648 | tf_op jit(solution)/shard_map/ppermute | solution.py:555
  3.4 8.7 %collective-permute-start.6 = (f32[136,128]{1,0:T(8,128)S(1)}, f32[136,128]{1,0:T(8,128)S(1)}, u32[]{:S(2)}, u32[]{:S(2)}) collective-permute-start(f32[136,128]{1,0:T(8,128)S(1)} %get-tuple-element.28.eto_ref), channel_id=1, source_target_pairs={{0,1},{1,0},{2,3},{3,2},{4,5},{5,4},{6,7},{7,6},{8,9},{9,8},{10,11... | collective-permute-start | bytes 208904 | tf_op jit(solution)/shard_map/ppermute | solution.py:559
  6.3 10.9 %collective-permute-start.2 = (bf16[24,1280]{1,0:T(8,128)(2,1)S(1)}, bf16[24,1280]{1,0:T(8,128)(2,1)S(1)}, u32[]{:S(2)}, u32[]{:S(2)}) collective-permute-start(bf16[24,1280]{1,0:T(8,128)(2,1)S(1)} %get-tuple-element.27), channel_id=1, source_target_pairs={{0,2},{2,4},{4,6},{6,8},{8,10},{10,12},{12,14},{14,16},{16,18},{18... | collective-permute-start | bytes 184328 | tf_op jit(solution)/shard_map/ppermute | solution.py:557
  7.7 9.5 %collective-permute-start.5 = (bf16[24,1280]{1,0:T(8,128)(2,1)S(1)}, bf16[24,1280]{1,0:T(8,128)(2,1)S(1)}, u32[]{:S(2)}, u32[]{:S(2)}) collective-permute-start(bf16[24,1280]{1,0:T(8,128)(2,1)S(1)} %get-tuple-element.26.p0), channel_id=1, source_target_pairs={{0,8},{2,10},{4,12},{6,14},{8,16},{10,18},{12,20},{14,22},{16,24},... | collective-permute-start | bytes 184328 | tf_op jit(solution)/shard_map/ppermute | solution.py:557
  9.3 8.7 %collective-permute-start.4 = (bf16[24,1280]{1,0:T(8,128)(2,1)S(1)}, bf16[24,1280]{1,0:T(8,128)(2,1)S(1)}, u32[]{:S(2)}, u32[]{:S(2)}) collective-permute-start(bf16[24,1280]{1,0:T(8,128)(2,1)S(1)} %get-tuple-element.26.p0), channel_id=1, source_target_pairs={{0,6},{2,8},{4,10},{6,12},{8,14},{10,16},{12,18},{14,20},{16,22},{... | collective-permute-start | bytes 184328 | tf_op jit(solution)/shard_map/ppermute | solution.py:557
  12.1 8.8 %collective-permute-start.3 = (bf16[24,1280]{1,0:T(8,128)(2,1)S(1)}, bf16[24,1280]{1,0:T(8,128)(2,1)S(1)}, u32[]{:S(2)}, u32[]{:S(2)}) collective-permute-start(bf16[24,1280]{1,0:T(8,128)(2,1)S(1)} %get-tuple-element.26.p0), channel_id=1, source_target_pairs={{0,4},{2,6},{4,8},{6,10},{8,12},{10,14},{12,16},{14,18},{16,20},{1... | collective-permute-start | bytes 184328 | tf_op jit(solution)/shard_map/ppermute | solution.py:557
  27.9 7.4 %copy-start.7 = (bf16[4,4,4,64,128]{4,3,2,1,0:T(8,128)(2,1)S(1)}, bf16[4,4,4,64,128]{4,3,2,1,0:T(8,128)(2,1)}, u32[]{:S(2)}) copy-start(bf16[4,4,4,64,128]{4,3,2,1,0:T(8,128)(2,1)} %get-tuple-element.34.before_ref) | copy-start | bytes 3145732
  27.9 22.4 %all-to-all-start = ((bf16[64,72,128]{2,1,0:T(8,128)(2,1)}), bf16[64,72,128]{2,1,0:T(8,128)(2,1)S(1)}, u32[]{:S(2)}, u32[]{:S(2)}) async-start(bf16[64,72,128]{2,1,0:T(8,128)(2,1)} %get-tuple-element.37), calls=%async_computation | async-start | bytes 2359296 | tf_op jit(solution)/shard_map/all_to_all | solution.py:564
  32.7 4.0 %collective-permute-start.8 = (f32[5,8,1280]{2,1,0:T(8,128)S(1)}, f32[5,8,1280]{2,1,0:T(8,128)S(1)}, u32[]{:S(2)}, u32[]{:S(2)}) collective-permute-start(f32[5,8,1280]{2,1,0:T(8,128)S(1)} %get-tuple-element.30.own_w_ref), channel_id=1, source_target_pairs={{0,1},{1,0},{2,3},{3,2},{4,5},{5,4},{6,7},{7,6},{8,9},{9,8},{10,11... | collective-permute-start | bytes 614408 | tf_op jit(solution)/shard_map/ppermute | solution.py:567
  35.1 1.6 %collective-permute-start.7 = (bf16[3,8,1280]{2,1,0:T(8,128)(2,1)S(1)}, bf16[3,8,1280]{2,1,0:T(8,128)(2,1)S(1)}, u32[]{:S(2)}, u32[]{:S(2)}) collective-permute-start(bf16[3,8,1280]{2,1,0:T(8,128)(2,1)S(1)} %get-tuple-element.29.own_halo_ref), channel_id=1, source_target_pairs={{0,1},{1,0},{2,3},{3,2},{4,5},{5,4},{6,7},{7,6},{8,9},{9,8},{10,11... | collective-permute-start | bytes 184328 | tf_op jit(solution)/shard_map/ppermute | solution.py:566
  35.2 26.5 %collective-permute-start.9 = (bf16[4,4,4,64,128]{4,3,2,1,0:T(8,128)(2,1)S(1)}, bf16[4,4,4,64,128]{4,3,2,1,0:T(8,128)(2,1)}, u32[]{:S(2)}, u32[]{:S(2)}) collective-permute-start(bf16[4,4,4,64,128]{4,3,2,1,0:T(8,128)(2,1)S(1)} %copy-done.7), channel_id=1, source_target_pairs={{0,1},{2,3},{4,5},{6,7},{8,9},{10,11},{12,13},{14,15},{16,17},{18,... | collective-permute-start | bytes 3145736 | tf_op jit(solution)/shard_map/ppermute | solution.py:565
  50.2 5.8 %copy-start.8 = (f32[128]{0:T(128)S(1)}, f32[128]{0:T(128)}, u32[]{:S(2)}) copy-start(f32[128]{0:T(128)} %param.16) | copy-start | bytes 1540
  51.4 19.8 %all-to-all-start.1 = ((bf16[64,64,128]{2,1,0:T(8,128)(2,1)}), bf16[64,64,128]{2,1,0:T(8,128)(2,1)S(1)}, u32[]{:S(2)}, u32[]{:S(2)}) async-start(bf16[64,64,128]{2,1,0:T(8,128)(2,1)} %scan.1), calls=%async_computation.1 | async-start | bytes 2097152 | tf_op jit(solution)/shard_map/all_to_all | solution.py:573
  61.7 13.8 %copy-start = (bf16[8,128,256]{2,1,0:T(8,128)(2,1)S(1)}, bf16[8,128,256]{2,1,0:T(8,128)(2,1)}, u32[]{:S(2)}) copy-start(bf16[8,128,256]{2,1,0:T(8,128)(2,1)} %get-tuple-element.32.bc_ref) | copy-start | bytes 1572868
  61.7 13.8 %copy-start.3 = (f32[8192]{0:T(1024)S(1)}, f32[8192]{0:T(1024)}, u32[]{:S(2)}) copy-start(f32[8192]{0:T(1024)} %param.17) | copy-start | bytes 98308
  71.1 4.4 %copy-start.6 = (bf16[64,64,128]{2,1,0:T(8,128)(2,1)}, bf16[64,64,128]{2,1,0:T(8,128)(2,1)S(1)}, u32[]{:S(2)}) copy-start(bf16[64,64,128]{2,1,0:T(8,128)(2,1)S(1)} %all-to-all-done.1.state_ref) | copy-start | bytes 3145732
  71.1 7.0 %collective-permute-start.10 = (bf16[64,64,128]{2,1,0:T(8,128)(2,1)S(1)}, bf16[64,64,128]{2,1,0:T(8,128)(2,1)S(1)}, u32[]{:S(2)}, u32[]{:S(2)}) collective-permute-start(bf16[64,64,128]{2,1,0:T(8,128)(2,1)S(1)} %all-to-all-done.1.state_ref), channel_id=1, source_target_pairs={{0,1},{1,0},{2,3},{3,2},{4,5},{5,4},{6,7},{7,6},{8,9},{9,8},{10,11... | collective-permute-start | bytes 3145736 | tf_op jit(solution)/shard_map/ppermute | solution.py:575
  75.5 2.6 %copy-start.1 = (bf16[4,128,1024]{2,1,0:T(8,128)(2,1)S(1)}, bf16[4,128,1024]{2,1,0:T(8,128)(2,1)}, u32[]{:S(2)}) copy-start(bf16[4,128,1024]{2,1,0:T(8,128)(2,1)} %get-tuple-element.35.p_ref) | copy-start | bytes 3145732
  75.6 2.6 %copy-start.2 = (bf16[4,128,1024]{2,1,0:T(8,128)(2,1)S(1)}, bf16[4,128,1024]{2,1,0:T(8,128)(2,1)}, u32[]{:S(2)}) copy-start(bf16[4,128,1024]{2,1,0:T(8,128)(2,1)} %get-tuple-element.36.q_ref) | copy-start | bytes 3145732

commit v7 on v5

--- a/solution.py
+++ b/solution.py
@@ -364,7 +364,7 @@
 
 def scan_kernel(chips, in_ref, done_ref, out_hbm, out_ref, sems):
     each = CHUNKS // chips
-    parts = 4
+    parts = 8
     size = CHUNKS // parts
     states = [jnp.zeros((64, LANE), F32) for _ in range(each)]
     stores = []
@@ -388,7 +388,7 @@
         in_specs=in_vmem(1) + [pl.BlockSpec(memory_space=pl.ANY)],
         out_specs=in_hbm(1)[0],
         out_shape=hbm((CHUNKS, 64, LANE)),
-        scratch_shapes=[pltpu.VMEM((CHUNKS, 64, LANE), BF16), pltpu.SemaphoreType.DMA((4,))],
+        scratch_shapes=[pltpu.VMEM((CHUNKS, 64, LANE), BF16), pltpu.SemaphoreType.DMA((8,))],
         compiler_params=params(4),
         name="scan",
     )(pieces, done)

time: 80.7 us -> 80.7 us (level)
  no operation moved by 1% of the time
where the time goes in v7:
time: 80.7 us; the launch traced here: 80.1 us
  Pallas kernels  30.2 us (37%)
  starting transfers between devices  27.4 us (34%)
  waiting for transfers between devices  20.7 us (26%)
  between operations  1.64 us (2%)
    pallas_call x2, Pallas kernels, local(): pl.pallas_call(functools.partial(local_kernel, other), grid_spec=pltpu.Pr...  11 us
    all_to_all x1, waiting for transfers between devices, body(): pieces = lax.all_to_all(pieces, CHIPS, 0, 0, tiled=True)  8.08 us
    ppermute x4, starting transfers between devices, body(): lax.ppermute(tail if k > 1 else onward, CHIPS, [(c, (c + k) % chips) for...  7.52 us
    pallas_call x1, Pallas kernels, chip_states(): pl.pallas_call(states_kernel, in_specs=in_smem(2) + in_hbm(2) + in_vmem(7...  7.05 us
    ppermute x4, waiting for transfers between devices, body(): lax.ppermute(tail if k > 1 else onward, CHIPS, [(c, (c + k) % chips) for...  6.44 us
    pallas_call x1, Pallas kernels, activate(): pl.pallas_call(act_kernel, in_specs=in_smem(1) + in_hbm(2) + in_vmem(4),...  5.45 us
    all_to_all x1, starting transfers between devices, body(): pieces = lax.all_to_all(pieces, CHIPS, 0, 0, tiled=True)  4.8 us
    all_to_all x1, starting transfers between devices, body(): states = lax.all_to_all(scan(chips, pieces, done), CHIPS, 0, 0, tiled=True)  4.66 us
  transfers between devices with their start and end apart: 13, of which 6 were waited for; matrix products, arithmetic and copies ran while one was open for 0% of the time, Pallas kernels for 27%

profile of v7, /device:TPU:1, one launch (start us, length us, event | category | flops | bytes accessed | tf_op | source)
XLA Modules:
  0.0 80.1 jit_solution(11202353151682381359)
XLA Ops:
  0.0 1.4 %collective-permute-start = (bf16[128,8,1280]{2,1,0:T(8,128)(2,1)}, bf16[128,8,1280]{2,1,0:T(8,128)(2,1)}, u32[]{:S(2)}, u32[]{:S(2)}) collective-permute-start(bf16[128,8,1280]{2,1,0:T(8,128)(2,1)} %conv_hbm.3), channel_id=1, source_target_pairs={{0,1},{1,0},{2,3},{3,2},{4,5},{5,4},{6,7},{7,6},{8,9},{9,8},{10,11... | collective-permute-start | bytes 7864328 | tf_op jit(solution)/shard_map/ppermute | solution.py:554
  2.1 1.2 %start.1 = (f32[3,128,128]{2,1,0:T(8,128)S(1)}, f32[136,128]{1,0:T(8,128)S(1)}, bf16[6,8,1280]{2,1,0:T(8,128)(2,1)S(1)}) custom-call(s32[1]{0:T(128)S(6)} %copy.11.len_ref, bf16[128,128]{1,0:T(8,128)(2,1)} %decay_hbm.1, bf16[128,128]{1,0:T(8,128)(2,1)} %step_hbm.1, bf16[128,8,1280]{2,1,0:T(8,128)(2,1)} %conv_hbm.3), custom_call_target="tpu_custom_call" | custom-call | tf_op jit(solution)/shard_map/start/pallas_call | solution.py:109
  3.9 2.2 %collective-permute-done.1.sib_ref = bf16[6,8,1280]{2,1,0:T(8,128)(2,1)S(1)} collective-permute-done((bf16[6,8,1280]{2,1,0:T(8,128)(2,1)S(1)}, bf16[6,8,1280]{2,1,0:T(8,128)(2,1)S(1)}, u32[]{:S(2)}, u32[]{:S(2)}) %collective-permute-start.1) | collective-permute-done | bytes 122912 | tf_op jit(solution)/shard_map/ppermute | solution.py:556
  6.3 1.4 %collective-permute-start.2 = (bf16[24,1280]{1,0:T(8,128)(2,1)S(1)}, bf16[24,1280]{1,0:T(8,128)(2,1)S(1)}, u32[]{:S(2)}, u32[]{:S(2)}) collective-permute-start(bf16[24,1280]{1,0:T(8,128)(2,1)S(1)} %get-tuple-element.27), channel_id=1, source_target_pairs={{0,2},{2,4},{4,6},{6,8},{8,10},{10,12},{12,14},{14,16},{16,18},{18... | collective-permute-start | bytes 184328 | tf_op jit(solution)/shard_map/ppermute | solution.py:558
  7.7 1.6 %collective-permute-start.5 = (bf16[24,1280]{1,0:T(8,128)(2,1)S(1)}, bf16[24,1280]{1,0:T(8,128)(2,1)S(1)}, u32[]{:S(2)}, u32[]{:S(2)}) collective-permute-start(bf16[24,1280]{1,0:T(8,128)(2,1)S(1)} %get-tuple-element.26.p0), channel_id=1, source_target_pairs={{0,8},{2,10},{4,12},{6,14},{8,16},{10,18},{12,20},{14,22},{16,24},... | collective-permute-start | bytes 184328 | tf_op jit(solution)/shard_map/ppermute | solution.py:558
  9.3 2.7 %collective-permute-start.4 = (bf16[24,1280]{1,0:T(8,128)(2,1)S(1)}, bf16[24,1280]{1,0:T(8,128)(2,1)S(1)}, u32[]{:S(2)}, u32[]{:S(2)}) collective-permute-start(bf16[24,1280]{1,0:T(8,128)(2,1)S(1)} %get-tuple-element.26.p0), channel_id=1, source_target_pairs={{0,6},{2,8},{4,10},{6,12},{8,14},{10,16},{12,18},{14,20},{16,22},{... | collective-permute-start | bytes 184328 | tf_op jit(solution)/shard_map/ppermute | solution.py:558
  12.1 1.7 %collective-permute-start.3 = (bf16[24,1280]{1,0:T(8,128)(2,1)S(1)}, bf16[24,1280]{1,0:T(8,128)(2,1)S(1)}, u32[]{:S(2)}, u32[]{:S(2)}) collective-permute-start(bf16[24,1280]{1,0:T(8,128)(2,1)S(1)} %get-tuple-element.26.p0), channel_id=1, source_target_pairs={{0,4},{2,6},{4,8},{6,10},{8,12},{10,14},{12,16},{14,18},{16,20},{1... | collective-permute-start | bytes 184328 | tf_op jit(solution)/shard_map/ppermute | solution.py:558
  14.4 2.7 %collective-permute-done.2.p1 = bf16[24,1280]{1,0:T(8,128)(2,1)S(1)} collective-permute-done((bf16[24,1280]{1,0:T(8,128)(2,1)S(1)}, bf16[24,1280]{1,0:T(8,128)(2,1)S(1)}, u32[]{:S(2)}, u32[]{:S(2)}) %collective-permute-start.2) | collective-permute-done | bytes 61472 | tf_op jit(solution)/shard_map/ppermute | solution.py:558
  17.2 0.9 %collective-permute-done.4.p3 = bf16[24,1280]{1,0:T(8,128)(2,1)S(1)} collective-permute-done((bf16[24,1280]{1,0:T(8,128)(2,1)S(1)}, bf16[24,1280]{1,0:T(8,128)(2,1)S(1)}, u32[]{:S(2)}, u32[]{:S(2)}) %collective-permute-start.4) | collective-permute-done | bytes 61472 | tf_op jit(solution)/shard_map/ppermute | solution.py:558
  18.0 2.9 %collective-permute-done.3.p2 = bf16[24,1280]{1,0:T(8,128)(2,1)S(1)} collective-permute-done((bf16[24,1280]{1,0:T(8,128)(2,1)S(1)}, bf16[24,1280]{1,0:T(8,128)(2,1)S(1)}, u32[]{:S(2)}, u32[]{:S(2)}) %collective-permute-start.3) | collective-permute-done | bytes 61472 | tf_op jit(solution)/shard_map/ppermute | solution.py:558
  20.9 7.0 %chip_states.1 = (bf16[64,72,128]{2,1,0:T(8,128)(2,1)}, bf16[4,4,4,64,128]{4,3,2,1,0:T(8,128)(2,1)}, f32[5,8,1280]{2,1,0:T(8,128)S(1)}, bf16[3,8,1280]{2,1,0:T(8,128)(2,1)S(1)}) custom-call(s32[1]{0:T(128)} %bitcast.core_ref, s32[1]{0:T(128)S(6)} %copy.12.first_ref, bf16[128,8,1280]{2,1,0:T(8,128)(2,1)} %conv_hbm.3, ...), custom_call_target="tpu_custom_call" | custom-call | tf_op jit(solution)/shard_map/chip_states/pallas_call | solution.py:273
  27.9 4.8 %all-to-all-start = ((bf16[64,72,128]{2,1,0:T(8,128)(2,1)}), bf16[64,72,128]{2,1,0:T(8,128)(2,1)S(1)}, u32[]{:S(2)}, u32[]{:S(2)}) async-start(bf16[64,72,128]{2,1,0:T(8,128)(2,1)} %get-tuple-element.37), calls=%async_computation | async-start | bytes 2359296 | tf_op jit(solution)/shard_map/all_to_all | solution.py:565
  32.8 2.4 %collective-permute-start.8 = (f32[5,8,1280]{2,1,0:T(8,128)S(1)}, f32[5,8,1280]{2,1,0:T(8,128)S(1)}, u32[]{:S(2)}, u32[]{:S(2)}) collective-permute-start(f32[5,8,1280]{2,1,0:T(8,128)S(1)} %get-tuple-element.30.own_w_ref), channel_id=1, source_target_pairs={{0,1},{1,0},{2,3},{3,2},{4,5},{5,4},{6,7},{7,6},{8,9},{9,8},{10,11... | collective-permute-start | bytes 614408 | tf_op jit(solution)/shard_map/ppermute | solution.py:568
  35.3 1.5 %collective-permute-start.9 = (bf16[4,4,4,64,128]{4,3,2,1,0:T(8,128)(2,1)S(1)}, bf16[4,4,4,64,128]{4,3,2,1,0:T(8,128)(2,1)}, u32[]{:S(2)}, u32[]{:S(2)}) collective-permute-start(bf16[4,4,4,64,128]{4,3,2,1,0:T(8,128)(2,1)S(1)} %copy-done.7), channel_id=1, source_target_pairs={{0,1},{2,3},{4,5},{6,7},{8,9},{10,11},{12,13},{14,15},{16,17},{18,... | collective-permute-start | bytes 3145736 | tf_op jit(solution)/shard_map/ppermute | solution.py:566
  36.8 5.4 %activate.1 = (bf16[8,128,1024]{2,1,0:T(8,128)(2,1)}, bf16[8,128,256]{2,1,0:T(8,128)(2,1)}, f32[8,128]{1,0:T(8,128)S(1)}) custom-call(s32[1]{0:T(128)} %bitcast.core_ref, bf16[128,8,1280]{2,1,0:T(8,128)(2,1)} %conv_hbm.3, bf16[128,8,1280]{2,1,0:T(8,128)(2,1)} %collective-permute-done.sib_hbm, bf16[3,8,1280]{2,1,0:T(8,128)(2,1)S(1)} %get-tuple-element.29.own_halo_ref, ...), custom_call_target="tpu_custom_call" | custom-call | flops 20000000 | bytes 8000000 | tf_op jit(solution)/shard_map/activate/pallas_call | solution.py:345
  42.2 8.1 %all-to-all-done.in_ref = bf16[64,72,128]{2,1,0:T(8,128)(2,1)S(1)} async-done(((bf16[64,72,128]{2,1,0:T(8,128)(2,1)}), bf16[64,72,128]{2,1,0:T(8,128)(2,1)S(1)}, u32[]{:S(2)}, u32[]{:S(2)}) %all-to-all-start) | async-done | bytes 1179680 | tf_op jit(solution)/shard_map/all_to_all | solution.py:565
  50.3 1.1 %scan.1 = bf16[64,64,128]{2,1,0:T(8,128)(2,1)} custom-call(bf16[64,72,128]{2,1,0:T(8,128)(2,1)S(1)} %all-to-all-done.in_ref, f32[8,128]{1,0:T(8,128)S(1)} %get-tuple-element.38.done_ref), custom_call_target="tpu_custom_call" | custom-call | tf_op jit(solution)/shard_map/scan/pallas_call | solution.py:386
  51.4 4.7 %all-to-all-start.1 = ((bf16[64,64,128]{2,1,0:T(8,128)(2,1)}), bf16[64,64,128]{2,1,0:T(8,128)(2,1)S(1)}, u32[]{:S(2)}, u32[]{:S(2)}) async-start(bf16[64,64,128]{2,1,0:T(8,128)(2,1)} %scan.1), calls=%async_computation.1 | async-start | bytes 2097152 | tf_op jit(solution)/shard_map/all_to_all | solution.py:574
  56.3 5.5 %local.3 = (bf16[4,128,1024]{2,1,0:T(8,128)(2,1)}, bf16[4,128,1024]{2,1,0:T(8,128)(2,1)}, f32[8,128]{1,0:T(8,128)S(1)}) custom-call(s32[1]{0:T(128)} %bitcast.core_ref, s32[1]{0:T(128)S(6)} %copy.11.len_ref, bf16[8,128,1024]{2,1,0:T(8,128)(2,1)} %get-tuple-element.31.x_ref, bf16[8,128,256]{2,1,0:T(8,128)(2,1)} %get-tuple-element.32.bc_ref, ...), custom_call_target="tpu_custom_call" | custom-call | flops 400000000 | bytes 8000000 | tf_op jit(solution)/shard_map/local/pallas_call | solution.py:433
  61.8 5.5 %local.2 = (bf16[4,128,1024]{2,1,0:T(8,128)(2,1)}, bf16[4,128,1024]{2,1,0:T(8,128)(2,1)}, f32[8,128]{1,0:T(8,128)S(1)}) custom-call(s32[1]{0:T(128)} %bitcast.core_ref, s32[1]{0:T(128)S(6)} %copy.11.len_ref, bf16[8,128,1024]{2,1,0:T(8,128)(2,1)} %get-tuple-element.31.x_ref, bf16[8,128,256]{2,1,0:T(8,128)(2,1)} %get-tuple-element.32.bc_ref, ...), custom_call_target="tpu_custom_call" | custom-call | flops 400000000 | bytes 8000000 | tf_op jit(solution)/shard_map/local/pallas_call | solution.py:433
  67.3 3.9 %all-to-all-done.1.state_ref = bf16[64,64,128]{2,1,0:T(8,128)(2,1)S(1)} async-done(((bf16[64,64,128]{2,1,0:T(8,128)(2,1)}), bf16[64,64,128]{2,1,0:T(8,128)(2,1)S(1)}, u32[]{:S(2)}, u32[]{:S(2)}) %all-to-all-start.1) | async-done | bytes 1048608 | tf_op jit(solution)/shard_map/all_to_all | solution.py:574
  71.2 4.4 %collective-permute-start.10 = (bf16[64,64,128]{2,1,0:T(8,128)(2,1)S(1)}, bf16[64,64,128]{2,1,0:T(8,128)(2,1)S(1)}, u32[]{:S(2)}, u32[]{:S(2)}) collective-permute-start(bf16[64,64,128]{2,1,0:T(8,128)(2,1)S(1)} %all-to-all-done.1.state_ref), channel_id=1, source_target_pairs={{0,1},{1,0},{2,3},{3,2},{4,5},{5,4},{6,7},{7,6},{8,9},{9,8},{10,11... | collective-permute-start | bytes 3145736 | tf_op jit(solution)/shard_map/ppermute | solution.py:576
  75.6 2.6 %finish.2.rest_0_ = bf16[4,128,1024]{2,1,0:T(8,128)(2,1)S(1)} custom-call(s32[1]{0:T(128)} %bitcast.core_ref, bf16[4,128,1024]{2,1,0:T(8,128)(2,1)} %get-tuple-element.42.p_ref, bf16[4,128,1024]{2,1,0:T(8,128)(2,1)} %get-tuple-element.43.q_ref, bf16[8,128,256]{2,1,0:T(8,128)(2,1)S(1)} %copy-done, bf16[64,64,128]{2,1,0:T(8,128)(2,1)} %copy-done.6, ...), custom_call_target="tpu_custom_call" | custom-call | flops 200000000 | bytes 4000000 | tf_op jit(solution)/shard_map/finish/pallas_call | solution.py:524
  78.2 1.7 %finish.3 = bf16[128,8192]{1,0:T(8,128)(2,1)} custom-call(s32[1]{0:T(128)} %bitcast.core_ref, bf16[4,128,1024]{2,1,0:T(8,128)(2,1)S(1)} %copy-done.1, bf16[4,128,1024]{2,1,0:T(8,128)(2,1)S(1)} %copy-done.2, bf16[8,128,256]{2,1,0:T(8,128)(2,1)S(1)} %copy-done, bf16[64,64,128]{2,1,0:T(8,128)(2,1)S(1)} %collective-permute-done.10.state_ref, ...), custom_call_target="tpu_custom_call" | custom-call | flops 200000000 | bytes 4000000 | tf_op jit(solution)/shard_map/finish/pallas_call | solution.py:524
  (32 shorter events, 1.0 us)
Async XLA Ops:
  0.0 6.1 %copy-start.5 = (f32[1,1280]{1,0:T(1,128)S(1)}, f32[1,1280]{1,0:T(1,128)}, u32[]{:S(2)}) copy-start(f32[1,1280]{1,0:T(1,128)} %bias_ref.1) | copy-start | bytes 15364
  0.0 6.1 %copy-start.4 = (f32[4,1,1280]{2,1,0:T(1,128)S(1)}, f32[4,1,1280]{2,1,0:T(1,128)}, u32[]{:S(2)}) copy-start(f32[4,1,1280]{2,1,0:T(1,128)} %weight_ref.1) | copy-start | bytes 61444
  0.0 20.9 %collective-permute-start = (bf16[128,8,1280]{2,1,0:T(8,128)(2,1)}, bf16[128,8,1280]{2,1,0:T(8,128)(2,1)}, u32[]{:S(2)}, u32[]{:S(2)}) collective-permute-start(bf16[128,8,1280]{2,1,0:T(8,128)(2,1)} %conv_hbm.3), channel_id=1, source_target_pairs={{0,1},{1,0},{2,3},{3,2},{4,5},{5,4},{6,7},{7,6},{8,9},{9,8},{10,11... | collective-permute-start | bytes 7864328 | tf_op jit(solution)/shard_map/ppermute | solution.py:554
  3.3 2.8 %collective-permute-start.1 = (bf16[6,8,1280]{2,1,0:T(8,128)(2,1)S(1)}, bf16[6,8,1280]{2,1,0:T(8,128)(2,1)S(1)}, u32[]{:S(2)}, u32[]{:S(2)}) collective-permute-start(bf16[6,8,1280]{2,1,0:T(8,128)(2,1)S(1)} %get-tuple-element.25.own_ref), channel_id=1, source_target_pairs={{0,1},{1,0},{2,3},{3,2},{4,5},{5,4},{6,7},{7,6},{8,9},{9,8},{10,11... | collective-permute-start | bytes 368648 | tf_op jit(solution)/shard_map/ppermute | solution.py:556
  3.4 8.6 %collective-permute-start.6 = (f32[136,128]{1,0:T(8,128)S(1)}, f32[136,128]{1,0:T(8,128)S(1)}, u32[]{:S(2)}, u32[]{:S(2)}) collective-permute-start(f32[136,128]{1,0:T(8,128)S(1)} %get-tuple-element.28.eto_ref), channel_id=1, source_target_pairs={{0,1},{1,0},{2,3},{3,2},{4,5},{5,4},{6,7},{7,6},{8,9},{9,8},{10,11... | collective-permute-start | bytes 208904 | tf_op jit(solution)/shard_map/ppermute | solution.py:560
  6.3 10.9 %collective-permute-start.2 = (bf16[24,1280]{1,0:T(8,128)(2,1)S(1)}, bf16[24,1280]{1,0:T(8,128)(2,1)S(1)}, u32[]{:S(2)}, u32[]{:S(2)}) collective-permute-start(bf16[24,1280]{1,0:T(8,128)(2,1)S(1)} %get-tuple-element.27), channel_id=1, source_target_pairs={{0,2},{2,4},{4,6},{6,8},{8,10},{10,12},{12,14},{14,16},{16,18},{18... | collective-permute-start | bytes 184328 | tf_op jit(solution)/shard_map/ppermute | solution.py:558
  7.7 9.5 %collective-permute-start.5 = (bf16[24,1280]{1,0:T(8,128)(2,1)S(1)}, bf16[24,1280]{1,0:T(8,128)(2,1)S(1)}, u32[]{:S(2)}, u32[]{:S(2)}) collective-permute-start(bf16[24,1280]{1,0:T(8,128)(2,1)S(1)} %get-tuple-element.26.p0), channel_id=1, source_target_pairs={{0,8},{2,10},{4,12},{6,14},{8,16},{10,18},{12,20},{14,22},{16,24},... | collective-permute-start | bytes 184328 | tf_op jit(solution)/shard_map/ppermute | solution.py:558
  9.3 8.7 %collective-permute-start.4 = (bf16[24,1280]{1,0:T(8,128)(2,1)S(1)}, bf16[24,1280]{1,0:T(8,128)(2,1)S(1)}, u32[]{:S(2)}, u32[]{:S(2)}) collective-permute-start(bf16[24,1280]{1,0:T(8,128)(2,1)S(1)} %get-tuple-element.26.p0), channel_id=1, source_target_pairs={{0,6},{2,8},{4,10},{6,12},{8,14},{10,16},{12,18},{14,20},{16,22},{... | collective-permute-start | bytes 184328 | tf_op jit(solution)/shard_map/ppermute | solution.py:558
  12.1 8.8 %collective-permute-start.3 = (bf16[24,1280]{1,0:T(8,128)(2,1)S(1)}, bf16[24,1280]{1,0:T(8,128)(2,1)S(1)}, u32[]{:S(2)}, u32[]{:S(2)}) collective-permute-start(bf16[24,1280]{1,0:T(8,128)(2,1)S(1)} %get-tuple-element.26.p0), channel_id=1, source_target_pairs={{0,4},{2,6},{4,8},{6,10},{8,12},{10,14},{12,16},{14,18},{16,20},{1... | collective-permute-start | bytes 184328 | tf_op jit(solution)/shard_map/ppermute | solution.py:558
  27.9 7.4 %copy-start.7 = (bf16[4,4,4,64,128]{4,3,2,1,0:T(8,128)(2,1)S(1)}, bf16[4,4,4,64,128]{4,3,2,1,0:T(8,128)(2,1)}, u32[]{:S(2)}) copy-start(bf16[4,4,4,64,128]{4,3,2,1,0:T(8,128)(2,1)} %get-tuple-element.34.before_ref) | copy-start | bytes 3145732
  27.9 22.4 %all-to-all-start = ((bf16[64,72,128]{2,1,0:T(8,128)(2,1)}), bf16[64,72,128]{2,1,0:T(8,128)(2,1)S(1)}, u32[]{:S(2)}, u32[]{:S(2)}) async-start(bf16[64,72,128]{2,1,0:T(8,128)(2,1)} %get-tuple-element.37), calls=%async_computation | async-start | bytes 2359296 | tf_op jit(solution)/shard_map/all_to_all | solution.py:565
  32.8 4.0 %collective-permute-start.8 = (f32[5,8,1280]{2,1,0:T(8,128)S(1)}, f32[5,8,1280]{2,1,0:T(8,128)S(1)}, u32[]{:S(2)}, u32[]{:S(2)}) collective-permute-start(f32[5,8,1280]{2,1,0:T(8,128)S(1)} %get-tuple-element.30.own_w_ref), channel_id=1, source_target_pairs={{0,1},{1,0},{2,3},{3,2},{4,5},{5,4},{6,7},{7,6},{8,9},{9,8},{10,11... | collective-permute-start | bytes 614408 | tf_op jit(solution)/shard_map/ppermute | solution.py:568
  35.2 1.6 %collective-permute-start.7 = (bf16[3,8,1280]{2,1,0:T(8,128)(2,1)S(1)}, bf16[3,8,1280]{2,1,0:T(8,128)(2,1)S(1)}, u32[]{:S(2)}, u32[]{:S(2)}) collective-permute-start(bf16[3,8,1280]{2,1,0:T(8,128)(2,1)S(1)} %get-tuple-element.29.own_halo_ref), channel_id=1, source_target_pairs={{0,1},{1,0},{2,3},{3,2},{4,5},{5,4},{6,7},{7,6},{8,9},{9,8},{10,11... | collective-permute-start | bytes 184328 | tf_op jit(solution)/shard_map/ppermute | solution.py:567
  35.3 26.5 %collective-permute-start.9 = (bf16[4,4,4,64,128]{4,3,2,1,0:T(8,128)(2,1)S(1)}, bf16[4,4,4,64,128]{4,3,2,1,0:T(8,128)(2,1)}, u32[]{:S(2)}, u32[]{:S(2)}) collective-permute-start(bf16[4,4,4,64,128]{4,3,2,1,0:T(8,128)(2,1)S(1)} %copy-done.7), channel_id=1, source_target_pairs={{0,1},{2,3},{4,5},{6,7},{8,9},{10,11},{12,13},{14,15},{16,17},{18,... | collective-permute-start | bytes 3145736 | tf_op jit(solution)/shard_map/ppermute | solution.py:566
  50.3 5.8 %copy-start.8 = (f32[128]{0:T(128)S(1)}, f32[128]{0:T(128)}, u32[]{:S(2)}) copy-start(f32[128]{0:T(128)} %param.16) | copy-start | bytes 1540
  51.4 19.8 %all-to-all-start.1 = ((bf16[64,64,128]{2,1,0:T(8,128)(2,1)}), bf16[64,64,128]{2,1,0:T(8,128)(2,1)S(1)}, u32[]{:S(2)}, u32[]{:S(2)}) async-start(bf16[64,64,128]{2,1,0:T(8,128)(2,1)} %scan.1), calls=%async_computation.1 | async-start | bytes 2097152 | tf_op jit(solution)/shard_map/all_to_all | solution.py:574
  61.8 13.9 %copy-start = (bf16[8,128,256]{2,1,0:T(8,128)(2,1)S(1)}, bf16[8,128,256]{2,1,0:T(8,128)(2,1)}, u32[]{:S(2)}) copy-start(bf16[8,128,256]{2,1,0:T(8,128)(2,1)} %get-tuple-element.32.bc_ref) | copy-start | bytes 1572868
  61.8 13.9 %copy-start.3 = (f32[8192]{0:T(1024)S(1)}, f32[8192]{0:T(1024)}, u32[]{:S(2)}) copy-start(f32[8192]{0:T(1024)} %param.17) | copy-start | bytes 98308
  71.2 4.4 %copy-start.6 = (bf16[64,64,128]{2,1,0:T(8,128)(2,1)}, bf16[64,64,128]{2,1,0:T(8,128)(2,1)S(1)}, u32[]{:S(2)}) copy-start(bf16[64,64,128]{2,1,0:T(8,128)(2,1)S(1)} %all-to-all-done.1.state_ref) | copy-start | bytes 3145732
  71.2 7.0 %collective-permute-start.10 = (bf16[64,64,128]{2,1,0:T(8,128)(2,1)S(1)}, bf16[64,64,128]{2,1,0:T(8,128)(2,1)S(1)}, u32[]{:S(2)}, u32[]{:S(2)}) collective-permute-start(bf16[64,64,128]{2,1,0:T(8,128)(2,1)S(1)} %all-to-all-done.1.state_ref), channel_id=1, source_target_pairs={{0,1},{1,0},{2,3},{3,2},{4,5},{5,4},{6,7},{7,6},{8,9},{9,8},{10,11... | collective-permute-start | bytes 3145736 | tf_op jit(solution)/shard_map/ppermute | solution.py:576
  75.6 2.6 %copy-start.1 = (bf16[4,128,1024]{2,1,0:T(8,128)(2,1)S(1)}, bf16[4,128,1024]{2,1,0:T(8,128)(2,1)}, u32[]{:S(2)}) copy-start(bf16[4,128,1024]{2,1,0:T(8,128)(2,1)} %get-tuple-element.35.p_ref) | copy-start | bytes 3145732
  75.6 2.6 %copy-start.2 = (bf16[4,128,1024]{2,1,0:T(8,128)(2,1)S(1)}, bf16[4,128,1024]{2,1,0:T(8,128)(2,1)}, u32[]{:S(2)}) copy-start(bf16[4,128,1024]{2,1,0:T(8,128)(2,1)} %get-tuple-element.36.q_ref) | copy-start | bytes 3145732
